TPU v7x, 32 devices: a whole 2x2x4 slice. The times are simulated.
32 devices in a mesh: tpair: 8 (over z, x), col: 4 (over y, core).
Axes of the slice: x: 2, y: 2, z: 4, core: 2. Of those that a mesh axis runs over, the one named last changes fastest.
Arguments:
- peramb: bfloat16 [8, 2, 2048, 2048], P('tpair', None, None, 'col'), may hold values from -6 to 6
- sink_ops: bfloat16 [8, 2, 2, 512, 512], P('tpair'), may hold values from -0.1875 to 0.1875
- op_table: bfloat16 [2048, 2, 512], P('tpair'), may hold values from -0.1875 to 0.1875
- row_slot: int32 [2048], replicated, may hold values from 0 to 2047, each once
- pair_source: int32 [8], P('tpair'), may hold values from 0 to 1
- op_index: int32 [16, 2], P('tpair'), may hold values from 0 to 1
- listed_rows: int32 [16, 128], P('tpair'), may hold values from 0 to 511
Outputs:
- contracted: bfloat16 [16, 4, 128, 2, 2048], P('tpair', None, 'col')
Inputs may be any that keep to these rules, and one draw needn't show every extreme that they name: `row_slot`: every position of 0 to 2047 appears once.
All inputs are finite; a program needn't handle non-finite values.
Results may differ from a plain program's by a relative error of at most 0.0049.
Values may be sent and summed in bfloat16 or wider, within the bound.
No kernel may reach another device: no remote copies, remote signals or barrier semaphores. Data moves between devices by JAX's collectives and lax.ppermute only.
A program may use at most 64 MiB of HBM per device.

v0:
```python
import functools

import jax
import jax.numpy as jnp
from jax import lax
from jax.experimental import pallas as pl
from jax.experimental.pallas import tpu as pltpu
from jax.sharding import PartitionSpec as P

NS = 4
LANES = 128
VMEM_LIMIT = 24 * 1024 * 1024
BF16, F32 = jnp.bfloat16, jnp.float32


def iota(shape, dim):
    return lax.broadcasted_iota(jnp.int32, shape, dim)


def dot(a, b):
    return jnp.dot(a, b, preferred_element_type=F32)


def column(row):
    wide = jnp.broadcast_to(row, (LANES, LANES)).astype(F32)
    return jnp.transpose(wide).astype(jnp.int32)


def one_hot(col, first, width):
    tiles = [
        jnp.where(col - (first + n) == iota((col.shape[0], LANES), 1), 1.0, 0.0)
        for n in range(0, width, LANES)
    ]
    return jnp.concatenate(tiles, axis=1).astype(BF16)


def mix_kernel(op_ref, listed_ref, sink_ref, peramb_ref, *refs):
    outs, (left, held, sems) = refs[:-3], refs[-3:]
    n_cols = sum(out.shape[0] for out in outs)
    products, listed = listed_ref.shape
    eigen, local_cols = sink_ref.shape[-1], peramb_ref.shape[-1]
    loads = [
        pltpu.make_async_copy(
            peramb_ref.at[0, :, pl.ds(s * eigen, eigen), :], held.at[s], sems.at[s]
        )
        for s in range(NS)
    ]
    for load in loads:
        load.start()
    own2 = 2 * listed // n_cols
    me = lax.axis_index("col")
    row = iota((2 * listed, 2 * listed), 0)
    wanted = ((row // own2) ^ me) * (own2 // 2) + (row % own2) // 2 + (row % 2) * listed
    order = jnp.where(wanted == iota((2 * listed, 2 * listed), 1), 1.0, 0.0).astype(BF16)
    for k in range(products):
        op = op_ref[k, 0]
        onehot = one_hot(column(listed_ref[k : k + 1, :]), 0, eigen)
        real = dot(onehot, sink_ref[0, op, 0])
        imag = dot(onehot, sink_ref[0, op, 1])
        top = jnp.concatenate([real, -imag], axis=1)
        bottom = jnp.concatenate([imag, real], axis=1)
        both = jnp.concatenate([top, bottom], axis=0).astype(BF16)
        rows = dot(order, both).astype(BF16)
        for j in range(n_cols):
            at = (j * products + k) * own2
            left[at : at + own2, :] = rows[j * own2 : (j + 1) * own2]
    for s in range(NS):
        loads[s].wait()
        mixed = dot(left[...], held[s].reshape(2 * eigen, local_cols)).astype(BF16)
        j = 0
        for out in outs:
            for n in range(out.shape[0]):
                for k in range(products):
                    at = (j * products + k) * own2
                    out[n, k, s] = mixed[at : at + own2]
                j += 1


def mix(op_index, listed_rows, sink_ops, peramb, groups):
    products, listed = listed_rows.shape
    eigen = sink_ops.shape[-1]
    local_cols = peramb.shape[3]
    own2 = 2 * listed // sum(groups)
    blocks = [
        jax.ShapeDtypeStruct((group, products, NS, own2, local_cols), BF16) for group in groups
    ]
    vmem = pl.BlockSpec(memory_space=pltpu.VMEM)
    return pl.pallas_call(
        mix_kernel,
        in_specs=[
            pl.BlockSpec(memory_space=pltpu.SMEM), vmem, vmem, pl.BlockSpec(memory_space=pltpu.HBM)
        ],
        out_specs=[vmem] * len(groups),
        out_shape=blocks,
        scratch_shapes=[
            pltpu.VMEM((products * 2 * listed, 2 * eigen), BF16),
            pltpu.VMEM((NS, 2, eigen, local_cols), BF16),
            pltpu.SemaphoreType.DMA((NS,)),
        ],
        compiler_params=pltpu.CompilerParams(vmem_limit_bytes=VMEM_LIMIT),
        cost_estimate=pl.CostEstimate(flops=1000, bytes_accessed=1000, transcendentals=0),
        name="mix",
    )(op_index, listed_rows, sink_ops, pltpu.with_memory_space_constraint(peramb, pltpu.HBM))


def add_pieces(places, scalars_ref, slot_ref, pieces, products, eigen):
    source_ref, op_ref = scalars_ref
    blocks = eigen // LANES
    nops = slot_ref.shape[0] // blocks // 2
    pair, side = lax.axis_index("tpair"), lax.axis_index("col") % 2
    cols = []
    for k in products:
        op = source_ref[0] * nops + op_ref[k, 1]
        cols += [
            column(slot_ref[pl.ds(op * blocks + b, 1), :]) for b in range(blocks)
        ]
    col = jnp.concatenate(cols, axis=0)
    tiles, tables = [], []
    for owners, parts in zip(places, pieces):
        height = sum(part.shape[0] for part in parts) // len(owners)
        for owner in owners:
            first = owner
            if isinstance(owner, tuple):
                first = (2 * (pair ^ owner[0]) + (side ^ owner[1])) * height
            tiles.append(one_hot(col, first, height))
        tables += [part[...] for part in parts]
    return dot(jnp.concatenate(tiles, axis=1), jnp.concatenate(tables, axis=0))


def grouped(counts, refs):
    groups = []
    for count in counts:
        groups.append(refs[:count])
        refs = refs[count:]
    return groups, refs


def assemble_kernel(places, counts, source_ref, op_ref, slot_ref, *refs):
    pieces, (out_ref,) = grouped(counts, refs)
    products, eigen = out_ref.shape[0], out_ref.shape[2]
    total = add_pieces(places, (source_ref, op_ref), slot_ref, pieces, range(products), eigen)
    total = total.astype(BF16)
    for k in range(products):
        rows = slice(k * eigen, (k + 1) * eigen)
        out_ref[k, :eigen] = total[rows, :eigen]
        out_ref[k, eigen:] = total[rows, eigen:]


def assemble(places, pieces, source, op_index, slots, eigen):
    products = op_index.shape[0]
    vmem = pl.BlockSpec(memory_space=pltpu.VMEM)
    smem = pl.BlockSpec(memory_space=pltpu.SMEM)
    return pl.pallas_call(
        functools.partial(assemble_kernel, places, [len(group) for group in pieces]),
        in_specs=[smem, smem] + [vmem] * (1 + sum(len(group) for group in pieces)),
        out_specs=vmem,
        out_shape=jax.ShapeDtypeStruct((products, 2 * eigen, eigen), BF16),
        compiler_params=pltpu.CompilerParams(vmem_limit_bytes=VMEM_LIMIT),
        cost_estimate=pl.CostEstimate(flops=1000, bytes_accessed=1000, transcendentals=0),
        name="assemble",
    )(source, op_index, slots, *[part for group in pieces for part in group])


def block_rows(parts, k):
    found = [part[0, k] for part in parts]
    return jnp.concatenate([f.reshape(-1, f.shape[-1]) for f in found], axis=0)


def times_right(blocks, masks, right, k):
    eigen = right.shape[2]
    local_cols = blocks[0][0].shape[4]
    me = lax.axis_index("col")
    per_time = eigen // local_cols
    direct = [block_rows(parts, k) for parts in blocks]
    rows = direct[0].shape[0]
    odd = iota((rows, local_cols), 0) % 2 == 1
    turned = []
    for x in direct:
        wide = x.astype(F32)
        y = jnp.where(odd, pltpu.roll(wide, 1, 0), -pltpu.roll(wide, rows - 1, 0))
        turned.append(y.astype(BF16))
    if per_time == 1:
        lhs = jnp.concatenate(
            [jnp.concatenate(direct, axis=0), jnp.concatenate(turned, axis=0)], axis=1
        )
        whole = dot(lhs, right[k]).astype(BF16)
        results = [whole[n * rows : (n + 1) * rows] for n in range(len(masks))]
    else:
        results = []
        for n, mask in enumerate(masks):
            first = pl.multiple_of(((me ^ mask) % per_time) * local_cols, local_cols)
            second = pl.multiple_of(eigen + first, local_cols)
            part = dot(direct[n], right[k, pl.ds(first, local_cols), :])
            part += dot(turned[n], right[k, pl.ds(second, local_cols), :])
            if n % per_time:
                results[-1] += part
            else:
                results.append(part)
        results = [result.astype(BF16) for result in results]
    times = [(me ^ mask) // per_time for mask in masks[::per_time]]
    return list(zip(times, results))


def near_kernel(places, masks, counts, source_ref, op_ref, slot_ref, partial_ref, *refs):
    groups, (right, done) = grouped(counts, refs)
    pieces, blocks = groups[: len(places)], groups[len(places) :]
    products, eigen = right.shape[0], right.shape[2]
    scalars = (source_ref, op_ref)
    for k in range(products):
        total = add_pieces(places, scalars, slot_ref, pieces, [k], eigen).astype(BF16)
        right[k, :eigen] = partial_ref[k, :eigen] + total[:, :eigen]
        right[k, eigen:] = partial_ref[k, eigen:] + total[:, eigen:]
    for k in range(products):
        for n, (_, result) in enumerate(times_right(blocks, masks, right, k)):
            done[k, n] = result.reshape(done.shape[2:])


def far_kernel(near_masks, masks, counts, right, near_ref, *refs):
    blocks, (out_ref, done, near_sems, sems) = grouped(counts, refs)
    products, eigen = right.shape[0], right.shape[2]
    near_times, times = near_ref.shape[1], done.shape[1]
    per_time = len(masks) // times
    me = lax.axis_index("col")

    def send(source, k, time, sem):
        at = pl.multiple_of(time * eigen, eigen)
        copy = pltpu.make_async_copy(source, out_ref.at[k, :, :, :, pl.ds(at, eigen)], sem)
        copy.start()
        return copy

    copies = []
    for k in range(products):
        for n in range(near_times):
            time = (me ^ near_masks[n * per_time]) // per_time
            copies.append(send(near_ref.at[k, n], k, time, near_sems.at[k, n]))
    for k in range(products):
        for n, (time, result) in enumerate(times_right(blocks, masks, right, k)):
            done[k, n] = result.reshape(done.shape[2:])
            copies.append(send(done.at[k, n], k, time, sems.at[k, n]))
    for copy in copies:
        copy.wait()


def flat(groups):
    return [part for group in groups for part in group]


def contract(places, pieces, partial, source, op_index, slots, blocks):
    _, products, _, own2, local_cols = blocks[0][0].shape
    n_cols = len(blocks)
    eigen = partial.shape[2]
    times = n_cols * local_cols // eigen
    near = n_cols // 2
    near_masks, far_masks = list(range(near)), list(range(near, n_cols))
    vmem = pl.BlockSpec(memory_space=pltpu.VMEM)
    smem = pl.BlockSpec(memory_space=pltpu.SMEM)
    params = pltpu.CompilerParams(vmem_limit_bytes=VMEM_LIMIT)
    cost = pl.CostEstimate(flops=1000 * 10**6, bytes_accessed=1000, transcendentals=0)
    half = (products, times // 2, NS, own2 // 2, 2, eigen)
    groups = pieces + blocks[:near]
    right, done = pl.pallas_call(
        functools.partial(near_kernel, places, near_masks, [len(g) for g in groups]),
        in_specs=[smem, smem] + [vmem] * (2 + len(flat(groups))),
        out_specs=[vmem, vmem],
        out_shape=[
            jax.ShapeDtypeStruct((products, 2 * eigen, eigen), BF16),
            jax.ShapeDtypeStruct(half, BF16),
        ],
        compiler_params=params,
        cost_estimate=cost,
        name="near",
    )(source, op_index, slots, partial, *flat(groups))
    groups = blocks[near:]
    return pl.pallas_call(
        functools.partial(far_kernel, near_masks, far_masks, [len(g) for g in groups]),
        in_specs=[vmem] * (2 + len(flat(groups))),
        out_specs=pl.BlockSpec(memory_space=pl.ANY),
        out_shape=jax.ShapeDtypeStruct((products, NS, own2 // 2, 2, times * eigen), BF16),
        scratch_shapes=[
            pltpu.VMEM(half, BF16),
            pltpu.SemaphoreType.DMA(half[:2]),
            pltpu.SemaphoreType.DMA(half[:2]),
        ],
        compiler_params=params,
        cost_estimate=cost,
        name="far",
    )(right, done, *flat(groups))


def swap(array, axis, size, mask):
    return lax.ppermute(array, axis, [(i, i ^ mask) for i in range(size)])


def after(array, *others):
    return lax.optimization_barrier((array, *others))[0]


def per_device(peramb, sink_ops, op_table, row_slot, pair_source, op_index, listed_rows):
    n_cols = lax.axis_size("col")
    n_pair = lax.axis_size("tpair")
    rows, _, eigen = op_table.shape
    slots = row_slot.reshape(-1, LANES)

    def across(array, mask):
        return swap(array, "tpair", n_pair, mask)

    def beside(array):
        return swap(array, "col", n_cols, 1)

    if n_cols != 4 or n_pair != 8 or rows % 32:
        own = jnp.concatenate([op_table[:, 0], op_table[:, 1]], axis=1)
        whole = lax.all_gather(own, "tpair", axis=0, tiled=True)
        half = whole.shape[0] // 2
        mixed = mix(op_index, listed_rows, sink_ops, peramb, [1] * n_cols)
        blocks = [[mixed[0]]] + [[swap(mixed[j], "col", n_cols, j)] for j in range(1, n_cols)]
        partial = assemble([[0]], [[whole[:half]]], pair_source, op_index, slots, eigen)
        return contract(
            [[half]], [[whole[half:]]], partial, pair_source, op_index, slots, blocks
        )
    half = rows // 2
    own = lax.dynamic_slice_in_dim(op_table, lax.axis_index("col") % 2 * half, half, 0)
    own = jnp.concatenate([own[:, 0], own[:, 1]], axis=1)
    beside_own = beside(own)
    z1 = across(own, 2)
    z2 = across(own, 4)
    x0 = across(own, 1)
    mixed = mix(op_index, listed_rows, sink_ops, peramb, [1, 1, 2])
    crossed = swap(mixed[2], "col", n_cols, 2)
    beside_mixed = beside(mixed[1])
    beside_x0 = beside(after(x0, mixed[0]))
    z12 = after(jnp.concatenate([z1, after(z2, x0)]), mixed[0])
    z3 = across(after(own, z12), 6)
    x12 = across(z12, 1)
    x3 = across(after(z3, x12, beside_x0, beside_mixed), 1)
    early = [
        ([(0, 0)], own), ([(0, 1)], beside_own),
        ([(1, 0)], x0), ([(1, 1)], beside_x0),
        ([(2, 0), (4, 0)], z12), ([(2, 1), (4, 1)], beside(z12)),
        ([(6, 0)], z3), ([(6, 1)], beside(z3)),
        ([(3, 0), (5, 0)], x12),
    ]
    places, pieces = [p for p, _ in early], [[piece] for _, piece in early]
    partial = assemble(places, pieces, pair_source, op_index, slots, eigen)
    spins = [crossed[1:, :, : NS - 1], crossed[1:, :, NS - 1 :]]
    over = [beside(after(some, partial)) for some in spins]
    blocks = [[mixed[0]], [beside_mixed], [crossed], over]
    late = [[x3], [beside(after(x3, partial))], [beside(x12)]]
    places = [[(7, 0)], [(7, 1)], [(3, 1), (5, 1)]]
    return contract(places, late, partial, pair_source, op_index, slots, blocks)


def solution(mesh):
    in_specs = (
        P("tpair", None, None, "col"),
        P("tpair", None, None, None, None),
        P("tpair", None, None),
        P(),
        P("tpair"),
        P("tpair", None),
        P("tpair", None),
    )
    out_specs = P("tpair", None, "col", None, None)
    return jax.shard_map(
        per_device, mesh=mesh, in_specs=in_specs, out_specs=out_specs, check_vma=False
    )
```

profile of v0, /device:TPU:0, one launch (start us, length us, event | category | flops | bytes accessed | tf_op | source)
XLA Modules:
  0.0 46.3 jit_solution(7111034914140406013)
XLA Ops:
  0.0 1.6 %constant_dynamic-slice_fusion = (bf16[128,1,512]{2,1,0:T(2,128)(2,1)S(1)}, bf16[128,1,512]{2,1,0:T(2,128)(2,1)S(1)}) fusion(bf16[256,2,512]{2,1,0:T(2,128)(2,1)} %param.9, s32[]{:T(128)S(6)} %select_n.11, s32[]{:T(128)S(6)} %add.9), kind=kLoop, calls=%fused_computation.4 | loop fusion | bytes 524296 | tf_op jit(solution)/shard_map/slice | solution.py:322
  1.7 0.0 copy-start.1
  1.7 4.1 %collective-permute-start.4 = (bf16[128,1024]{1,0:T(8,128)(2,1)S(1)}, bf16[128,1024]{1,0:T(8,128)(2,1)S(1)}, u32[]{:S(2)}, u32[]{:S(2)}) collective-permute-start(bf16[128,1024]{1,0:T(8,128)(2,1)S(1)} %pad_maximum_fusion.1.refs_0_), channel_id=1, source_target_pairs={{0,16},{4,20},{8,24},{12,28},{16,0},{20,4},{24,8},{28,12},{1,17},{... | collective-permute-start | bytes 786440 | tf_op jit(solution)/shard_map/ppermute | solution.py:291
  5.8 1.5 %collective-permute-start.1 = (bf16[128,1024]{1,0:T(8,128)(2,1)S(1)}, bf16[128,1024]{1,0:T(8,128)(2,1)S(1)}, u32[]{:S(2)}, u32[]{:S(2)}) collective-permute-start(bf16[128,1024]{1,0:T(8,128)(2,1)S(1)} %pad_maximum_fusion.1.refs_0_), channel_id=1, source_target_pairs={{0,4},{4,0},{8,12},{12,8},{16,20},{20,16},{24,28},{28,24},{1,5},{5... | collective-permute-start | bytes 786440 | tf_op jit(solution)/shard_map/ppermute | solution.py:291
  7.3 1.6 %collective-permute-start.3 = (bf16[128,1024]{1,0:T(8,128)(2,1)S(1)}, bf16[128,1024]{1,0:T(8,128)(2,1)S(1)}, u32[]{:S(2)}, u32[]{:S(2)}) collective-permute-start(bf16[128,1024]{1,0:T(8,128)(2,1)S(1)} %pad_maximum_fusion.1.refs_0_), channel_id=1, source_target_pairs={{0,8},{4,12},{8,0},{12,4},{16,24},{20,28},{24,16},{28,20},{1,9},{5... | collective-permute-start | bytes 786440 | tf_op jit(solution)/shard_map/ppermute | solution.py:291
  8.9 5.0 %mix.1 = (bf16[1,2,4,64,512]{4,3,2,1,0:T(8,128)(2,1)S(1)}, bf16[1,2,4,64,512]{4,3,2,1,0:T(8,128)(2,1)S(1)}, bf16[2,2,4,64,512]{4,3,2,1,0:T(8,128)(2,1)S(1)}) custom-call(s32[2,2]{1,0:T(2,128)S(1)} %copy-done.2, s32[2,128]{1,0:T(2,128)S(1)} %copy-done.3, bf16[1,2,2,512,512]{4,3,2,1,0:T(8,128)(2,1)S(1)} %copy-done, bf16[1,2,2048,512]{3,2,1,0:T(8,128)(2,1)} %peramb_ref.1), custom_call_target="tpu_custom_call" | custom-call | flops 1000 | bytes 1000 | tf_op jit(solution)/shard_map/mix/pallas_call | solution.py:88
  13.9 1.6 %collective-permute-start.13 = (bf16[2,2,4,64,512]{4,3,2,1,0:T(8,128)(2,1)S(1)}, bf16[2,2,4,64,512]{4,3,2,1,0:T(8,128)(2,1)S(1)}, u32[]{:S(2)}, u32[]{:S(2)}) collective-permute-start(bf16[2,2,4,64,512]{4,3,2,1,0:T(8,128)(2,1)S(1)} %get-tuple-element.28), channel_id=1, source_target_pairs={{0,2},{1,3},{2,0},{3,1},{4,6},{5,7},{6,4},{7,5},{8,10},{9,11},{10,... | collective-permute-start | bytes 3145736 | tf_op jit(solution)/shard_map/ppermute | solution.py:291
  15.5 0.0 collective-permute-start.9
  15.5 2.4 %collective-permute-done.4 = bf16[128,1024]{1,0:T(8,128)(2,1)S(1)} collective-permute-done((bf16[128,1024]{1,0:T(8,128)(2,1)S(1)}, bf16[128,1024]{1,0:T(8,128)(2,1)S(1)}, u32[]{:S(2)}, u32[]{:S(2)}) %collective-permute-start.4) | collective-permute-done | bytes 262176 | tf_op jit(solution)/shard_map/ppermute | solution.py:291
  17.9 0.0 collective-permute-done.1.refs_2_
  17.9 0.0 collective-permute-start.2
  17.9 1.4 %collective-permute-done.3 = bf16[128,1024]{1,0:T(8,128)(2,1)S(1)} collective-permute-done((bf16[128,1024]{1,0:T(8,128)(2,1)S(1)}, bf16[128,1024]{1,0:T(8,128)(2,1)S(1)}, u32[]{:S(2)}, u32[]{:S(2)}) %collective-permute-start.3) | collective-permute-done | bytes 262176 | tf_op jit(solution)/shard_map/ppermute | solution.py:291
  19.3 0.6 %collective-permute-start.8 = (bf16[256,1024]{1,0:T(8,128)(2,1)S(1)}, bf16[256,1024]{1,0:T(8,128)(2,1)S(1)}, u32[]{:S(2)}, u32[]{:S(2)}) collective-permute-start(bf16[256,1024]{1,0:T(8,128)(2,1)S(1)} %pad_maximum_fusion.refs_4_), channel_id=1, source_target_pairs={{0,4},{4,0},{8,12},{12,8},{16,20},{20,16},{24,28},{28,24},{1,5},{5... | collective-permute-start | bytes 1572872 | tf_op jit(solution)/shard_map/ppermute | solution.py:291
  19.9 3.0 %collective-permute-start.6 = (bf16[128,1024]{1,0:T(8,128)(2,1)S(1)}, bf16[128,1024]{1,0:T(8,128)(2,1)S(1)}, u32[]{:S(2)}, u32[]{:S(2)}) collective-permute-start(bf16[128,1024]{1,0:T(8,128)(2,1)S(1)} %pad_maximum_fusion.1.refs_0_), channel_id=1, source_target_pairs={{0,24},{4,28},{8,16},{12,20},{16,8},{20,12},{24,0},{28,4},{1,25},{... | collective-permute-start | bytes 786440 | tf_op jit(solution)/shard_map/ppermute | solution.py:291
  22.9 0.0 collective-permute-done.2.refs_3_
  22.9 6.9 %collective-permute-done.6.refs_6_ = bf16[128,1024]{1,0:T(8,128)(2,1)S(1)} collective-permute-done((bf16[128,1024]{1,0:T(8,128)(2,1)S(1)}, bf16[128,1024]{1,0:T(8,128)(2,1)S(1)}, u32[]{:S(2)}, u32[]{:S(2)}) %collective-permute-start.6) | collective-permute-done | bytes 262176 | tf_op jit(solution)/shard_map/ppermute | solution.py:291
  29.9 0.0 collective-permute-start
  29.9 0.0 collective-permute-done.9.refs_4_
  29.9 0.5 %collective-permute-start.7 = (bf16[128,1024]{1,0:T(8,128)(2,1)S(1)}, bf16[128,1024]{1,0:T(8,128)(2,1)S(1)}, u32[]{:S(2)}, u32[]{:S(2)}) collective-permute-start(bf16[128,1024]{1,0:T(8,128)(2,1)S(1)} %collective-permute-done.6.refs_6_), channel_id=1, source_target_pairs={{0,1},{1,0},{2,3},{3,2},{4,5},{5,4},{6,7},{7,6},{8,9},{9,8},{10,11... | collective-permute-start | bytes 786440 | tf_op jit(solution)/shard_map/ppermute | solution.py:291
  30.4 1.9 %collective-permute-done.8.refs_8_ = bf16[256,1024]{1,0:T(8,128)(2,1)S(1)} collective-permute-done((bf16[256,1024]{1,0:T(8,128)(2,1)S(1)}, bf16[256,1024]{1,0:T(8,128)(2,1)S(1)}, u32[]{:S(2)}, u32[]{:S(2)}) %collective-permute-start.8) | collective-permute-done | bytes 524320 | tf_op jit(solution)/shard_map/ppermute | solution.py:291
  32.3 1.5 %collective-permute-start.10 = (bf16[128,1024]{1,0:T(8,128)(2,1)S(1)}, bf16[128,1024]{1,0:T(8,128)(2,1)S(1)}, u32[]{:S(2)}, u32[]{:S(2)}) collective-permute-start(bf16[128,1024]{1,0:T(8,128)(2,1)S(1)} %collective-permute-done.6.refs_6_), channel_id=1, source_target_pairs={{0,4},{4,0},{8,12},{12,8},{16,20},{20,16},{24,28},{28,24},{1,5},{5... | collective-permute-start | bytes 786440 | tf_op jit(solution)/shard_map/ppermute | solution.py:291
  33.8 0.0 collective-permute-done.refs_1_
  34.5 0.0 collective-permute-done.5.refs_5_
  34.5 4.0 %assemble.1.partial_ref = bf16[2,1024,512]{2,1,0:T(8,128)(2,1)S(1)} custom-call(s32[1]{0:T(128)S(6)} %copy.14.source_ref, s32[2,2]{1,0:T(2,128)S(1)} %copy-done.2, s32[16,128]{1,0:T(8,128)S(1)} %bitcast.5, bf16[128,1024]{1,0:T(8,128)(2,1)S(1)} %pad_maximum_fusion.1.refs_0_, bf16[128,1024]{1,0:T(8,128)(2,1)S(1)} %collective-permute-done.refs_1_, ...), custom_call_target="tpu_custom_call" | custom-call | flops 1000 | bytes 1000 | tf_op jit(solution)/shard_map/assemble/pallas_call | solution.py:153
  38.6 0.6 %collective-permute-start.14 = (bf16[1,2,3,64,512]{4,3,2,1,0:T(8,128)(2,1)S(1)}, bf16[1,2,3,64,512]{4,3,2,1,0:T(8,128)(2,1)S(1)}, u32[]{:S(2)}, u32[]{:S(2)}) collective-permute-start(bf16[1,2,3,64,512]{4,3,2,1,0:T(8,128)(2,1)S(1)} %slice.16), channel_id=1, source_target_pairs={{0,1},{1,0},{2,3},{3,2},{4,5},{5,4},{6,7},{7,6},{8,9},{9,8},{10,11... | collective-permute-start | bytes 1179656 | tf_op jit(solution)/shard_map/ppermute | solution.py:291
  39.2 0.4 collective-permute-done.10.refs_0_
  39.5 0.0 collective-permute-start.11
  39.6 0.6 %collective-permute-start.15 = (bf16[1,2,1,64,512]{4,3,2,1,0:T(8,128)(2,1)S(1)}, bf16[1,2,1,64,512]{4,3,2,1,0:T(8,128)(2,1)S(1)}, u32[]{:S(2)}, u32[]{:S(2)}) collective-permute-start(bf16[1,2,1,64,512]{4,3,2,1,0:T(8,128)(2,1)S(1)} %slice.17), channel_id=1, source_target_pairs={{0,1},{1,0},{2,3},{3,2},{4,5},{5,4},{6,7},{7,6},{8,9},{9,8},{10,11... | collective-permute-start | bytes 393224 | tf_op jit(solution)/shard_map/ppermute | solution.py:291
  40.1 0.9 %collective-permute-done.11.refs_1_ = bf16[128,1024]{1,0:T(8,128)(2,1)S(1)} collective-permute-done((bf16[128,1024]{1,0:T(8,128)(2,1)S(1)}, bf16[128,1024]{1,0:T(8,128)(2,1)S(1)}, u32[]{:S(2)}, u32[]{:S(2)}) %collective-permute-start.11) | collective-permute-done | bytes 262176 | tf_op jit(solution)/shard_map/ppermute | solution.py:291
  41.1 3.0 %near.1 = (bf16[2,1024,512]{2,1,0:T(8,128)(2,1)S(1)}, bf16[2,2,4,32,2,512]{5,4,3,2,1,0:T(2,128)(2,1)S(1)}) custom-call(s32[1]{0:T(128)S(6)} %copy.14.source_ref, s32[2,2]{1,0:T(2,128)S(1)} %copy-done.2, s32[16,128]{1,0:T(8,128)S(1)} %bitcast.6, bf16[2,1024,512]{2,1,0:T(8,128)(2,1)S(1)} %assemble.1.partial_ref, ...), custom_call_target="tpu_custom_call" | custom-call | flops 1000000000 | bytes 1000 | tf_op jit(solution)/shard_map/near/pallas_call | solution.py:261
  44.1 0.0 collective-permute-done.14.refs_1_
  44.1 2.2 %far.1 = bf16[2,4,32,2,2048]{4,3,2,1,0:T(2,128)(2,1)} custom-call(bf16[2,1024,512]{2,1,0:T(8,128)(2,1)S(1)} %get-tuple-element.26.right, bf16[2,2,4,32,2,512]{5,4,3,2,1,0:T(2,128)(2,1)S(1)} %get-tuple-element.27.near_ref, bf16[2,2,4,64,512]{4,3,2,1,0:T(8,128)(2,1)S(1)} %collective-permute-done.13.refs_0_, ...), custom_call_target="tpu_custom_call" | custom-call | flops 1000000000 | bytes 1000 | tf_op jit(solution)/shard_map/far/pallas_call | solution.py:274
  (18 shorter events, 0.2 us)
Async XLA Ops:
  0.0 8.9 %copy-start.2 = (s32[2,2]{1,0:T(2,128)S(1)}, s32[2,2]{1,0:T(2,128)}, u32[]{:S(2)}) copy-start(s32[2,2]{1,0:T(2,128)} %op_ref.5) | copy-start | bytes 52
  0.0 8.9 %copy-start.3 = (s32[2,128]{1,0:T(2,128)S(1)}, s32[2,128]{1,0:T(2,128)}, u32[]{:S(2)}) copy-start(s32[2,128]{1,0:T(2,128)} %listed_ref.1) | copy-start | bytes 3076
  0.0 8.9 %copy-start = (bf16[1,2,2,512,512]{4,3,2,1,0:T(8,128)(2,1)S(1)}, bf16[1,2,2,512,512]{4,3,2,1,0:T(8,128)(2,1)}, u32[]{:S(2)}) copy-start(bf16[1,2,2,512,512]{4,3,2,1,0:T(8,128)(2,1)} %sink_ref.1) | copy-start | bytes 6291460
  1.7 32.8 %copy-start.1 = (s32[2048]{0:T(1024)S(1)}, s32[2048]{0:T(1024)}, u32[]{:S(2)}) copy-start(s32[2048]{0:T(1024)} %param.10) | copy-start | bytes 24580
  1.7 16.2 %collective-permute-start.4 = (bf16[128,1024]{1,0:T(8,128)(2,1)S(1)}, bf16[128,1024]{1,0:T(8,128)(2,1)S(1)}, u32[]{:S(2)}, u32[]{:S(2)}) collective-permute-start(bf16[128,1024]{1,0:T(8,128)(2,1)S(1)} %pad_maximum_fusion.1.refs_0_), channel_id=1, source_target_pairs={{0,16},{4,20},{8,24},{12,28},{16,0},{20,4},{24,8},{28,12},{1,17},{... | collective-permute-start | bytes 786440 | tf_op jit(solution)/shard_map/ppermute | solution.py:291
  5.8 12.0 %collective-permute-start.1 = (bf16[128,1024]{1,0:T(8,128)(2,1)S(1)}, bf16[128,1024]{1,0:T(8,128)(2,1)S(1)}, u32[]{:S(2)}, u32[]{:S(2)}) collective-permute-start(bf16[128,1024]{1,0:T(8,128)(2,1)S(1)} %pad_maximum_fusion.1.refs_0_), channel_id=1, source_target_pairs={{0,4},{4,0},{8,12},{12,8},{16,20},{20,16},{24,28},{28,24},{1,5},{5... | collective-permute-start | bytes 786440 | tf_op jit(solution)/shard_map/ppermute | solution.py:291
  7.3 11.9 %collective-permute-start.3 = (bf16[128,1024]{1,0:T(8,128)(2,1)S(1)}, bf16[128,1024]{1,0:T(8,128)(2,1)S(1)}, u32[]{:S(2)}, u32[]{:S(2)}) collective-permute-start(bf16[128,1024]{1,0:T(8,128)(2,1)S(1)} %pad_maximum_fusion.1.refs_0_), channel_id=1, source_target_pairs={{0,8},{4,12},{8,0},{12,4},{16,24},{20,28},{24,16},{28,20},{1,9},{5... | collective-permute-start | bytes 786440 | tf_op jit(solution)/shard_map/ppermute | solution.py:291
  13.9 24.7 %collective-permute-start.13 = (bf16[2,2,4,64,512]{4,3,2,1,0:T(8,128)(2,1)S(1)}, bf16[2,2,4,64,512]{4,3,2,1,0:T(8,128)(2,1)S(1)}, u32[]{:S(2)}, u32[]{:S(2)}) collective-permute-start(bf16[2,2,4,64,512]{4,3,2,1,0:T(8,128)(2,1)S(1)} %get-tuple-element.28), channel_id=1, source_target_pairs={{0,2},{1,3},{2,0},{3,1},{4,6},{5,7},{6,4},{7,5},{8,10},{9,11},{10,... | collective-permute-start | bytes 3145736 | tf_op jit(solution)/shard_map/ppermute | solution.py:291
  15.5 14.4 %collective-permute-start.9 = (bf16[1,2,4,64,512]{4,3,2,1,0:T(8,128)(2,1)S(1)}, bf16[1,2,4,64,512]{4,3,2,1,0:T(8,128)(2,1)S(1)}, u32[]{:S(2)}, u32[]{:S(2)}) collective-permute-start(bf16[1,2,4,64,512]{4,3,2,1,0:T(8,128)(2,1)S(1)} %get-tuple-element.23), channel_id=1, source_target_pairs={{0,1},{1,0},{2,3},{3,2},{4,5},{5,4},{6,7},{7,6},{8,9},{9,8},{10,11... | collective-permute-start | bytes 1572872 | tf_op jit(solution)/shard_map/ppermute | solution.py:291
  17.9 5.1 %collective-permute-start.2 = (bf16[128,1024]{1,0:T(8,128)(2,1)S(1)}, bf16[128,1024]{1,0:T(8,128)(2,1)S(1)}, u32[]{:S(2)}, u32[]{:S(2)}) collective-permute-start(bf16[128,1024]{1,0:T(8,128)(2,1)S(1)} %collective-permute-done.1.refs_2_), channel_id=1, source_target_pairs={{0,1},{1,0},{2,3},{3,2},{4,5},{5,4},{6,7},{7,6},{8,9},{9,8},{10,11... | collective-permute-start | bytes 786440 | tf_op jit(solution)/shard_map/ppermute | solution.py:291
  19.3 13.0 %collective-permute-start.8 = (bf16[256,1024]{1,0:T(8,128)(2,1)S(1)}, bf16[256,1024]{1,0:T(8,128)(2,1)S(1)}, u32[]{:S(2)}, u32[]{:S(2)}) collective-permute-start(bf16[256,1024]{1,0:T(8,128)(2,1)S(1)} %pad_maximum_fusion.refs_4_), channel_id=1, source_target_pairs={{0,4},{4,0},{8,12},{12,8},{16,20},{20,16},{24,28},{28,24},{1,5},{5... | collective-permute-start | bytes 1572872 | tf_op jit(solution)/shard_map/ppermute | solution.py:291
  19.9 9.9 %collective-permute-start.6 = (bf16[128,1024]{1,0:T(8,128)(2,1)S(1)}, bf16[128,1024]{1,0:T(8,128)(2,1)S(1)}, u32[]{:S(2)}, u32[]{:S(2)}) collective-permute-start(bf16[128,1024]{1,0:T(8,128)(2,1)S(1)} %pad_maximum_fusion.1.refs_0_), channel_id=1, source_target_pairs={{0,24},{4,28},{8,16},{12,20},{16,8},{20,12},{24,0},{28,4},{1,25},{... | collective-permute-start | bytes 786440 | tf_op jit(solution)/shard_map/ppermute | solution.py:291
  22.9 11.6 %collective-permute-start.5 = (bf16[256,1024]{1,0:T(8,128)(2,1)S(1)}, bf16[256,1024]{1,0:T(8,128)(2,1)S(1)}, u32[]{:S(2)}, u32[]{:S(2)}) collective-permute-start(bf16[256,1024]{1,0:T(8,128)(2,1)S(1)} %pad_maximum_fusion.refs_4_), channel_id=1, source_target_pairs={{0,1},{1,0},{2,3},{3,2},{4,5},{5,4},{6,7},{7,6},{8,9},{9,8},{10,11... | collective-permute-start | bytes 1572872 | tf_op jit(solution)/shard_map/ppermute | solution.py:291
  29.9 4.0 %collective-permute-start = (bf16[128,1024]{1,0:T(8,128)(2,1)S(1)}, bf16[128,1024]{1,0:T(8,128)(2,1)S(1)}, u32[]{:S(2)}, u32[]{:S(2)}) collective-permute-start(bf16[128,1024]{1,0:T(8,128)(2,1)S(1)} %pad_maximum_fusion.1.refs_0_), channel_id=1, source_target_pairs={{0,1},{1,0},{2,3},{3,2},{4,5},{5,4},{6,7},{7,6},{8,9},{9,8},{10,11... | collective-permute-start | bytes 786440 | tf_op jit(solution)/shard_map/ppermute | solution.py:291
  29.9 4.7 %collective-permute-start.7 = (bf16[128,1024]{1,0:T(8,128)(2,1)S(1)}, bf16[128,1024]{1,0:T(8,128)(2,1)S(1)}, u32[]{:S(2)}, u32[]{:S(2)}) collective-permute-start(bf16[128,1024]{1,0:T(8,128)(2,1)S(1)} %collective-permute-done.6.refs_6_), channel_id=1, source_target_pairs={{0,1},{1,0},{2,3},{3,2},{4,5},{5,4},{6,7},{7,6},{8,9},{9,8},{10,11... | collective-permute-start | bytes 786440 | tf_op jit(solution)/shard_map/ppermute | solution.py:291
  32.3 7.2 %collective-permute-start.10 = (bf16[128,1024]{1,0:T(8,128)(2,1)S(1)}, bf16[128,1024]{1,0:T(8,128)(2,1)S(1)}, u32[]{:S(2)}, u32[]{:S(2)}) collective-permute-start(bf16[128,1024]{1,0:T(8,128)(2,1)S(1)} %collective-permute-done.6.refs_6_), channel_id=1, source_target_pairs={{0,4},{4,0},{8,12},{12,8},{16,20},{20,16},{24,28},{28,24},{1,5},{5... | collective-permute-start | bytes 786440 | tf_op jit(solution)/shard_map/ppermute | solution.py:291
  33.9 6.3 %collective-permute-start.12 = (bf16[256,1024]{1,0:T(8,128)(2,1)S(1)}, bf16[256,1024]{1,0:T(8,128)(2,1)S(1)}, u32[]{:S(2)}, u32[]{:S(2)}) collective-permute-start(bf16[256,1024]{1,0:T(8,128)(2,1)S(1)} %collective-permute-done.8.refs_8_), channel_id=1, source_target_pairs={{0,1},{1,0},{2,3},{3,2},{4,5},{5,4},{6,7},{7,6},{8,9},{9,8},{10,11... | collective-permute-start | bytes 1572872 | tf_op jit(solution)/shard_map/ppermute | solution.py:291
  38.6 5.5 %collective-permute-start.14 = (bf16[1,2,3,64,512]{4,3,2,1,0:T(8,128)(2,1)S(1)}, bf16[1,2,3,64,512]{4,3,2,1,0:T(8,128)(2,1)S(1)}, u32[]{:S(2)}, u32[]{:S(2)}) collective-permute-start(bf16[1,2,3,64,512]{4,3,2,1,0:T(8,128)(2,1)S(1)} %slice.16), channel_id=1, source_target_pairs={{0,1},{1,0},{2,3},{3,2},{4,5},{5,4},{6,7},{7,6},{8,9},{9,8},{10,11... | collective-permute-start | bytes 1179656 | tf_op jit(solution)/shard_map/ppermute | solution.py:291
  39.5 1.5 %collective-permute-start.11 = (bf16[128,1024]{1,0:T(8,128)(2,1)S(1)}, bf16[128,1024]{1,0:T(8,128)(2,1)S(1)}, u32[]{:S(2)}, u32[]{:S(2)}) collective-permute-start(bf16[128,1024]{1,0:T(8,128)(2,1)S(1)} %collective-permute-done.10.refs_0_), channel_id=1, source_target_pairs={{0,1},{1,0},{2,3},{3,2},{4,5},{5,4},{6,7},{7,6},{8,9},{9,8},{10,11... | collective-permute-start | bytes 786440 | tf_op jit(solution)/shard_map/ppermute | solution.py:291
  39.6 4.5 %collective-permute-start.15 = (bf16[1,2,1,64,512]{4,3,2,1,0:T(8,128)(2,1)S(1)}, bf16[1,2,1,64,512]{4,3,2,1,0:T(8,128)(2,1)S(1)}, u32[]{:S(2)}, u32[]{:S(2)}) collective-permute-start(bf16[1,2,1,64,512]{4,3,2,1,0:T(8,128)(2,1)S(1)} %slice.17), channel_id=1, source_target_pairs={{0,1},{1,0},{2,3},{3,2},{4,5},{5,4},{6,7},{7,6},{8,9},{9,8},{10,11... | collective-permute-start | bytes 393224 | tf_op jit(solution)/shard_map/ppermute | solution.py:291
where the time goes:
time: 47.1 us; the launch traced here: 46.3 us
  starting transfers between devices  15.6 us (33%)
  Pallas kernels  14.2 us (30%)
  waiting for transfers between devices  14 us (30%)
  local copies, waits for them, and re-layouts  1.69 us (4%)
  between operations  0.78 us (2%)
    ppermute x16, starting transfers between devices, swap(): return lax.ppermute(array, axis, [(i, i ^ mask) for i in range(size)])  15.6 us
    ppermute x16, waiting for transfers between devices, swap(): return lax.ppermute(array, axis, [(i, i ^ mask) for i in range(size)])  14 us
    pallas_call x1, Pallas kernels, mix(): pl.pallas_call(mix_kernel, in_specs=[pl.BlockSpec(memory_space=pltpu.SMEM...  4.99 us
    pallas_call x1, Pallas kernels, assemble(): pl.pallas_call(functools.partial(assemble_kernel, places, [len(group) for...  4.01 us
    pallas_call x1, Pallas kernels, contract(): pl.pallas_call(functools.partial(near_kernel, places, near_masks, [len(g)...  2.99 us
    pallas_call x1, Pallas kernels, contract(): pl.pallas_call(functools.partial(far_kernel, near_masks, far_masks, [len(...  2.16 us
    slice x1, local copies, waits for them, and re-layouts, per_device(): own = jnp.concatenate([own[:, 0], own[:, 1]], axis=1)  1.6 us
  transfers between devices with their start and end apart: 16, of which 6 were waited for; matrix products, arithmetic and copies ran while one was open for 0% of the time, Pallas kernels for 26%

commit v1 on v0

--- a/solution.py
+++ b/solution.py
@@ -35,10 +35,12 @@
 
 
 def mix_kernel(op_ref, listed_ref, sink_ref, peramb_ref, *refs):
-    outs, (left, held, sems) = refs[:-3], refs[-3:]
+    outs, (left, sink, held, sink_sem, sems) = refs[:-5], refs[-5:]
     n_cols = sum(out.shape[0] for out in outs)
     products, listed = listed_ref.shape
     eigen, local_cols = sink_ref.shape[-1], peramb_ref.shape[-1]
+    fetch = pltpu.make_async_copy(sink_ref.at[0], sink, sink_sem)
+    fetch.start()
     loads = [
         pltpu.make_async_copy(
             peramb_ref.at[0, :, pl.ds(s * eigen, eigen), :], held.at[s], sems.at[s]
@@ -52,11 +54,12 @@
     row = iota((2 * listed, 2 * listed), 0)
     wanted = ((row // own2) ^ me) * (own2 // 2) + (row % own2) // 2 + (row % 2) * listed
     order = jnp.where(wanted == iota((2 * listed, 2 * listed), 1), 1.0, 0.0).astype(BF16)
+    onehots = [one_hot(column(listed_ref[k : k + 1, :]), 0, eigen) for k in range(products)]
+    fetch.wait()
     for k in range(products):
         op = op_ref[k, 0]
-        onehot = one_hot(column(listed_ref[k : k + 1, :]), 0, eigen)
-        real = dot(onehot, sink_ref[0, op, 0])
-        imag = dot(onehot, sink_ref[0, op, 1])
+        real = dot(onehots[k], sink[op, 0])
+        imag = dot(onehots[k], sink[op, 1])
         top = jnp.concatenate([real, -imag], axis=1)
         bottom = jnp.concatenate([imag, real], axis=1)
         both = jnp.concatenate([top, bottom], axis=0).astype(BF16)
@@ -88,19 +91,29 @@
     return pl.pallas_call(
         mix_kernel,
         in_specs=[
-            pl.BlockSpec(memory_space=pltpu.SMEM), vmem, vmem, pl.BlockSpec(memory_space=pltpu.HBM)
+            pl.BlockSpec(memory_space=pltpu.SMEM),
+            vmem,
+            pl.BlockSpec(memory_space=pltpu.HBM),
+            pl.BlockSpec(memory_space=pltpu.HBM),
         ],
         out_specs=[vmem] * len(groups),
         out_shape=blocks,
         scratch_shapes=[
             pltpu.VMEM((products * 2 * listed, 2 * eigen), BF16),
+            pltpu.VMEM(sink_ops.shape[1:], BF16),
             pltpu.VMEM((NS, 2, eigen, local_cols), BF16),
+            pltpu.SemaphoreType.DMA,
             pltpu.SemaphoreType.DMA((NS,)),
         ],
         compiler_params=pltpu.CompilerParams(vmem_limit_bytes=VMEM_LIMIT),
         cost_estimate=pl.CostEstimate(flops=1000, bytes_accessed=1000, transcendentals=0),
         name="mix",
-    )(op_index, listed_rows, sink_ops, pltpu.with_memory_space_constraint(peramb, pltpu.HBM))
+    )(
+        op_index,
+        listed_rows,
+        pltpu.with_memory_space_constraint(sink_ops, pltpu.HBM),
+        pltpu.with_memory_space_constraint(peramb, pltpu.HBM),
+    )
 
 
 def add_pieces(places, scalars_ref, slot_ref, pieces, products, eigen):
@@ -127,6 +140,10 @@
     return dot(jnp.concatenate(tiles, axis=1), jnp.concatenate(tables, axis=0))
 
 
+def flat(groups):
+    return [part for group in groups for part in group]
+
+
 def grouped(counts, refs):
     groups = []
     for count in counts:
@@ -136,29 +153,33 @@
 
 
 def assemble_kernel(places, counts, source_ref, op_ref, slot_ref, *refs):
-    pieces, (out_ref,) = grouped(counts, refs)
+    pieces, (*earlier, out_ref) = grouped(counts, refs)
     products, eigen = out_ref.shape[0], out_ref.shape[2]
-    total = add_pieces(places, (source_ref, op_ref), slot_ref, pieces, range(products), eigen)
-    total = total.astype(BF16)
-    for k in range(products):
-        rows = slice(k * eigen, (k + 1) * eigen)
-        out_ref[k, :eigen] = total[rows, :eigen]
-        out_ref[k, eigen:] = total[rows, eigen:]
-
-
-def assemble(places, pieces, source, op_index, slots, eigen):
+    for k in range(products):
+        total = add_pieces(places, (source_ref, op_ref), slot_ref, pieces, [k], eigen)
+        total = total.astype(BF16)
+        real, imag = total[:, :eigen], total[:, eigen:]
+        if earlier:
+            real += earlier[0][k, :eigen]
+            imag += earlier[0][k, eigen:]
+        out_ref[k, :eigen] = real
+        out_ref[k, eigen:] = imag
+
+
+def assemble(places, pieces, source, op_index, slots, eigen, *earlier):
     products = op_index.shape[0]
     vmem = pl.BlockSpec(memory_space=pltpu.VMEM)
     smem = pl.BlockSpec(memory_space=pltpu.SMEM)
+    inputs = [*flat(pieces), *earlier]
     return pl.pallas_call(
         functools.partial(assemble_kernel, places, [len(group) for group in pieces]),
-        in_specs=[smem, smem] + [vmem] * (1 + sum(len(group) for group in pieces)),
+        in_specs=[smem, smem] + [vmem] * (1 + len(inputs)),
         out_specs=vmem,
         out_shape=jax.ShapeDtypeStruct((products, 2 * eigen, eigen), BF16),
         compiler_params=pltpu.CompilerParams(vmem_limit_bytes=VMEM_LIMIT),
         cost_estimate=pl.CostEstimate(flops=1000, bytes_accessed=1000, transcendentals=0),
         name="assemble",
-    )(source, op_index, slots, *[part for group in pieces for part in group])
+    )(source, op_index, slots, *inputs)
 
 
 def block_rows(parts, k):
@@ -239,10 +260,6 @@
             copies.append(send(done.at[k, n], k, time, sems.at[k, n]))
     for copy in copies:
         copy.wait()
-
-
-def flat(groups):
-    return [part for group in groups for part in group]
 
 
 def contract(places, pieces, partial, source, op_index, slots, blocks):
@@ -329,7 +346,7 @@
     beside_mixed = beside(mixed[1])
     beside_x0 = beside(after(x0, mixed[0]))
     z12 = after(jnp.concatenate([z1, after(z2, x0)]), mixed[0])
-    z3 = across(after(own, z12), 6)
+    z3 = across(after(own, z12, beside_x0), 6)
     x12 = across(z12, 1)
     x3 = across(after(z3, x12, beside_x0, beside_mixed), 1)
     early = [
@@ -344,9 +361,10 @@
     spins = [crossed[1:, :, : NS - 1], crossed[1:, :, NS - 1 :]]
     over = [beside(after(some, partial)) for some in spins]
     blocks = [[mixed[0]], [beside_mixed], [crossed], over]
-    late = [[x3], [beside(after(x3, partial))], [beside(x12)]]
-    places = [[(7, 0)], [(7, 1)], [(3, 1), (5, 1)]]
-    return contract(places, late, partial, pair_source, op_index, slots, blocks)
+    last = beside(after(x3, partial))
+    places, late = [[(7, 0)], [(3, 1), (5, 1)]], [[x3], [beside(x12)]]
+    most = assemble(places, late, pair_source, op_index, slots, eigen, partial)
+    return contract([[(7, 1)]], [[last]], most, pair_source, op_index, slots, blocks)
 
 
 def solution(mesh):

time: 47.1 us -> 48.4 us (1.028); the launches traced: 46.3 us -> 48.3 us
  Pallas kernels: 14.2 us -> 17.5 us
  starting transfers between devices: 15.6 us -> 14.3 us
    pallas_call x1, Pallas kernels: 4.99 us -> 6.97 us  [mix(): pl.pallas_call(mix_kernel, in_specs=[pl.BlockSpec(memory_space=pltpu.SMEM...]
    pallas_call x1 -> x2, Pallas kernels: 4.01 us -> 5.91 us  [assemble(): pl.pallas_call(functools.partial(assemble_kernel, places, [len(group) for...]
    ppermute x16, starting transfers between devices: 15.6 us -> 14.3 us  [swap(): return lax.ppermute(array, axis, [(i, i ^ mask) for i in range(size)])]
    pallas_call x1, Pallas kernels: 2.99 us -> 2.46 us  [contract(): pl.pallas_call(functools.partial(near_kernel, places, near_masks, [len(g)...]
  transfers between devices with their start and end apart: 16 -> 16, of which waited for: 6 -> 7; matrix products, arithmetic and copies ran while one was open for 0% -> 0% of each run, Pallas kernels for 26% -> 32%
where the time goes in v1:
time: 48.4 us; the launch traced here: 48.3 us
  Pallas kernels  17.5 us (36%)
  starting transfers between devices  14.3 us (30%)
  waiting for transfers between devices  14 us (29%)
  local copies, waits for them, and re-layouts  1.57 us (3%)
  between operations  0.8 us (2%)
    ppermute x16, starting transfers between devices, swap(): return lax.ppermute(array, axis, [(i, i ^ mask) for i in range(size)])  14.3 us
    ppermute x16, waiting for transfers between devices, swap(): return lax.ppermute(array, axis, [(i, i ^ mask) for i in range(size)])  14 us
    pallas_call x1, Pallas kernels, mix(): pl.pallas_call(mix_kernel, in_specs=[pl.BlockSpec(memory_space=pltpu.SMEM...  6.97 us
    pallas_call x2, Pallas kernels, assemble(): pl.pallas_call(functools.partial(assemble_kernel, places, [len(group) for...  5.91 us
    pallas_call x1, Pallas kernels, contract(): pl.pallas_call(functools.partial(near_kernel, places, near_masks, [len(g)...  2.46 us
    pallas_call x1, Pallas kernels, contract(): pl.pallas_call(functools.partial(far_kernel, near_masks, far_masks, [len(...  2.16 us
    slice x1, local copies, waits for them, and re-layouts, per_device(): own = jnp.concatenate([own[:, 0], own[:, 1]], axis=1)  1.48 us
  transfers between devices with their start and end apart: 16, of which 7 were waited for; matrix products, arithmetic and copies ran while one was open for 0% of the time, Pallas kernels for 32%

profile of v1, /device:TPU:0, one launch (start us, length us, event | category | flops | bytes accessed | tf_op | source)
XLA Modules:
  0.0 48.3 jit_solution(2846497392109293056)
XLA Ops:
  0.0 1.5 %constant_dynamic-slice_fusion = (bf16[128,1,512]{2,1,0:T(2,128)(2,1)S(1)}, bf16[128,1,512]{2,1,0:T(2,128)(2,1)S(1)}) fusion(bf16[256,2,512]{2,1,0:T(2,128)(2,1)} %param.9, s32[]{:T(128)S(6)} %select_n.11, s32[]{:T(128)S(6)} %add.9), kind=kLoop, calls=%fused_computation.4 | loop fusion | bytes 524296 | tf_op jit(solution)/shard_map/slice | solution.py:339
  1.6 0.0 copy-start
  1.6 3.0 %collective-permute-start.2 = (bf16[128,1024]{1,0:T(8,128)(2,1)S(1)}, bf16[128,1024]{1,0:T(8,128)(2,1)S(1)}, u32[]{:S(2)}, u32[]{:S(2)}) collective-permute-start(bf16[128,1024]{1,0:T(8,128)(2,1)S(1)} %pad_maximum_fusion.1.refs_0_), channel_id=1, source_target_pairs={{0,4},{4,0},{8,12},{12,8},{16,20},{20,16},{24,28},{28,24},{1,5},{5... | collective-permute-start | bytes 786440 | tf_op jit(solution)/shard_map/ppermute | solution.py:308
  4.6 2.6 %collective-permute-start.1 = (bf16[128,1024]{1,0:T(8,128)(2,1)S(1)}, bf16[128,1024]{1,0:T(8,128)(2,1)S(1)}, u32[]{:S(2)}, u32[]{:S(2)}) collective-permute-start(bf16[128,1024]{1,0:T(8,128)(2,1)S(1)} %pad_maximum_fusion.1.refs_0_), channel_id=1, source_target_pairs={{0,16},{4,20},{8,24},{12,28},{16,0},{20,4},{24,8},{28,12},{1,17},{... | collective-permute-start | bytes 786440 | tf_op jit(solution)/shard_map/ppermute | solution.py:308
  7.2 1.6 %collective-permute-start = (bf16[128,1024]{1,0:T(8,128)(2,1)S(1)}, bf16[128,1024]{1,0:T(8,128)(2,1)S(1)}, u32[]{:S(2)}, u32[]{:S(2)}) collective-permute-start(bf16[128,1024]{1,0:T(8,128)(2,1)S(1)} %pad_maximum_fusion.1.refs_0_), channel_id=1, source_target_pairs={{0,8},{4,12},{8,0},{12,4},{16,24},{20,28},{24,16},{28,20},{1,9},{5... | collective-permute-start | bytes 786440 | tf_op jit(solution)/shard_map/ppermute | solution.py:308
  8.8 7.0 %mix.1 = (bf16[1,2,4,64,512]{4,3,2,1,0:T(8,128)(2,1)S(1)}, bf16[1,2,4,64,512]{4,3,2,1,0:T(8,128)(2,1)S(1)}, bf16[2,2,4,64,512]{4,3,2,1,0:T(8,128)(2,1)S(1)}) custom-call(s32[2,2]{1,0:T(2,128)S(1)} %copy-done.1, s32[2,128]{1,0:T(2,128)S(1)} %copy-done.2, bf16[1,2,2,512,512]{4,3,2,1,0:T(8,128)(2,1)} %sink_ref.1, bf16[1,2,2048,512]{3,2,1,0:T(8,128)(2,1)} %peramb_ref.1), custom_call_target="tpu_custom_call" | custom-call | flops 1000 | bytes 1000 | tf_op jit(solution)/shard_map/mix/pallas_call | solution.py:91
  15.7 1.6 %collective-permute-start.13 = (bf16[2,2,4,64,512]{4,3,2,1,0:T(8,128)(2,1)S(1)}, bf16[2,2,4,64,512]{4,3,2,1,0:T(8,128)(2,1)S(1)}, u32[]{:S(2)}, u32[]{:S(2)}) collective-permute-start(bf16[2,2,4,64,512]{4,3,2,1,0:T(8,128)(2,1)S(1)} %get-tuple-element.28), channel_id=1, source_target_pairs={{0,2},{1,3},{2,0},{3,1},{4,6},{5,7},{6,4},{7,5},{8,10},{9,11},{10,... | collective-permute-start | bytes 3145736 | tf_op jit(solution)/shard_map/ppermute | solution.py:308
  17.3 0.0 collective-permute-start.6
  17.3 0.0 collective-permute-done.2.refs_2_
  17.3 1.6 %collective-permute-done.1 = bf16[128,1024]{1,0:T(8,128)(2,1)S(1)} collective-permute-done((bf16[128,1024]{1,0:T(8,128)(2,1)S(1)}, bf16[128,1024]{1,0:T(8,128)(2,1)S(1)}, u32[]{:S(2)}, u32[]{:S(2)}) %collective-permute-start.1) | collective-permute-done | bytes 262176 | tf_op jit(solution)/shard_map/ppermute | solution.py:308
  19.0 0.0 collective-permute-start.3
  19.0 0.2 collective-permute-done
  19.2 0.5 %collective-permute-start.5 = (bf16[256,1024]{1,0:T(8,128)(2,1)S(1)}, bf16[256,1024]{1,0:T(8,128)(2,1)S(1)}, u32[]{:S(2)}, u32[]{:S(2)}) collective-permute-start(bf16[256,1024]{1,0:T(8,128)(2,1)S(1)} %pad_maximum_fusion.refs_4_), channel_id=1, source_target_pairs={{0,4},{4,0},{8,12},{12,8},{16,20},{20,16},{24,28},{28,24},{1,5},{5... | collective-permute-start | bytes 1572872 | tf_op jit(solution)/shard_map/ppermute | solution.py:308
  19.7 0.8 %collective-permute-done.3.refs_3_ = bf16[128,1024]{1,0:T(8,128)(2,1)S(1)} collective-permute-done((bf16[128,1024]{1,0:T(8,128)(2,1)S(1)}, bf16[128,1024]{1,0:T(8,128)(2,1)S(1)}, u32[]{:S(2)}, u32[]{:S(2)}) %collective-permute-start.3) | collective-permute-done | bytes 262176 | tf_op jit(solution)/shard_map/ppermute | solution.py:308
  20.5 3.4 %collective-permute-start.4 = (bf16[128,1024]{1,0:T(8,128)(2,1)S(1)}, bf16[128,1024]{1,0:T(8,128)(2,1)S(1)}, u32[]{:S(2)}, u32[]{:S(2)}) collective-permute-start(bf16[128,1024]{1,0:T(8,128)(2,1)S(1)} %pad_maximum_fusion.1.refs_0_), channel_id=1, source_target_pairs={{0,24},{4,28},{8,16},{12,20},{16,8},{20,12},{24,0},{28,4},{1,25},{... | collective-permute-start | bytes 786440 | tf_op jit(solution)/shard_map/ppermute | solution.py:308
  23.9 0.0 collective-permute-start.10
  23.9 0.0 collective-permute-done.6.refs_2_
  23.9 0.5 %collective-permute-start.9 = (bf16[128,1024]{1,0:T(8,128)(2,1)S(1)}, bf16[128,1024]{1,0:T(8,128)(2,1)S(1)}, u32[]{:S(2)}, u32[]{:S(2)}) collective-permute-start(bf16[128,1024]{1,0:T(8,128)(2,1)S(1)} %pad_maximum_fusion.1.refs_0_), channel_id=1, source_target_pairs={{0,1},{1,0},{2,3},{3,2},{4,5},{5,4},{6,7},{7,6},{8,9},{9,8},{10,11... | collective-permute-start | bytes 786440 | tf_op jit(solution)/shard_map/ppermute | solution.py:308
  24.4 6.4 %collective-permute-done.4.refs_6_ = bf16[128,1024]{1,0:T(8,128)(2,1)S(1)} collective-permute-done((bf16[128,1024]{1,0:T(8,128)(2,1)S(1)}, bf16[128,1024]{1,0:T(8,128)(2,1)S(1)}, u32[]{:S(2)}, u32[]{:S(2)}) %collective-permute-start.4) | collective-permute-done | bytes 262176 | tf_op jit(solution)/shard_map/ppermute | solution.py:308
  30.8 0.0 collective-permute-start.11
  30.8 2.7 %collective-permute-done.5.refs_8_ = bf16[256,1024]{1,0:T(8,128)(2,1)S(1)} collective-permute-done((bf16[256,1024]{1,0:T(8,128)(2,1)S(1)}, bf16[256,1024]{1,0:T(8,128)(2,1)S(1)}, u32[]{:S(2)}, u32[]{:S(2)}) %collective-permute-start.5) | collective-permute-done | bytes 524320 | tf_op jit(solution)/shard_map/ppermute | solution.py:308
  33.4 0.5 %collective-permute-start.7 = (bf16[128,1024]{1,0:T(8,128)(2,1)S(1)}, bf16[128,1024]{1,0:T(8,128)(2,1)S(1)}, u32[]{:S(2)}, u32[]{:S(2)}) collective-permute-start(bf16[128,1024]{1,0:T(8,128)(2,1)S(1)} %collective-permute-done.4.refs_6_), channel_id=1, source_target_pairs={{0,4},{4,0},{8,12},{12,8},{16,20},{20,16},{24,28},{28,24},{1,5},{5... | collective-permute-start | bytes 786440 | tf_op jit(solution)/shard_map/ppermute | solution.py:308
  33.9 0.0 collective-permute-done.9.refs_1_
  33.9 0.0 collective-permute-start.8
  34.6 4.0 %assemble.2.refs_2_ = bf16[2,1024,512]{2,1,0:T(8,128)(2,1)S(1)} custom-call(s32[1]{0:T(128)S(6)} %copy.14.source_ref, s32[2,2]{1,0:T(2,128)S(1)} %copy-done.1, s32[16,128]{1,0:T(8,128)S(1)} %bitcast.5, bf16[128,1024]{1,0:T(8,128)(2,1)S(1)} %pad_maximum_fusion.1.refs_0_, bf16[128,1024]{1,0:T(8,128)(2,1)S(1)} %collective-permute-done.9.refs_1_, ...), custom_call_target="tpu_custom_call" | custom-call | flops 1000 | bytes 1000 | tf_op jit(solution)/shard_map/assemble/pallas_call | solution.py:174
  38.6 1.2 %collective-permute-done.13.refs_0_ = bf16[2,2,4,64,512]{4,3,2,1,0:T(8,128)(2,1)S(1)} collective-permute-done((bf16[2,2,4,64,512]{4,3,2,1,0:T(8,128)(2,1)S(1)}, bf16[2,2,4,64,512]{4,3,2,1,0:T(8,128)(2,1)S(1)}, u32[]{:S(2)}, u32[]{:S(2)}) %collective-permute-start.13) | collective-permute-done | bytes 1048608 | tf_op jit(solution)/shard_map/ppermute | solution.py:308
  39.9 0.1 collective-permute-start.14
  40.0 1.2 %collective-permute-done.7.refs_0_ = bf16[128,1024]{1,0:T(8,128)(2,1)S(1)} collective-permute-done((bf16[128,1024]{1,0:T(8,128)(2,1)S(1)}, bf16[128,1024]{1,0:T(8,128)(2,1)S(1)}, u32[]{:S(2)}, u32[]{:S(2)}) %collective-permute-start.7) | collective-permute-done | bytes 262176 | tf_op jit(solution)/shard_map/ppermute | solution.py:308
  41.2 0.6 %collective-permute-start.15 = (bf16[1,2,1,64,512]{4,3,2,1,0:T(8,128)(2,1)S(1)}, bf16[1,2,1,64,512]{4,3,2,1,0:T(8,128)(2,1)S(1)}, u32[]{:S(2)}, u32[]{:S(2)}) collective-permute-start(bf16[1,2,1,64,512]{4,3,2,1,0:T(8,128)(2,1)S(1)} %slice.17), channel_id=1, source_target_pairs={{0,1},{1,0},{2,3},{3,2},{4,5},{5,4},{6,7},{7,6},{8,9},{9,8},{10,11... | collective-permute-start | bytes 393224 | tf_op jit(solution)/shard_map/ppermute | solution.py:308
  41.7 1.9 %assemble.3.partial_ref = bf16[2,1024,512]{2,1,0:T(8,128)(2,1)S(1)} custom-call(s32[1]{0:T(128)S(6)} %copy.14.source_ref, s32[2,2]{1,0:T(2,128)S(1)} %copy-done.1, s32[16,128]{1,0:T(8,128)S(1)} %bitcast.6, bf16[128,1024]{1,0:T(8,128)(2,1)S(1)} %collective-permute-done.7.refs_0_, bf16[256,1024]{1,0:T(8,128)(2,1)S(1)} %collective-permute-done.8.refs_1_, ...), custom_call_target="tpu_custom_call" | custom-call | flops 1000 | bytes 1000 | tf_op jit(solution)/shard_map/assemble/pallas_call | solution.py:174
  43.6 2.5 %near.1 = (bf16[2,1024,512]{2,1,0:T(8,128)(2,1)S(1)}, bf16[2,2,4,32,2,512]{5,4,3,2,1,0:T(2,128)(2,1)S(1)}) custom-call(s32[1]{0:T(128)S(6)} %copy.14.source_ref, s32[2,2]{1,0:T(2,128)S(1)} %copy-done.1, s32[16,128]{1,0:T(8,128)S(1)} %bitcast.7, bf16[2,1024,512]{2,1,0:T(8,128)(2,1)S(1)} %assemble.3.partial_ref, ...), custom_call_target="tpu_custom_call" | custom-call | flops 1000000000 | bytes 1000 | tf_op jit(solution)/shard_map/near/pallas_call | solution.py:278
  46.1 2.2 %far.1 = bf16[2,4,32,2,2048]{4,3,2,1,0:T(2,128)(2,1)} custom-call(bf16[2,1024,512]{2,1,0:T(8,128)(2,1)S(1)} %get-tuple-element.26.right, bf16[2,2,4,32,2,512]{5,4,3,2,1,0:T(2,128)(2,1)S(1)} %get-tuple-element.27.near_ref, bf16[2,2,4,64,512]{4,3,2,1,0:T(8,128)(2,1)S(1)} %collective-permute-done.13.refs_0_, ...), custom_call_target="tpu_custom_call" | custom-call | flops 1000000000 | bytes 1000 | tf_op jit(solution)/shard_map/far/pallas_call | solution.py:291
  (17 shorter events, 0.2 us)
Async XLA Ops:
  0.0 8.7 %copy-start.1 = (s32[2,2]{1,0:T(2,128)S(1)}, s32[2,2]{1,0:T(2,128)}, u32[]{:S(2)}) copy-start(s32[2,2]{1,0:T(2,128)} %op_ref.7) | copy-start | bytes 52
  0.0 8.7 %copy-start.2 = (s32[2,128]{1,0:T(2,128)S(1)}, s32[2,128]{1,0:T(2,128)}, u32[]{:S(2)}) copy-start(s32[2,128]{1,0:T(2,128)} %listed_ref.1) | copy-start | bytes 3076
  1.6 33.0 %copy-start = (s32[2048]{0:T(1024)S(1)}, s32[2048]{0:T(1024)}, u32[]{:S(2)}) copy-start(s32[2048]{0:T(1024)} %param.10) | copy-start | bytes 24580
  1.6 15.8 %collective-permute-start.2 = (bf16[128,1024]{1,0:T(8,128)(2,1)S(1)}, bf16[128,1024]{1,0:T(8,128)(2,1)S(1)}, u32[]{:S(2)}, u32[]{:S(2)}) collective-permute-start(bf16[128,1024]{1,0:T(8,128)(2,1)S(1)} %pad_maximum_fusion.1.refs_0_), channel_id=1, source_target_pairs={{0,4},{4,0},{8,12},{12,8},{16,20},{20,16},{24,28},{28,24},{1,5},{5... | collective-permute-start | bytes 786440 | tf_op jit(solution)/shard_map/ppermute | solution.py:308
  4.6 14.4 %collective-permute-start.1 = (bf16[128,1024]{1,0:T(8,128)(2,1)S(1)}, bf16[128,1024]{1,0:T(8,128)(2,1)S(1)}, u32[]{:S(2)}, u32[]{:S(2)}) collective-permute-start(bf16[128,1024]{1,0:T(8,128)(2,1)S(1)} %pad_maximum_fusion.1.refs_0_), channel_id=1, source_target_pairs={{0,16},{4,20},{8,24},{12,28},{16,0},{20,4},{24,8},{28,12},{1,17},{... | collective-permute-start | bytes 786440 | tf_op jit(solution)/shard_map/ppermute | solution.py:308
  7.2 12.0 %collective-permute-start = (bf16[128,1024]{1,0:T(8,128)(2,1)S(1)}, bf16[128,1024]{1,0:T(8,128)(2,1)S(1)}, u32[]{:S(2)}, u32[]{:S(2)}) collective-permute-start(bf16[128,1024]{1,0:T(8,128)(2,1)S(1)} %pad_maximum_fusion.1.refs_0_), channel_id=1, source_target_pairs={{0,8},{4,12},{8,0},{12,4},{16,24},{20,28},{24,16},{28,20},{1,9},{5... | collective-permute-start | bytes 786440 | tf_op jit(solution)/shard_map/ppermute | solution.py:308
  15.7 24.1 %collective-permute-start.13 = (bf16[2,2,4,64,512]{4,3,2,1,0:T(8,128)(2,1)S(1)}, bf16[2,2,4,64,512]{4,3,2,1,0:T(8,128)(2,1)S(1)}, u32[]{:S(2)}, u32[]{:S(2)}) collective-permute-start(bf16[2,2,4,64,512]{4,3,2,1,0:T(8,128)(2,1)S(1)} %get-tuple-element.28), channel_id=1, source_target_pairs={{0,2},{1,3},{2,0},{3,1},{4,6},{5,7},{6,4},{7,5},{8,10},{9,11},{10,... | collective-permute-start | bytes 3145736 | tf_op jit(solution)/shard_map/ppermute | solution.py:308
  17.3 6.6 %collective-permute-start.6 = (bf16[1,2,4,64,512]{4,3,2,1,0:T(8,128)(2,1)S(1)}, bf16[1,2,4,64,512]{4,3,2,1,0:T(8,128)(2,1)S(1)}, u32[]{:S(2)}, u32[]{:S(2)}) collective-permute-start(bf16[1,2,4,64,512]{4,3,2,1,0:T(8,128)(2,1)S(1)} %get-tuple-element.23), channel_id=1, source_target_pairs={{0,1},{1,0},{2,3},{3,2},{4,5},{5,4},{6,7},{7,6},{8,9},{9,8},{10,11... | collective-permute-start | bytes 1572872 | tf_op jit(solution)/shard_map/ppermute | solution.py:308
  19.0 1.5 %collective-permute-start.3 = (bf16[128,1024]{1,0:T(8,128)(2,1)S(1)}, bf16[128,1024]{1,0:T(8,128)(2,1)S(1)}, u32[]{:S(2)}, u32[]{:S(2)}) collective-permute-start(bf16[128,1024]{1,0:T(8,128)(2,1)S(1)} %collective-permute-done.2.refs_2_), channel_id=1, source_target_pairs={{0,1},{1,0},{2,3},{3,2},{4,5},{5,4},{6,7},{7,6},{8,9},{9,8},{10,11... | collective-permute-start | bytes 786440 | tf_op jit(solution)/shard_map/ppermute | solution.py:308
  19.2 14.2 %collective-permute-start.5 = (bf16[256,1024]{1,0:T(8,128)(2,1)S(1)}, bf16[256,1024]{1,0:T(8,128)(2,1)S(1)}, u32[]{:S(2)}, u32[]{:S(2)}) collective-permute-start(bf16[256,1024]{1,0:T(8,128)(2,1)S(1)} %pad_maximum_fusion.refs_4_), channel_id=1, source_target_pairs={{0,4},{4,0},{8,12},{12,8},{16,20},{20,16},{24,28},{28,24},{1,5},{5... | collective-permute-start | bytes 1572872 | tf_op jit(solution)/shard_map/ppermute | solution.py:308
  20.5 10.3 %collective-permute-start.4 = (bf16[128,1024]{1,0:T(8,128)(2,1)S(1)}, bf16[128,1024]{1,0:T(8,128)(2,1)S(1)}, u32[]{:S(2)}, u32[]{:S(2)}) collective-permute-start(bf16[128,1024]{1,0:T(8,128)(2,1)S(1)} %pad_maximum_fusion.1.refs_0_), channel_id=1, source_target_pairs={{0,24},{4,28},{8,16},{12,20},{16,8},{20,12},{24,0},{28,4},{1,25},{... | collective-permute-start | bytes 786440 | tf_op jit(solution)/shard_map/ppermute | solution.py:308
  23.9 10.7 %collective-permute-start.10 = (bf16[256,1024]{1,0:T(8,128)(2,1)S(1)}, bf16[256,1024]{1,0:T(8,128)(2,1)S(1)}, u32[]{:S(2)}, u32[]{:S(2)}) collective-permute-start(bf16[256,1024]{1,0:T(8,128)(2,1)S(1)} %pad_maximum_fusion.refs_4_), channel_id=1, source_target_pairs={{0,1},{1,0},{2,3},{3,2},{4,5},{5,4},{6,7},{7,6},{8,9},{9,8},{10,11... | collective-permute-start | bytes 1572872 | tf_op jit(solution)/shard_map/ppermute | solution.py:308
  23.9 10.0 %collective-permute-start.9 = (bf16[128,1024]{1,0:T(8,128)(2,1)S(1)}, bf16[128,1024]{1,0:T(8,128)(2,1)S(1)}, u32[]{:S(2)}, u32[]{:S(2)}) collective-permute-start(bf16[128,1024]{1,0:T(8,128)(2,1)S(1)} %pad_maximum_fusion.1.refs_0_), channel_id=1, source_target_pairs={{0,1},{1,0},{2,3},{3,2},{4,5},{5,4},{6,7},{7,6},{8,9},{9,8},{10,11... | collective-permute-start | bytes 786440 | tf_op jit(solution)/shard_map/ppermute | solution.py:308
  30.8 3.8 %collective-permute-start.11 = (bf16[128,1024]{1,0:T(8,128)(2,1)S(1)}, bf16[128,1024]{1,0:T(8,128)(2,1)S(1)}, u32[]{:S(2)}, u32[]{:S(2)}) collective-permute-start(bf16[128,1024]{1,0:T(8,128)(2,1)S(1)} %collective-permute-done.4.refs_6_), channel_id=1, source_target_pairs={{0,1},{1,0},{2,3},{3,2},{4,5},{5,4},{6,7},{7,6},{8,9},{9,8},{10,11... | collective-permute-start | bytes 786440 | tf_op jit(solution)/shard_map/ppermute | solution.py:308
  33.4 7.7 %collective-permute-start.7 = (bf16[128,1024]{1,0:T(8,128)(2,1)S(1)}, bf16[128,1024]{1,0:T(8,128)(2,1)S(1)}, u32[]{:S(2)}, u32[]{:S(2)}) collective-permute-start(bf16[128,1024]{1,0:T(8,128)(2,1)S(1)} %collective-permute-done.4.refs_6_), channel_id=1, source_target_pairs={{0,4},{4,0},{8,12},{12,8},{16,20},{20,16},{24,28},{28,24},{1,5},{5... | collective-permute-start | bytes 786440 | tf_op jit(solution)/shard_map/ppermute | solution.py:308
  33.9 7.8 %collective-permute-start.8 = (bf16[256,1024]{1,0:T(8,128)(2,1)S(1)}, bf16[256,1024]{1,0:T(8,128)(2,1)S(1)}, u32[]{:S(2)}, u32[]{:S(2)}) collective-permute-start(bf16[256,1024]{1,0:T(8,128)(2,1)S(1)} %collective-permute-done.5.refs_8_), channel_id=1, source_target_pairs={{0,1},{1,0},{2,3},{3,2},{4,5},{5,4},{6,7},{7,6},{8,9},{9,8},{10,11... | collective-permute-start | bytes 1572872 | tf_op jit(solution)/shard_map/ppermute | solution.py:308
  39.9 6.2 %collective-permute-start.14 = (bf16[1,2,3,64,512]{4,3,2,1,0:T(8,128)(2,1)S(1)}, bf16[1,2,3,64,512]{4,3,2,1,0:T(8,128)(2,1)S(1)}, u32[]{:S(2)}, u32[]{:S(2)}) collective-permute-start(bf16[1,2,3,64,512]{4,3,2,1,0:T(8,128)(2,1)S(1)} %slice.16), channel_id=1, source_target_pairs={{0,1},{1,0},{2,3},{3,2},{4,5},{5,4},{6,7},{7,6},{8,9},{9,8},{10,11... | collective-permute-start | bytes 1179656 | tf_op jit(solution)/shard_map/ppermute | solution.py:308
  41.1 2.5 %collective-permute-start.12 = (bf16[128,1024]{1,0:T(8,128)(2,1)S(1)}, bf16[128,1024]{1,0:T(8,128)(2,1)S(1)}, u32[]{:S(2)}, u32[]{:S(2)}) collective-permute-start(bf16[128,1024]{1,0:T(8,128)(2,1)S(1)} %collective-permute-done.7.refs_0_), channel_id=1, source_target_pairs={{0,1},{1,0},{2,3},{3,2},{4,5},{5,4},{6,7},{7,6},{8,9},{9,8},{10,11... | collective-permute-start | bytes 786440 | tf_op jit(solution)/shard_map/ppermute | solution.py:308
  41.2 4.9 %collective-permute-start.15 = (bf16[1,2,1,64,512]{4,3,2,1,0:T(8,128)(2,1)S(1)}, bf16[1,2,1,64,512]{4,3,2,1,0:T(8,128)(2,1)S(1)}, u32[]{:S(2)}, u32[]{:S(2)}) collective-permute-start(bf16[1,2,1,64,512]{4,3,2,1,0:T(8,128)(2,1)S(1)} %slice.17), channel_id=1, source_target_pairs={{0,1},{1,0},{2,3},{3,2},{4,5},{5,4},{6,7},{7,6},{8,9},{9,8},{10,11... | collective-permute-start | bytes 393224 | tf_op jit(solution)/shard_map/ppermute | solution.py:308

commit v2 on v1

--- a/solution.py
+++ b/solution.py
@@ -35,31 +35,28 @@
 
 
 def mix_kernel(op_ref, listed_ref, sink_ref, peramb_ref, *refs):
-    outs, (left, sink, held, sink_sem, sems) = refs[:-5], refs[-5:]
+    outs, (left, held, sems) = refs[:-3], refs[-3:]
     n_cols = sum(out.shape[0] for out in outs)
     products, listed = listed_ref.shape
     eigen, local_cols = sink_ref.shape[-1], peramb_ref.shape[-1]
-    fetch = pltpu.make_async_copy(sink_ref.at[0], sink, sink_sem)
-    fetch.start()
     loads = [
         pltpu.make_async_copy(
             peramb_ref.at[0, :, pl.ds(s * eigen, eigen), :], held.at[s], sems.at[s]
         )
         for s in range(NS)
     ]
-    for load in loads:
+    for load in loads[:2]:
         load.start()
     own2 = 2 * listed // n_cols
     me = lax.axis_index("col")
     row = iota((2 * listed, 2 * listed), 0)
     wanted = ((row // own2) ^ me) * (own2 // 2) + (row % own2) // 2 + (row % 2) * listed
     order = jnp.where(wanted == iota((2 * listed, 2 * listed), 1), 1.0, 0.0).astype(BF16)
-    onehots = [one_hot(column(listed_ref[k : k + 1, :]), 0, eigen) for k in range(products)]
-    fetch.wait()
     for k in range(products):
         op = op_ref[k, 0]
-        real = dot(onehots[k], sink[op, 0])
-        imag = dot(onehots[k], sink[op, 1])
+        onehot = one_hot(column(listed_ref[k : k + 1, :]), 0, eigen)
+        real = dot(onehot, sink_ref[0, op, 0])
+        imag = dot(onehot, sink_ref[0, op, 1])
         top = jnp.concatenate([real, -imag], axis=1)
         bottom = jnp.concatenate([imag, real], axis=1)
         both = jnp.concatenate([top, bottom], axis=0).astype(BF16)
@@ -69,6 +66,8 @@
             left[at : at + own2, :] = rows[j * own2 : (j + 1) * own2]
     for s in range(NS):
         loads[s].wait()
+        if s + 2 < NS:
+            loads[s + 2].start()
         mixed = dot(left[...], held[s].reshape(2 * eigen, local_cols)).astype(BF16)
         j = 0
         for out in outs:
@@ -91,29 +90,19 @@
     return pl.pallas_call(
         mix_kernel,
         in_specs=[
-            pl.BlockSpec(memory_space=pltpu.SMEM),
-            vmem,
-            pl.BlockSpec(memory_space=pltpu.HBM),
-            pl.BlockSpec(memory_space=pltpu.HBM),
+            pl.BlockSpec(memory_space=pltpu.SMEM), vmem, vmem, pl.BlockSpec(memory_space=pltpu.HBM)
         ],
         out_specs=[vmem] * len(groups),
         out_shape=blocks,
         scratch_shapes=[
             pltpu.VMEM((products * 2 * listed, 2 * eigen), BF16),
-            pltpu.VMEM(sink_ops.shape[1:], BF16),
             pltpu.VMEM((NS, 2, eigen, local_cols), BF16),
-            pltpu.SemaphoreType.DMA,
             pltpu.SemaphoreType.DMA((NS,)),
         ],
         compiler_params=pltpu.CompilerParams(vmem_limit_bytes=VMEM_LIMIT),
         cost_estimate=pl.CostEstimate(flops=1000, bytes_accessed=1000, transcendentals=0),
         name="mix",
-    )(
-        op_index,
-        listed_rows,
-        pltpu.with_memory_space_constraint(sink_ops, pltpu.HBM),
-        pltpu.with_memory_space_constraint(peramb, pltpu.HBM),
-    )
+    )(op_index, listed_rows, sink_ops, pltpu.with_memory_space_constraint(peramb, pltpu.HBM))
 
 
 def add_pieces(places, scalars_ref, slot_ref, pieces, products, eigen):
@@ -348,23 +337,27 @@
     z12 = after(jnp.concatenate([z1, after(z2, x0)]), mixed[0])
     z3 = across(after(own, z12, beside_x0), 6)
     x12 = across(z12, 1)
-    x3 = across(after(z3, x12, beside_x0, beside_mixed), 1)
-    early = [
+    spread = [
         ([(0, 0)], own), ([(0, 1)], beside_own),
         ([(1, 0)], x0), ([(1, 1)], beside_x0),
         ([(2, 0), (4, 0)], z12), ([(2, 1), (4, 1)], beside(z12)),
-        ([(6, 0)], z3), ([(6, 1)], beside(z3)),
-        ([(3, 0), (5, 0)], x12),
     ]
-    places, pieces = [p for p, _ in early], [[piece] for _, piece in early]
-    partial = assemble(places, pieces, pair_source, op_index, slots, eigen)
+
+    def add(found, *earlier):
+        places, pieces = [p for p, _ in found], [[piece] for _, piece in found]
+        return assemble(places, pieces, pair_source, op_index, slots, eigen, *earlier)
+
+    first = add(spread)
+    x3 = across(after(z3, x12, first, beside_mixed), 1)
+    spread = [([(6, 0)], z3), ([(6, 1)], beside(z3)), ([(3, 0), (5, 0)], x12)]
+    second = add(spread, first)
     spins = [crossed[1:, :, : NS - 1], crossed[1:, :, NS - 1 :]]
-    over = [beside(after(some, partial)) for some in spins]
+    over = [beside(after(some, second)) for some in spins]
     blocks = [[mixed[0]], [beside_mixed], [crossed], over]
-    last = beside(after(x3, partial))
-    places, late = [[(7, 0)], [(3, 1), (5, 1)]], [[x3], [beside(x12)]]
-    most = assemble(places, late, pair_source, op_index, slots, eigen, partial)
-    return contract([[(7, 1)]], [[last]], most, pair_source, op_index, slots, blocks)
+    last = beside(after(x3, second))
+    third = add([([(3, 1), (5, 1)], beside(x12))], second)
+    late, places = [[x3], [last]], [[(7, 0)], [(7, 1)]]
+    return contract(places, late, third, pair_source, op_index, slots, blocks)
 
 
 def solution(mesh):

time: 48.4 us -> 51.9 us (1.072)
  the two profiles are of different devices: /device:TPU:0 before, /device:TPU:13 now
where the time goes in v2:
time: 51.9 us; the launch traced here: 51.7 us
  waiting for transfers between devices  21.2 us (41%)
  Pallas kernels  15.8 us (30%)
  starting transfers between devices  12.1 us (23%)
  local copies, waits for them, and re-layouts  1.7 us (3%)
  between operations  0.84 us (2%)
    ppermute x16, waiting for transfers between devices, swap(): return lax.ppermute(array, axis, [(i, i ^ mask) for i in range(size)])  21.2 us
    ppermute x16, starting transfers between devices, swap(): return lax.ppermute(array, axis, [(i, i ^ mask) for i in range(size)])  12.1 us
    pallas_call x3, Pallas kernels, assemble(): pl.pallas_call(functools.partial(assemble_kernel, places, [len(group) for...  6.18 us
    pallas_call x1, Pallas kernels, mix(): pl.pallas_call(mix_kernel, in_specs=[pl.BlockSpec(memory_space=pltpu.SMEM...  5 us
    pallas_call x1, Pallas kernels, contract(): pl.pallas_call(functools.partial(near_kernel, places, near_masks, [len(g)...  2.44 us
    pallas_call x1, Pallas kernels, contract(): pl.pallas_call(functools.partial(far_kernel, near_masks, far_masks, [len(...  2.16 us
    slice x1, local copies, waits for them, and re-layouts, per_device(): own = jnp.concatenate([own[:, 0], own[:, 1]], axis=1)  1.61 us
  transfers between devices with their start and end apart: 16, of which 3 were waited for; matrix products, arithmetic and copies ran while one was open for 0% of the time, Pallas kernels for 26%

profile of v2, /device:TPU:13, one launch (start us, length us, event | category | flops | bytes accessed | tf_op | source)
XLA Modules:
  0.0 51.7 jit_solution(16968382621122345718)
XLA Ops:
  0.0 1.6 %constant_dynamic-slice_fusion = (bf16[128,1,512]{2,1,0:T(2,128)(2,1)S(1)}, bf16[128,1,512]{2,1,0:T(2,128)(2,1)S(1)}) fusion(bf16[256,2,512]{2,1,0:T(2,128)(2,1)} %param.9, s32[]{:T(128)S(6)} %select_n.11, s32[]{:T(128)S(6)} %add.9), kind=kLoop, calls=%fused_computation.4 | loop fusion | bytes 524296 | tf_op jit(solution)/shard_map/slice | solution.py:328
  1.7 0.0 copy-start.1
  1.7 1.3 %collective-permute-start.2 = (bf16[128,1024]{1,0:T(8,128)(2,1)S(1)}, bf16[128,1024]{1,0:T(8,128)(2,1)S(1)}, u32[]{:S(2)}, u32[]{:S(2)}) collective-permute-start(bf16[128,1024]{1,0:T(8,128)(2,1)S(1)} %pad_maximum_fusion.1.refs_0_), channel_id=1, source_target_pairs={{0,4},{4,0},{8,12},{12,8},{16,20},{20,16},{24,28},{28,24},{1,5},{5... | collective-permute-start | bytes 786440 | tf_op jit(solution)/shard_map/ppermute | solution.py:297
  3.0 2.3 %collective-permute-start.1 = (bf16[128,1024]{1,0:T(8,128)(2,1)S(1)}, bf16[128,1024]{1,0:T(8,128)(2,1)S(1)}, u32[]{:S(2)}, u32[]{:S(2)}) collective-permute-start(bf16[128,1024]{1,0:T(8,128)(2,1)S(1)} %pad_maximum_fusion.1.refs_0_), channel_id=1, source_target_pairs={{0,16},{4,20},{8,24},{12,28},{16,0},{20,4},{24,8},{28,12},{1,17},{... | collective-permute-start | bytes 786440 | tf_op jit(solution)/shard_map/ppermute | solution.py:297
  5.3 0.2 collective-permute-start
  5.5 5.0 %mix.1 = (bf16[1,2,4,64,512]{4,3,2,1,0:T(8,128)(2,1)S(1)}, bf16[1,2,4,64,512]{4,3,2,1,0:T(8,128)(2,1)S(1)}, bf16[2,2,4,64,512]{4,3,2,1,0:T(8,128)(2,1)S(1)}) custom-call(s32[2,2]{1,0:T(2,128)S(1)} %copy-done.2, s32[2,128]{1,0:T(2,128)S(1)} %copy-done.3, bf16[1,2,2,512,512]{4,3,2,1,0:T(8,128)(2,1)S(1)} %copy-done, bf16[1,2,2048,512]{3,2,1,0:T(8,128)(2,1)} %peramb_ref.1), custom_call_target="tpu_custom_call" | custom-call | flops 1000 | bytes 1000 | tf_op jit(solution)/shard_map/mix/pallas_call | solution.py:90
  10.5 0.3 collective-permute-start.13
  10.8 1.8 %collective-permute-start.5 = (bf16[128,1024]{1,0:T(8,128)(2,1)S(1)}, bf16[128,1024]{1,0:T(8,128)(2,1)S(1)}, u32[]{:S(2)}, u32[]{:S(2)}) collective-permute-start(bf16[128,1024]{1,0:T(8,128)(2,1)S(1)} %collective-permute-done.2.refs_2_), channel_id=1, source_target_pairs={{0,1},{1,0},{2,3},{3,2},{4,5},{5,4},{6,7},{7,6},{8,9},{9,8},{10,11... | collective-permute-start | bytes 786440 | tf_op jit(solution)/shard_map/ppermute | solution.py:297
  12.6 0.0 collective-permute-start.8
  12.6 4.3 %collective-permute-done.1 = bf16[128,1024]{1,0:T(8,128)(2,1)S(1)} collective-permute-done((bf16[128,1024]{1,0:T(8,128)(2,1)S(1)}, bf16[128,1024]{1,0:T(8,128)(2,1)S(1)}, u32[]{:S(2)}, u32[]{:S(2)}) %collective-permute-start.1) | collective-permute-done | bytes 262176 | tf_op jit(solution)/shard_map/ppermute | solution.py:297
  16.8 0.0 collective-permute-done
  16.9 1.6 %collective-permute-start.9 = (bf16[256,1024]{1,0:T(8,128)(2,1)S(1)}, bf16[256,1024]{1,0:T(8,128)(2,1)S(1)}, u32[]{:S(2)}, u32[]{:S(2)}) collective-permute-start(bf16[256,1024]{1,0:T(8,128)(2,1)S(1)} %pad_maximum_fusion.refs_4_), channel_id=1, source_target_pairs={{0,1},{1,0},{2,3},{3,2},{4,5},{5,4},{6,7},{7,6},{8,9},{9,8},{10,11... | collective-permute-start | bytes 1572872 | tf_op jit(solution)/shard_map/ppermute | solution.py:297
  18.5 0.1 collective-permute-start.10
  18.6 0.0 collective-permute-done.5.refs_3_
  18.6 0.3 collective-permute-start.3
  18.8 0.2 collective-permute-start.6
  19.0 12.7 %collective-permute-done.6.refs_0_ = bf16[128,1024]{1,0:T(8,128)(2,1)S(1)} collective-permute-done((bf16[128,1024]{1,0:T(8,128)(2,1)S(1)}, bf16[128,1024]{1,0:T(8,128)(2,1)S(1)}, u32[]{:S(2)}, u32[]{:S(2)}) %collective-permute-start.6) | collective-permute-done | bytes 262176 | tf_op jit(solution)/shard_map/ppermute | solution.py:297
  31.7 1.4 %collective-permute-start.7 = (bf16[128,1024]{1,0:T(8,128)(2,1)S(1)}, bf16[128,1024]{1,0:T(8,128)(2,1)S(1)}, u32[]{:S(2)}, u32[]{:S(2)}) collective-permute-start(bf16[128,1024]{1,0:T(8,128)(2,1)S(1)} %collective-permute-done.6.refs_0_), channel_id=1, source_target_pairs={{0,1},{1,0},{2,3},{3,2},{4,5},{5,4},{6,7},{7,6},{8,9},{9,8},{10,11... | collective-permute-start | bytes 786440 | tf_op jit(solution)/shard_map/ppermute | solution.py:297
  33.8 0.0 collective-permute-done.9.refs_5_
  33.9 3.0 %assemble.3.refs_3_ = bf16[2,1024,512]{2,1,0:T(8,128)(2,1)S(1)} custom-call(s32[1]{0:T(128)S(6)} %copy.14.source_ref, s32[2,2]{1,0:T(2,128)S(1)} %copy-done.2, s32[16,128]{1,0:T(8,128)S(1)} %bitcast.5, bf16[128,1024]{1,0:T(8,128)(2,1)S(1)} %pad_maximum_fusion.1.refs_0_, bf16[128,1024]{1,0:T(8,128)(2,1)S(1)} %collective-permute-done.8.refs_1_, ...), custom_call_target="tpu_custom_call" | custom-call | flops 1000 | bytes 1000 | tf_op jit(solution)/shard_map/assemble/pallas_call | solution.py:163
  36.8 0.0 collective-permute-done.10.refs_3_
  36.8 1.3 %collective-permute-start.11 = (bf16[128,1024]{1,0:T(8,128)(2,1)S(1)}, bf16[128,1024]{1,0:T(8,128)(2,1)S(1)}, u32[]{:S(2)}, u32[]{:S(2)}) collective-permute-start(bf16[128,1024]{1,0:T(8,128)(2,1)S(1)} %collective-permute-done.6.refs_0_), channel_id=1, source_target_pairs={{0,4},{4,0},{8,12},{12,8},{16,20},{20,16},{24,28},{28,24},{1,5},{5... | collective-permute-start | bytes 786440 | tf_op jit(solution)/shard_map/ppermute | solution.py:297
  38.1 0.3 collective-permute-start.4
  38.4 1.9 %assemble.4.refs_1_ = bf16[2,1024,512]{2,1,0:T(8,128)(2,1)S(1)} custom-call(s32[1]{0:T(128)S(6)} %copy.14.source_ref, s32[2,2]{1,0:T(2,128)S(1)} %copy-done.2, s32[16,128]{1,0:T(8,128)S(1)} %bitcast.6, bf16[128,1024]{1,0:T(8,128)(2,1)S(1)} %collective-permute-done.6.refs_0_, bf16[128,1024]{1,0:T(8,128)(2,1)S(1)} %collective-permute-done.7.refs_1_, ...), custom_call_target="tpu_custom_call" | custom-call | flops 1000 | bytes 1000 | tf_op jit(solution)/shard_map/assemble/pallas_call | solution.py:163
  40.4 0.3 collective-permute-start.14
  40.6 4.2 %collective-permute-done.11.refs_0_ = bf16[128,1024]{1,0:T(8,128)(2,1)S(1)} collective-permute-done((bf16[128,1024]{1,0:T(8,128)(2,1)S(1)}, bf16[128,1024]{1,0:T(8,128)(2,1)S(1)}, u32[]{:S(2)}, u32[]{:S(2)}) %collective-permute-start.11) | collective-permute-done | bytes 262176 | tf_op jit(solution)/shard_map/ppermute | solution.py:297
  44.8 0.8 %collective-permute-start.12 = (bf16[128,1024]{1,0:T(8,128)(2,1)S(1)}, bf16[128,1024]{1,0:T(8,128)(2,1)S(1)}, u32[]{:S(2)}, u32[]{:S(2)}) collective-permute-start(bf16[128,1024]{1,0:T(8,128)(2,1)S(1)} %collective-permute-done.11.refs_0_), channel_id=1, source_target_pairs={{0,1},{1,0},{2,3},{3,2},{4,5},{5,4},{6,7},{7,6},{8,9},{9,8},{10,11... | collective-permute-start | bytes 786440 | tf_op jit(solution)/shard_map/ppermute | solution.py:297
  45.6 0.1 collective-permute-start.15
  45.7 0.0 collective-permute-done.4.refs_0_
  45.7 1.3 %assemble.5.partial_ref = bf16[2,1024,512]{2,1,0:T(8,128)(2,1)S(1)} custom-call(s32[1]{0:T(128)S(6)} %copy.14.source_ref, s32[2,2]{1,0:T(2,128)S(1)} %copy-done.2, s32[16,128]{1,0:T(8,128)S(1)} %bitcast.7, bf16[256,1024]{1,0:T(8,128)(2,1)S(1)} %collective-permute-done.4.refs_0_, bf16[2,1024,512]{2,1,0:T(8,128)(2,1)S(1)} %assemble.4.refs_1_), custom_call_target="tpu_custom_call" | custom-call | flops 1000 | bytes 1000 | tf_op jit(solution)/shard_map/assemble/pallas_call | solution.py:163
  47.1 2.4 %near.1 = (bf16[2,1024,512]{2,1,0:T(8,128)(2,1)S(1)}, bf16[2,2,4,32,2,512]{5,4,3,2,1,0:T(2,128)(2,1)S(1)}) custom-call(s32[1]{0:T(128)S(6)} %copy.14.source_ref, s32[2,2]{1,0:T(2,128)S(1)} %copy-done.2, s32[16,128]{1,0:T(8,128)S(1)} %bitcast.8, bf16[2,1024,512]{2,1,0:T(8,128)(2,1)S(1)} %assemble.5.partial_ref, ...), custom_call_target="tpu_custom_call" | custom-call | flops 1000000000 | bytes 1000 | tf_op jit(solution)/shard_map/near/pallas_call | solution.py:267
  49.5 2.2 %far.1 = bf16[2,4,32,2,2048]{4,3,2,1,0:T(2,128)(2,1)} custom-call(bf16[2,1024,512]{2,1,0:T(8,128)(2,1)S(1)} %get-tuple-element.26.right, bf16[2,2,4,32,2,512]{5,4,3,2,1,0:T(2,128)(2,1)S(1)} %get-tuple-element.27.near_ref, bf16[2,2,4,64,512]{4,3,2,1,0:T(8,128)(2,1)S(1)} %collective-permute-done.13.refs_0_, ...), custom_call_target="tpu_custom_call" | custom-call | flops 1000000000 | bytes 1000 | tf_op jit(solution)/shard_map/far/pallas_call | solution.py:280
  (20 shorter events, 0.2 us)
Async XLA Ops:
  0.0 5.5 %copy-start.2 = (s32[2,2]{1,0:T(2,128)S(1)}, s32[2,2]{1,0:T(2,128)}, u32[]{:S(2)}) copy-start(s32[2,2]{1,0:T(2,128)} %op_ref.9) | copy-start | bytes 52
  0.0 5.5 %copy-start.3 = (s32[2,128]{1,0:T(2,128)S(1)}, s32[2,128]{1,0:T(2,128)}, u32[]{:S(2)}) copy-start(s32[2,128]{1,0:T(2,128)} %listed_ref.1) | copy-start | bytes 3076
  0.0 5.5 %copy-start = (bf16[1,2,2,512,512]{4,3,2,1,0:T(8,128)(2,1)S(1)}, bf16[1,2,2,512,512]{4,3,2,1,0:T(8,128)(2,1)}, u32[]{:S(2)}) copy-start(bf16[1,2,2,512,512]{4,3,2,1,0:T(8,128)(2,1)} %sink_ref.1) | copy-start | bytes 6291460
  1.7 32.1 %copy-start.1 = (s32[2048]{0:T(1024)S(1)}, s32[2048]{0:T(1024)}, u32[]{:S(2)}) copy-start(s32[2048]{0:T(1024)} %param.10) | copy-start | bytes 24580
  1.7 9.1 %collective-permute-start.2 = (bf16[128,1024]{1,0:T(8,128)(2,1)S(1)}, bf16[128,1024]{1,0:T(8,128)(2,1)S(1)}, u32[]{:S(2)}, u32[]{:S(2)}) collective-permute-start(bf16[128,1024]{1,0:T(8,128)(2,1)S(1)} %pad_maximum_fusion.1.refs_0_), channel_id=1, source_target_pairs={{0,4},{4,0},{8,12},{12,8},{16,20},{20,16},{24,28},{28,24},{1,5},{5... | collective-permute-start | bytes 786440 | tf_op jit(solution)/shard_map/ppermute | solution.py:297
  3.0 13.8 %collective-permute-start.1 = (bf16[128,1024]{1,0:T(8,128)(2,1)S(1)}, bf16[128,1024]{1,0:T(8,128)(2,1)S(1)}, u32[]{:S(2)}, u32[]{:S(2)}) collective-permute-start(bf16[128,1024]{1,0:T(8,128)(2,1)S(1)} %pad_maximum_fusion.1.refs_0_), channel_id=1, source_target_pairs={{0,16},{4,20},{8,24},{12,28},{16,0},{20,4},{24,8},{28,12},{1,17},{... | collective-permute-start | bytes 786440 | tf_op jit(solution)/shard_map/ppermute | solution.py:297
  5.3 11.5 %collective-permute-start = (bf16[128,1024]{1,0:T(8,128)(2,1)S(1)}, bf16[128,1024]{1,0:T(8,128)(2,1)S(1)}, u32[]{:S(2)}, u32[]{:S(2)}) collective-permute-start(bf16[128,1024]{1,0:T(8,128)(2,1)S(1)} %pad_maximum_fusion.1.refs_0_), channel_id=1, source_target_pairs={{0,8},{4,12},{8,0},{12,4},{16,24},{20,28},{24,16},{28,20},{1,9},{5... | collective-permute-start | bytes 786440 | tf_op jit(solution)/shard_map/ppermute | solution.py:297
  10.5 29.8 %collective-permute-start.13 = (bf16[2,2,4,64,512]{4,3,2,1,0:T(8,128)(2,1)S(1)}, bf16[2,2,4,64,512]{4,3,2,1,0:T(8,128)(2,1)S(1)}, u32[]{:S(2)}, u32[]{:S(2)}) collective-permute-start(bf16[2,2,4,64,512]{4,3,2,1,0:T(8,128)(2,1)S(1)} %get-tuple-element.28), channel_id=1, source_target_pairs={{0,2},{1,3},{2,0},{3,1},{4,6},{5,7},{6,4},{7,5},{8,10},{9,11},{10,... | collective-permute-start | bytes 3145736 | tf_op jit(solution)/shard_map/ppermute | solution.py:297
  10.8 7.8 %collective-permute-start.5 = (bf16[128,1024]{1,0:T(8,128)(2,1)S(1)}, bf16[128,1024]{1,0:T(8,128)(2,1)S(1)}, u32[]{:S(2)}, u32[]{:S(2)}) collective-permute-start(bf16[128,1024]{1,0:T(8,128)(2,1)S(1)} %collective-permute-done.2.refs_2_), channel_id=1, source_target_pairs={{0,1},{1,0},{2,3},{3,2},{4,5},{5,4},{6,7},{7,6},{8,9},{9,8},{10,11... | collective-permute-start | bytes 786440 | tf_op jit(solution)/shard_map/ppermute | solution.py:297
  12.6 6.3 %collective-permute-start.8 = (bf16[128,1024]{1,0:T(8,128)(2,1)S(1)}, bf16[128,1024]{1,0:T(8,128)(2,1)S(1)}, u32[]{:S(2)}, u32[]{:S(2)}) collective-permute-start(bf16[128,1024]{1,0:T(8,128)(2,1)S(1)} %pad_maximum_fusion.1.refs_0_), channel_id=1, source_target_pairs={{0,1},{1,0},{2,3},{3,2},{4,5},{5,4},{6,7},{7,6},{8,9},{9,8},{10,11... | collective-permute-start | bytes 786440 | tf_op jit(solution)/shard_map/ppermute | solution.py:297
  16.9 17.0 %collective-permute-start.9 = (bf16[256,1024]{1,0:T(8,128)(2,1)S(1)}, bf16[256,1024]{1,0:T(8,128)(2,1)S(1)}, u32[]{:S(2)}, u32[]{:S(2)}) collective-permute-start(bf16[256,1024]{1,0:T(8,128)(2,1)S(1)} %pad_maximum_fusion.refs_4_), channel_id=1, source_target_pairs={{0,1},{1,0},{2,3},{3,2},{4,5},{5,4},{6,7},{7,6},{8,9},{9,8},{10,11... | collective-permute-start | bytes 1572872 | tf_op jit(solution)/shard_map/ppermute | solution.py:297
  18.5 18.3 %collective-permute-start.10 = (bf16[1,2,4,64,512]{4,3,2,1,0:T(8,128)(2,1)S(1)}, bf16[1,2,4,64,512]{4,3,2,1,0:T(8,128)(2,1)S(1)}, u32[]{:S(2)}, u32[]{:S(2)}) collective-permute-start(bf16[1,2,4,64,512]{4,3,2,1,0:T(8,128)(2,1)S(1)} %get-tuple-element.23), channel_id=1, source_target_pairs={{0,1},{1,0},{2,3},{3,2},{4,5},{5,4},{6,7},{7,6},{8,9},{9,8},{10,11... | collective-permute-start | bytes 1572872 | tf_op jit(solution)/shard_map/ppermute | solution.py:297
  18.6 18.2 %collective-permute-start.3 = (bf16[256,1024]{1,0:T(8,128)(2,1)S(1)}, bf16[256,1024]{1,0:T(8,128)(2,1)S(1)}, u32[]{:S(2)}, u32[]{:S(2)}) collective-permute-start(bf16[256,1024]{1,0:T(8,128)(2,1)S(1)} %pad_maximum_fusion.refs_4_), channel_id=1, source_target_pairs={{0,4},{4,0},{8,12},{12,8},{16,20},{20,16},{24,28},{28,24},{1,5},{5... | collective-permute-start | bytes 1572872 | tf_op jit(solution)/shard_map/ppermute | solution.py:297
  18.8 12.9 %collective-permute-start.6 = (bf16[128,1024]{1,0:T(8,128)(2,1)S(1)}, bf16[128,1024]{1,0:T(8,128)(2,1)S(1)}, u32[]{:S(2)}, u32[]{:S(2)}) collective-permute-start(bf16[128,1024]{1,0:T(8,128)(2,1)S(1)} %pad_maximum_fusion.1.refs_0_), channel_id=1, source_target_pairs={{0,24},{4,28},{8,16},{12,20},{16,8},{20,12},{24,0},{28,4},{1,25},{... | collective-permute-start | bytes 786440 | tf_op jit(solution)/shard_map/ppermute | solution.py:297
  31.7 6.7 %collective-permute-start.7 = (bf16[128,1024]{1,0:T(8,128)(2,1)S(1)}, bf16[128,1024]{1,0:T(8,128)(2,1)S(1)}, u32[]{:S(2)}, u32[]{:S(2)}) collective-permute-start(bf16[128,1024]{1,0:T(8,128)(2,1)S(1)} %collective-permute-done.6.refs_0_), channel_id=1, source_target_pairs={{0,1},{1,0},{2,3},{3,2},{4,5},{5,4},{6,7},{7,6},{8,9},{9,8},{10,11... | collective-permute-start | bytes 786440 | tf_op jit(solution)/shard_map/ppermute | solution.py:297
  36.8 8.0 %collective-permute-start.11 = (bf16[128,1024]{1,0:T(8,128)(2,1)S(1)}, bf16[128,1024]{1,0:T(8,128)(2,1)S(1)}, u32[]{:S(2)}, u32[]{:S(2)}) collective-permute-start(bf16[128,1024]{1,0:T(8,128)(2,1)S(1)} %collective-permute-done.6.refs_0_), channel_id=1, source_target_pairs={{0,4},{4,0},{8,12},{12,8},{16,20},{20,16},{24,28},{28,24},{1,5},{5... | collective-permute-start | bytes 786440 | tf_op jit(solution)/shard_map/ppermute | solution.py:297
  38.1 7.6 %collective-permute-start.4 = (bf16[256,1024]{1,0:T(8,128)(2,1)S(1)}, bf16[256,1024]{1,0:T(8,128)(2,1)S(1)}, u32[]{:S(2)}, u32[]{:S(2)}) collective-permute-start(bf16[256,1024]{1,0:T(8,128)(2,1)S(1)} %collective-permute-done.3.refs_2_), channel_id=1, source_target_pairs={{0,1},{1,0},{2,3},{3,2},{4,5},{5,4},{6,7},{7,6},{8,9},{9,8},{10,11... | collective-permute-start | bytes 1572872 | tf_op jit(solution)/shard_map/ppermute | solution.py:297
  40.4 9.2 %collective-permute-start.14 = (bf16[1,2,3,64,512]{4,3,2,1,0:T(8,128)(2,1)S(1)}, bf16[1,2,3,64,512]{4,3,2,1,0:T(8,128)(2,1)S(1)}, u32[]{:S(2)}, u32[]{:S(2)}) collective-permute-start(bf16[1,2,3,64,512]{4,3,2,1,0:T(8,128)(2,1)S(1)} %slice.16), channel_id=1, source_target_pairs={{0,1},{1,0},{2,3},{3,2},{4,5},{5,4},{6,7},{7,6},{8,9},{9,8},{10,11... | collective-permute-start | bytes 1179656 | tf_op jit(solution)/shard_map/ppermute | solution.py:297
  44.8 2.2 %collective-permute-start.12 = (bf16[128,1024]{1,0:T(8,128)(2,1)S(1)}, bf16[128,1024]{1,0:T(8,128)(2,1)S(1)}, u32[]{:S(2)}, u32[]{:S(2)}) collective-permute-start(bf16[128,1024]{1,0:T(8,128)(2,1)S(1)} %collective-permute-done.11.refs_0_), channel_id=1, source_target_pairs={{0,1},{1,0},{2,3},{3,2},{4,5},{5,4},{6,7},{7,6},{8,9},{9,8},{10,11... | collective-permute-start | bytes 786440 | tf_op jit(solution)/shard_map/ppermute | solution.py:297
  45.6 3.9 %collective-permute-start.15 = (bf16[1,2,1,64,512]{4,3,2,1,0:T(8,128)(2,1)S(1)}, bf16[1,2,1,64,512]{4,3,2,1,0:T(8,128)(2,1)S(1)}, u32[]{:S(2)}, u32[]{:S(2)}) collective-permute-start(bf16[1,2,1,64,512]{4,3,2,1,0:T(8,128)(2,1)S(1)} %slice.17), channel_id=1, source_target_pairs={{0,1},{1,0},{2,3},{3,2},{4,5},{5,4},{6,7},{7,6},{8,9},{9,8},{10,11... | collective-permute-start | bytes 393224 | tf_op jit(solution)/shard_map/ppermute | solution.py:297

commit v3 on v0

--- a/solution.py
+++ b/solution.py
@@ -173,12 +173,10 @@
     per_time = eigen // local_cols
     direct = [block_rows(parts, k) for parts in blocks]
     rows = direct[0].shape[0]
-    odd = iota((rows, local_cols), 0) % 2 == 1
-    turned = []
-    for x in direct:
-        wide = x.astype(F32)
-        y = jnp.where(odd, pltpu.roll(wide, 1, 0), -pltpu.roll(wide, rows - 1, 0))
-        turned.append(y.astype(BF16))
+    row, other = iota((rows, rows), 0), iota((rows, rows), 1)
+    signs = jnp.where(row % 2 == 1, 1.0, -1.0)
+    turn = jnp.where(other == row + 1 - 2 * (row % 2), signs, 0.0).astype(BF16)
+    turned = [dot(turn, x).astype(BF16) for x in direct]
     if per_time == 1:
         lhs = jnp.concatenate(
             [jnp.concatenate(direct, axis=0), jnp.concatenate(turned, axis=0)], axis=1

time: 47.1 us -> 47.5 us (level)
  no operation moved by 1% of the time
where the time goes in v3:
time: 47.5 us; the launch traced here: 46.7 us
  starting transfers between devices  15.6 us (33%)
  Pallas kernels  14.6 us (31%)
  waiting for transfers between devices  14 us (29%)
  local copies, waits for them, and re-layouts  1.69 us (4%)
  between operations  0.78 us (2%)
    ppermute x16, starting transfers between devices, swap(): return lax.ppermute(array, axis, [(i, i ^ mask) for i in range(size)])  15.6 us
    ppermute x16, waiting for transfers between devices, swap(): return lax.ppermute(array, axis, [(i, i ^ mask) for i in range(size)])  14 us
    pallas_call x1, Pallas kernels, mix(): pl.pallas_call(mix_kernel, in_specs=[pl.BlockSpec(memory_space=pltpu.SMEM...  4.99 us
    pallas_call x1, Pallas kernels, assemble(): pl.pallas_call(functools.partial(assemble_kernel, places, [len(group) for...  4.01 us
    pallas_call x1, Pallas kernels, contract(): pl.pallas_call(functools.partial(near_kernel, places, near_masks, [len(g)...  3.25 us
    pallas_call x1, Pallas kernels, contract(): pl.pallas_call(functools.partial(far_kernel, near_masks, far_masks, [len(...  2.33 us
    slice x1, local copies, waits for them, and re-layouts, per_device(): own = jnp.concatenate([own[:, 0], own[:, 1]], axis=1)  1.6 us
  transfers between devices with their start and end apart: 16, of which 6 were waited for; matrix products, arithmetic and copies ran while one was open for 0% of the time, Pallas kernels for 26%

profile of v3, /device:TPU:0, one launch (start us, length us, event | category | flops | bytes accessed | tf_op | source)
XLA Modules:
  0.0 46.7 jit_solution(15777041425577530669)
XLA Ops:
  0.0 1.6 %constant_dynamic-slice_fusion = (bf16[128,1,512]{2,1,0:T(2,128)(2,1)S(1)}, bf16[128,1,512]{2,1,0:T(2,128)(2,1)S(1)}) fusion(bf16[256,2,512]{2,1,0:T(2,128)(2,1)} %param.9, s32[]{:T(128)S(6)} %select_n.11, s32[]{:T(128)S(6)} %add.9), kind=kLoop, calls=%fused_computation.4 | loop fusion | bytes 524296 | tf_op jit(solution)/shard_map/slice | solution.py:320
  1.7 0.0 copy-start.1
  1.7 4.1 %collective-permute-start.4 = (bf16[128,1024]{1,0:T(8,128)(2,1)S(1)}, bf16[128,1024]{1,0:T(8,128)(2,1)S(1)}, u32[]{:S(2)}, u32[]{:S(2)}) collective-permute-start(bf16[128,1024]{1,0:T(8,128)(2,1)S(1)} %pad_maximum_fusion.1.refs_0_), channel_id=1, source_target_pairs={{0,16},{4,20},{8,24},{12,28},{16,0},{20,4},{24,8},{28,12},{1,17},{... | collective-permute-start | bytes 786440 | tf_op jit(solution)/shard_map/ppermute | solution.py:289
  5.8 1.5 %collective-permute-start.1 = (bf16[128,1024]{1,0:T(8,128)(2,1)S(1)}, bf16[128,1024]{1,0:T(8,128)(2,1)S(1)}, u32[]{:S(2)}, u32[]{:S(2)}) collective-permute-start(bf16[128,1024]{1,0:T(8,128)(2,1)S(1)} %pad_maximum_fusion.1.refs_0_), channel_id=1, source_target_pairs={{0,4},{4,0},{8,12},{12,8},{16,20},{20,16},{24,28},{28,24},{1,5},{5... | collective-permute-start | bytes 786440 | tf_op jit(solution)/shard_map/ppermute | solution.py:289
  7.3 1.6 %collective-permute-start.3 = (bf16[128,1024]{1,0:T(8,128)(2,1)S(1)}, bf16[128,1024]{1,0:T(8,128)(2,1)S(1)}, u32[]{:S(2)}, u32[]{:S(2)}) collective-permute-start(bf16[128,1024]{1,0:T(8,128)(2,1)S(1)} %pad_maximum_fusion.1.refs_0_), channel_id=1, source_target_pairs={{0,8},{4,12},{8,0},{12,4},{16,24},{20,28},{24,16},{28,20},{1,9},{5... | collective-permute-start | bytes 786440 | tf_op jit(solution)/shard_map/ppermute | solution.py:289
  8.9 5.0 %mix.1 = (bf16[1,2,4,64,512]{4,3,2,1,0:T(8,128)(2,1)S(1)}, bf16[1,2,4,64,512]{4,3,2,1,0:T(8,128)(2,1)S(1)}, bf16[2,2,4,64,512]{4,3,2,1,0:T(8,128)(2,1)S(1)}) custom-call(s32[2,2]{1,0:T(2,128)S(1)} %copy-done.2, s32[2,128]{1,0:T(2,128)S(1)} %copy-done.3, bf16[1,2,2,512,512]{4,3,2,1,0:T(8,128)(2,1)S(1)} %copy-done, bf16[1,2,2048,512]{3,2,1,0:T(8,128)(2,1)} %peramb_ref.1), custom_call_target="tpu_custom_call" | custom-call | flops 1000 | bytes 1000 | tf_op jit(solution)/shard_map/mix/pallas_call | solution.py:88
  13.9 1.6 %collective-permute-start.13 = (bf16[2,2,4,64,512]{4,3,2,1,0:T(8,128)(2,1)S(1)}, bf16[2,2,4,64,512]{4,3,2,1,0:T(8,128)(2,1)S(1)}, u32[]{:S(2)}, u32[]{:S(2)}) collective-permute-start(bf16[2,2,4,64,512]{4,3,2,1,0:T(8,128)(2,1)S(1)} %get-tuple-element.28), channel_id=1, source_target_pairs={{0,2},{1,3},{2,0},{3,1},{4,6},{5,7},{6,4},{7,5},{8,10},{9,11},{10,... | collective-permute-start | bytes 3145736 | tf_op jit(solution)/shard_map/ppermute | solution.py:289
  15.5 0.0 collective-permute-start.9
  15.5 2.4 %collective-permute-done.4 = bf16[128,1024]{1,0:T(8,128)(2,1)S(1)} collective-permute-done((bf16[128,1024]{1,0:T(8,128)(2,1)S(1)}, bf16[128,1024]{1,0:T(8,128)(2,1)S(1)}, u32[]{:S(2)}, u32[]{:S(2)}) %collective-permute-start.4) | collective-permute-done | bytes 262176 | tf_op jit(solution)/shard_map/ppermute | solution.py:289
  17.9 0.0 collective-permute-done.1.refs_2_
  17.9 0.0 collective-permute-start.2
  17.9 1.4 %collective-permute-done.3 = bf16[128,1024]{1,0:T(8,128)(2,1)S(1)} collective-permute-done((bf16[128,1024]{1,0:T(8,128)(2,1)S(1)}, bf16[128,1024]{1,0:T(8,128)(2,1)S(1)}, u32[]{:S(2)}, u32[]{:S(2)}) %collective-permute-start.3) | collective-permute-done | bytes 262176 | tf_op jit(solution)/shard_map/ppermute | solution.py:289
  19.3 0.6 %collective-permute-start.8 = (bf16[256,1024]{1,0:T(8,128)(2,1)S(1)}, bf16[256,1024]{1,0:T(8,128)(2,1)S(1)}, u32[]{:S(2)}, u32[]{:S(2)}) collective-permute-start(bf16[256,1024]{1,0:T(8,128)(2,1)S(1)} %pad_maximum_fusion.refs_4_), channel_id=1, source_target_pairs={{0,4},{4,0},{8,12},{12,8},{16,20},{20,16},{24,28},{28,24},{1,5},{5... | collective-permute-start | bytes 1572872 | tf_op jit(solution)/shard_map/ppermute | solution.py:289
  19.9 3.0 %collective-permute-start.6 = (bf16[128,1024]{1,0:T(8,128)(2,1)S(1)}, bf16[128,1024]{1,0:T(8,128)(2,1)S(1)}, u32[]{:S(2)}, u32[]{:S(2)}) collective-permute-start(bf16[128,1024]{1,0:T(8,128)(2,1)S(1)} %pad_maximum_fusion.1.refs_0_), channel_id=1, source_target_pairs={{0,24},{4,28},{8,16},{12,20},{16,8},{20,12},{24,0},{28,4},{1,25},{... | collective-permute-start | bytes 786440 | tf_op jit(solution)/shard_map/ppermute | solution.py:289
  22.9 0.0 collective-permute-done.2.refs_3_
  22.9 6.9 %collective-permute-done.6.refs_6_ = bf16[128,1024]{1,0:T(8,128)(2,1)S(1)} collective-permute-done((bf16[128,1024]{1,0:T(8,128)(2,1)S(1)}, bf16[128,1024]{1,0:T(8,128)(2,1)S(1)}, u32[]{:S(2)}, u32[]{:S(2)}) %collective-permute-start.6) | collective-permute-done | bytes 262176 | tf_op jit(solution)/shard_map/ppermute | solution.py:289
  29.9 0.0 collective-permute-done.9.refs_4_
  29.9 0.5 %collective-permute-start.7 = (bf16[128,1024]{1,0:T(8,128)(2,1)S(1)}, bf16[128,1024]{1,0:T(8,128)(2,1)S(1)}, u32[]{:S(2)}, u32[]{:S(2)}) collective-permute-start(bf16[128,1024]{1,0:T(8,128)(2,1)S(1)} %collective-permute-done.6.refs_6_), channel_id=1, source_target_pairs={{0,1},{1,0},{2,3},{3,2},{4,5},{5,4},{6,7},{7,6},{8,9},{9,8},{10,11... | collective-permute-start | bytes 786440 | tf_op jit(solution)/shard_map/ppermute | solution.py:289
  30.4 1.9 %collective-permute-done.8.refs_8_ = bf16[256,1024]{1,0:T(8,128)(2,1)S(1)} collective-permute-done((bf16[256,1024]{1,0:T(8,128)(2,1)S(1)}, bf16[256,1024]{1,0:T(8,128)(2,1)S(1)}, u32[]{:S(2)}, u32[]{:S(2)}) %collective-permute-start.8) | collective-permute-done | bytes 524320 | tf_op jit(solution)/shard_map/ppermute | solution.py:289
  32.3 1.5 %collective-permute-start.10 = (bf16[128,1024]{1,0:T(8,128)(2,1)S(1)}, bf16[128,1024]{1,0:T(8,128)(2,1)S(1)}, u32[]{:S(2)}, u32[]{:S(2)}) collective-permute-start(bf16[128,1024]{1,0:T(8,128)(2,1)S(1)} %collective-permute-done.6.refs_6_), channel_id=1, source_target_pairs={{0,4},{4,0},{8,12},{12,8},{16,20},{20,16},{24,28},{28,24},{1,5},{5... | collective-permute-start | bytes 786440 | tf_op jit(solution)/shard_map/ppermute | solution.py:289
  33.8 0.0 collective-permute-done.refs_1_
  33.9 0.0 collective-permute-start.12
  34.5 0.0 collective-permute-done.5.refs_5_
  34.5 4.0 %assemble.1.partial_ref = bf16[2,1024,512]{2,1,0:T(8,128)(2,1)S(1)} custom-call(s32[1]{0:T(128)S(6)} %copy.14.source_ref, s32[2,2]{1,0:T(2,128)S(1)} %copy-done.2, s32[16,128]{1,0:T(8,128)S(1)} %bitcast.5, bf16[128,1024]{1,0:T(8,128)(2,1)S(1)} %pad_maximum_fusion.1.refs_0_, bf16[128,1024]{1,0:T(8,128)(2,1)S(1)} %collective-permute-done.refs_1_, ...), custom_call_target="tpu_custom_call" | custom-call | flops 1000 | bytes 1000 | tf_op jit(solution)/shard_map/assemble/pallas_call | solution.py:153
  38.6 0.6 %collective-permute-start.14 = (bf16[1,2,3,64,512]{4,3,2,1,0:T(8,128)(2,1)S(1)}, bf16[1,2,3,64,512]{4,3,2,1,0:T(8,128)(2,1)S(1)}, u32[]{:S(2)}, u32[]{:S(2)}) collective-permute-start(bf16[1,2,3,64,512]{4,3,2,1,0:T(8,128)(2,1)S(1)} %slice.16), channel_id=1, source_target_pairs={{0,1},{1,0},{2,3},{3,2},{4,5},{5,4},{6,7},{7,6},{8,9},{9,8},{10,11... | collective-permute-start | bytes 1179656 | tf_op jit(solution)/shard_map/ppermute | solution.py:289
  39.2 0.4 collective-permute-done.10.refs_0_
  39.5 0.0 collective-permute-start.11
  39.6 0.6 %collective-permute-start.15 = (bf16[1,2,1,64,512]{4,3,2,1,0:T(8,128)(2,1)S(1)}, bf16[1,2,1,64,512]{4,3,2,1,0:T(8,128)(2,1)S(1)}, u32[]{:S(2)}, u32[]{:S(2)}) collective-permute-start(bf16[1,2,1,64,512]{4,3,2,1,0:T(8,128)(2,1)S(1)} %slice.17), channel_id=1, source_target_pairs={{0,1},{1,0},{2,3},{3,2},{4,5},{5,4},{6,7},{7,6},{8,9},{9,8},{10,11... | collective-permute-start | bytes 393224 | tf_op jit(solution)/shard_map/ppermute | solution.py:289
  40.1 0.9 %collective-permute-done.11.refs_1_ = bf16[128,1024]{1,0:T(8,128)(2,1)S(1)} collective-permute-done((bf16[128,1024]{1,0:T(8,128)(2,1)S(1)}, bf16[128,1024]{1,0:T(8,128)(2,1)S(1)}, u32[]{:S(2)}, u32[]{:S(2)}) %collective-permute-start.11) | collective-permute-done | bytes 262176 | tf_op jit(solution)/shard_map/ppermute | solution.py:289
  41.1 3.2 %near.1 = (bf16[2,1024,512]{2,1,0:T(8,128)(2,1)S(1)}, bf16[2,2,4,32,2,512]{5,4,3,2,1,0:T(2,128)(2,1)S(1)}) custom-call(s32[1]{0:T(128)S(6)} %copy.14.source_ref, s32[2,2]{1,0:T(2,128)S(1)} %copy-done.2, s32[16,128]{1,0:T(8,128)S(1)} %bitcast.6, bf16[2,1024,512]{2,1,0:T(8,128)(2,1)S(1)} %assemble.1.partial_ref, ...), custom_call_target="tpu_custom_call" | custom-call | flops 1000000000 | bytes 1000 | tf_op jit(solution)/shard_map/near/pallas_call | solution.py:259
  44.3 0.0 collective-permute-done.14.refs_1_
  44.4 2.3 %far.1 = bf16[2,4,32,2,2048]{4,3,2,1,0:T(2,128)(2,1)} custom-call(bf16[2,1024,512]{2,1,0:T(8,128)(2,1)S(1)} %get-tuple-element.26.right, bf16[2,2,4,32,2,512]{5,4,3,2,1,0:T(2,128)(2,1)S(1)} %get-tuple-element.27.near_ref, bf16[2,2,4,64,512]{4,3,2,1,0:T(8,128)(2,1)S(1)} %collective-permute-done.13.refs_0_, ...), custom_call_target="tpu_custom_call" | custom-call | flops 1000000000 | bytes 1000 | tf_op jit(solution)/shard_map/far/pallas_call | solution.py:272
  (18 shorter events, 0.2 us)
Async XLA Ops:
  0.0 8.9 %copy-start.2 = (s32[2,2]{1,0:T(2,128)S(1)}, s32[2,2]{1,0:T(2,128)}, u32[]{:S(2)}) copy-start(s32[2,2]{1,0:T(2,128)} %op_ref.5) | copy-start | bytes 52
  0.0 8.9 %copy-start.3 = (s32[2,128]{1,0:T(2,128)S(1)}, s32[2,128]{1,0:T(2,128)}, u32[]{:S(2)}) copy-start(s32[2,128]{1,0:T(2,128)} %listed_ref.1) | copy-start | bytes 3076
  0.0 8.9 %copy-start = (bf16[1,2,2,512,512]{4,3,2,1,0:T(8,128)(2,1)S(1)}, bf16[1,2,2,512,512]{4,3,2,1,0:T(8,128)(2,1)}, u32[]{:S(2)}) copy-start(bf16[1,2,2,512,512]{4,3,2,1,0:T(8,128)(2,1)} %sink_ref.1) | copy-start | bytes 6291460
  1.7 32.8 %copy-start.1 = (s32[2048]{0:T(1024)S(1)}, s32[2048]{0:T(1024)}, u32[]{:S(2)}) copy-start(s32[2048]{0:T(1024)} %param.10) | copy-start | bytes 24580
  1.7 16.2 %collective-permute-start.4 = (bf16[128,1024]{1,0:T(8,128)(2,1)S(1)}, bf16[128,1024]{1,0:T(8,128)(2,1)S(1)}, u32[]{:S(2)}, u32[]{:S(2)}) collective-permute-start(bf16[128,1024]{1,0:T(8,128)(2,1)S(1)} %pad_maximum_fusion.1.refs_0_), channel_id=1, source_target_pairs={{0,16},{4,20},{8,24},{12,28},{16,0},{20,4},{24,8},{28,12},{1,17},{... | collective-permute-start | bytes 786440 | tf_op jit(solution)/shard_map/ppermute | solution.py:289
  5.8 12.0 %collective-permute-start.1 = (bf16[128,1024]{1,0:T(8,128)(2,1)S(1)}, bf16[128,1024]{1,0:T(8,128)(2,1)S(1)}, u32[]{:S(2)}, u32[]{:S(2)}) collective-permute-start(bf16[128,1024]{1,0:T(8,128)(2,1)S(1)} %pad_maximum_fusion.1.refs_0_), channel_id=1, source_target_pairs={{0,4},{4,0},{8,12},{12,8},{16,20},{20,16},{24,28},{28,24},{1,5},{5... | collective-permute-start | bytes 786440 | tf_op jit(solution)/shard_map/ppermute | solution.py:289
  7.3 11.9 %collective-permute-start.3 = (bf16[128,1024]{1,0:T(8,128)(2,1)S(1)}, bf16[128,1024]{1,0:T(8,128)(2,1)S(1)}, u32[]{:S(2)}, u32[]{:S(2)}) collective-permute-start(bf16[128,1024]{1,0:T(8,128)(2,1)S(1)} %pad_maximum_fusion.1.refs_0_), channel_id=1, source_target_pairs={{0,8},{4,12},{8,0},{12,4},{16,24},{20,28},{24,16},{28,20},{1,9},{5... | collective-permute-start | bytes 786440 | tf_op jit(solution)/shard_map/ppermute | solution.py:289
  13.9 24.7 %collective-permute-start.13 = (bf16[2,2,4,64,512]{4,3,2,1,0:T(8,128)(2,1)S(1)}, bf16[2,2,4,64,512]{4,3,2,1,0:T(8,128)(2,1)S(1)}, u32[]{:S(2)}, u32[]{:S(2)}) collective-permute-start(bf16[2,2,4,64,512]{4,3,2,1,0:T(8,128)(2,1)S(1)} %get-tuple-element.28), channel_id=1, source_target_pairs={{0,2},{1,3},{2,0},{3,1},{4,6},{5,7},{6,4},{7,5},{8,10},{9,11},{10,... | collective-permute-start | bytes 3145736 | tf_op jit(solution)/shard_map/ppermute | solution.py:289
  15.5 14.4 %collective-permute-start.9 = (bf16[1,2,4,64,512]{4,3,2,1,0:T(8,128)(2,1)S(1)}, bf16[1,2,4,64,512]{4,3,2,1,0:T(8,128)(2,1)S(1)}, u32[]{:S(2)}, u32[]{:S(2)}) collective-permute-start(bf16[1,2,4,64,512]{4,3,2,1,0:T(8,128)(2,1)S(1)} %get-tuple-element.23), channel_id=1, source_target_pairs={{0,1},{1,0},{2,3},{3,2},{4,5},{5,4},{6,7},{7,6},{8,9},{9,8},{10,11... | collective-permute-start | bytes 1572872 | tf_op jit(solution)/shard_map/ppermute | solution.py:289
  17.9 5.1 %collective-permute-start.2 = (bf16[128,1024]{1,0:T(8,128)(2,1)S(1)}, bf16[128,1024]{1,0:T(8,128)(2,1)S(1)}, u32[]{:S(2)}, u32[]{:S(2)}) collective-permute-start(bf16[128,1024]{1,0:T(8,128)(2,1)S(1)} %collective-permute-done.1.refs_2_), channel_id=1, source_target_pairs={{0,1},{1,0},{2,3},{3,2},{4,5},{5,4},{6,7},{7,6},{8,9},{9,8},{10,11... | collective-permute-start | bytes 786440 | tf_op jit(solution)/shard_map/ppermute | solution.py:289
  19.3 13.0 %collective-permute-start.8 = (bf16[256,1024]{1,0:T(8,128)(2,1)S(1)}, bf16[256,1024]{1,0:T(8,128)(2,1)S(1)}, u32[]{:S(2)}, u32[]{:S(2)}) collective-permute-start(bf16[256,1024]{1,0:T(8,128)(2,1)S(1)} %pad_maximum_fusion.refs_4_), channel_id=1, source_target_pairs={{0,4},{4,0},{8,12},{12,8},{16,20},{20,16},{24,28},{28,24},{1,5},{5... | collective-permute-start | bytes 1572872 | tf_op jit(solution)/shard_map/ppermute | solution.py:289
  19.9 9.9 %collective-permute-start.6 = (bf16[128,1024]{1,0:T(8,128)(2,1)S(1)}, bf16[128,1024]{1,0:T(8,128)(2,1)S(1)}, u32[]{:S(2)}, u32[]{:S(2)}) collective-permute-start(bf16[128,1024]{1,0:T(8,128)(2,1)S(1)} %pad_maximum_fusion.1.refs_0_), channel_id=1, source_target_pairs={{0,24},{4,28},{8,16},{12,20},{16,8},{20,12},{24,0},{28,4},{1,25},{... | collective-permute-start | bytes 786440 | tf_op jit(solution)/shard_map/ppermute | solution.py:289
  22.9 11.6 %collective-permute-start.5 = (bf16[256,1024]{1,0:T(8,128)(2,1)S(1)}, bf16[256,1024]{1,0:T(8,128)(2,1)S(1)}, u32[]{:S(2)}, u32[]{:S(2)}) collective-permute-start(bf16[256,1024]{1,0:T(8,128)(2,1)S(1)} %pad_maximum_fusion.refs_4_), channel_id=1, source_target_pairs={{0,1},{1,0},{2,3},{3,2},{4,5},{5,4},{6,7},{7,6},{8,9},{9,8},{10,11... | collective-permute-start | bytes 1572872 | tf_op jit(solution)/shard_map/ppermute | solution.py:289
  29.9 4.0 %collective-permute-start = (bf16[128,1024]{1,0:T(8,128)(2,1)S(1)}, bf16[128,1024]{1,0:T(8,128)(2,1)S(1)}, u32[]{:S(2)}, u32[]{:S(2)}) collective-permute-start(bf16[128,1024]{1,0:T(8,128)(2,1)S(1)} %pad_maximum_fusion.1.refs_0_), channel_id=1, source_target_pairs={{0,1},{1,0},{2,3},{3,2},{4,5},{5,4},{6,7},{7,6},{8,9},{9,8},{10,11... | collective-permute-start | bytes 786440 | tf_op jit(solution)/shard_map/ppermute | solution.py:289
  29.9 4.7 %collective-permute-start.7 = (bf16[128,1024]{1,0:T(8,128)(2,1)S(1)}, bf16[128,1024]{1,0:T(8,128)(2,1)S(1)}, u32[]{:S(2)}, u32[]{:S(2)}) collective-permute-start(bf16[128,1024]{1,0:T(8,128)(2,1)S(1)} %collective-permute-done.6.refs_6_), channel_id=1, source_target_pairs={{0,1},{1,0},{2,3},{3,2},{4,5},{5,4},{6,7},{7,6},{8,9},{9,8},{10,11... | collective-permute-start | bytes 786440 | tf_op jit(solution)/shard_map/ppermute | solution.py:289
  32.3 7.2 %collective-permute-start.10 = (bf16[128,1024]{1,0:T(8,128)(2,1)S(1)}, bf16[128,1024]{1,0:T(8,128)(2,1)S(1)}, u32[]{:S(2)}, u32[]{:S(2)}) collective-permute-start(bf16[128,1024]{1,0:T(8,128)(2,1)S(1)} %collective-permute-done.6.refs_6_), channel_id=1, source_target_pairs={{0,4},{4,0},{8,12},{12,8},{16,20},{20,16},{24,28},{28,24},{1,5},{5... | collective-permute-start | bytes 786440 | tf_op jit(solution)/shard_map/ppermute | solution.py:289
  33.9 6.3 %collective-permute-start.12 = (bf16[256,1024]{1,0:T(8,128)(2,1)S(1)}, bf16[256,1024]{1,0:T(8,128)(2,1)S(1)}, u32[]{:S(2)}, u32[]{:S(2)}) collective-permute-start(bf16[256,1024]{1,0:T(8,128)(2,1)S(1)} %collective-permute-done.8.refs_8_), channel_id=1, source_target_pairs={{0,1},{1,0},{2,3},{3,2},{4,5},{5,4},{6,7},{7,6},{8,9},{9,8},{10,11... | collective-permute-start | bytes 1572872 | tf_op jit(solution)/shard_map/ppermute | solution.py:289
  38.6 5.7 %collective-permute-start.14 = (bf16[1,2,3,64,512]{4,3,2,1,0:T(8,128)(2,1)S(1)}, bf16[1,2,3,64,512]{4,3,2,1,0:T(8,128)(2,1)S(1)}, u32[]{:S(2)}, u32[]{:S(2)}) collective-permute-start(bf16[1,2,3,64,512]{4,3,2,1,0:T(8,128)(2,1)S(1)} %slice.16), channel_id=1, source_target_pairs={{0,1},{1,0},{2,3},{3,2},{4,5},{5,4},{6,7},{7,6},{8,9},{9,8},{10,11... | collective-permute-start | bytes 1179656 | tf_op jit(solution)/shard_map/ppermute | solution.py:289
  39.5 1.5 %collective-permute-start.11 = (bf16[128,1024]{1,0:T(8,128)(2,1)S(1)}, bf16[128,1024]{1,0:T(8,128)(2,1)S(1)}, u32[]{:S(2)}, u32[]{:S(2)}) collective-permute-start(bf16[128,1024]{1,0:T(8,128)(2,1)S(1)} %collective-permute-done.10.refs_0_), channel_id=1, source_target_pairs={{0,1},{1,0},{2,3},{3,2},{4,5},{5,4},{6,7},{7,6},{8,9},{9,8},{10,11... | collective-permute-start | bytes 786440 | tf_op jit(solution)/shard_map/ppermute | solution.py:289
  39.6 4.8 %collective-permute-start.15 = (bf16[1,2,1,64,512]{4,3,2,1,0:T(8,128)(2,1)S(1)}, bf16[1,2,1,64,512]{4,3,2,1,0:T(8,128)(2,1)S(1)}, u32[]{:S(2)}, u32[]{:S(2)}) collective-permute-start(bf16[1,2,1,64,512]{4,3,2,1,0:T(8,128)(2,1)S(1)} %slice.17), channel_id=1, source_target_pairs={{0,1},{1,0},{2,3},{3,2},{4,5},{5,4},{6,7},{7,6},{8,9},{9,8},{10,11... | collective-permute-start | bytes 393224 | tf_op jit(solution)/shard_map/ppermute | solution.py:289

commit v4 on v0

--- a/solution.py
+++ b/solution.py
@@ -104,9 +104,8 @@
 
 
 def add_pieces(places, scalars_ref, slot_ref, pieces, products, eigen):
-    source_ref, op_ref = scalars_ref
+    nops, source_ref, op_ref = scalars_ref
     blocks = eigen // LANES
-    nops = slot_ref.shape[0] // blocks // 2
     pair, side = lax.axis_index("tpair"), lax.axis_index("col") % 2
     cols = []
     for k in products:
@@ -135,10 +134,12 @@
     return groups, refs
 
 
-def assemble_kernel(places, counts, source_ref, op_ref, slot_ref, *refs):
+def assemble_kernel(places, counts, nops, source_ref, op_ref, slot_ref, *refs):
     pieces, (out_ref,) = grouped(counts, refs)
     products, eigen = out_ref.shape[0], out_ref.shape[2]
-    total = add_pieces(places, (source_ref, op_ref), slot_ref, pieces, range(products), eigen)
+    total = add_pieces(
+        places, (nops, source_ref, op_ref), slot_ref, pieces, range(products), eigen
+    )
     total = total.astype(BF16)
     for k in range(products):
         rows = slice(k * eigen, (k + 1) * eigen)
@@ -146,12 +147,12 @@
         out_ref[k, eigen:] = total[rows, eigen:]
 
 
-def assemble(places, pieces, source, op_index, slots, eigen):
+def assemble(places, pieces, nops, source, op_index, slots, eigen):
     products = op_index.shape[0]
     vmem = pl.BlockSpec(memory_space=pltpu.VMEM)
     smem = pl.BlockSpec(memory_space=pltpu.SMEM)
     return pl.pallas_call(
-        functools.partial(assemble_kernel, places, [len(group) for group in pieces]),
+        functools.partial(assemble_kernel, places, [len(group) for group in pieces], nops),
         in_specs=[smem, smem] + [vmem] * (1 + sum(len(group) for group in pieces)),
         out_specs=vmem,
         out_shape=jax.ShapeDtypeStruct((products, 2 * eigen, eigen), BF16),
@@ -201,11 +202,11 @@
     return list(zip(times, results))
 
 
-def near_kernel(places, masks, counts, source_ref, op_ref, slot_ref, partial_ref, *refs):
+def near_kernel(places, masks, counts, nops, source_ref, op_ref, slot_ref, partial_ref, *refs):
     groups, (right, done) = grouped(counts, refs)
     pieces, blocks = groups[: len(places)], groups[len(places) :]
     products, eigen = right.shape[0], right.shape[2]
-    scalars = (source_ref, op_ref)
+    scalars = (nops, source_ref, op_ref)
     for k in range(products):
         total = add_pieces(places, scalars, slot_ref, pieces, [k], eigen).astype(BF16)
         right[k, :eigen] = partial_ref[k, :eigen] + total[:, :eigen]
@@ -245,7 +246,7 @@
     return [part for group in groups for part in group]
 
 
-def contract(places, pieces, partial, source, op_index, slots, blocks):
+def contract(places, pieces, partial, nops, source, op_index, slots, blocks):
     _, products, _, own2, local_cols = blocks[0][0].shape
     n_cols = len(blocks)
     eigen = partial.shape[2]
@@ -259,7 +260,7 @@
     half = (products, times // 2, NS, own2 // 2, 2, eigen)
     groups = pieces + blocks[:near]
     right, done = pl.pallas_call(
-        functools.partial(near_kernel, places, near_masks, [len(g) for g in groups]),
+        functools.partial(near_kernel, places, near_masks, [len(g) for g in groups], nops),
         in_specs=[smem, smem] + [vmem] * (2 + len(flat(groups))),
         out_specs=[vmem, vmem],
         out_shape=[
@@ -300,6 +301,7 @@
     n_pair = lax.axis_size("tpair")
     rows, _, eigen = op_table.shape
     slots = row_slot.reshape(-1, LANES)
+    nops = sink_ops.shape[1]
 
     def across(array, mask):
         return swap(array, "tpair", n_pair, mask)
@@ -313,9 +315,9 @@
         half = whole.shape[0] // 2
         mixed = mix(op_index, listed_rows, sink_ops, peramb, [1] * n_cols)
         blocks = [[mixed[0]]] + [[swap(mixed[j], "col", n_cols, j)] for j in range(1, n_cols)]
-        partial = assemble([[0]], [[whole[:half]]], pair_source, op_index, slots, eigen)
+        partial = assemble([[0]], [[whole[:half]]], nops, pair_source, op_index, slots, eigen)
         return contract(
-            [[half]], [[whole[half:]]], partial, pair_source, op_index, slots, blocks
+            [[half]], [[whole[half:]]], partial, nops, pair_source, op_index, slots, blocks
         )
     half = rows // 2
     own = lax.dynamic_slice_in_dim(op_table, lax.axis_index("col") % 2 * half, half, 0)
@@ -340,13 +342,13 @@
         ([(3, 0), (5, 0)], x12),
     ]
     places, pieces = [p for p, _ in early], [[piece] for _, piece in early]
-    partial = assemble(places, pieces, pair_source, op_index, slots, eigen)
+    partial = assemble(places, pieces, nops, pair_source, op_index, slots, eigen)
     spins = [crossed[1:, :, : NS - 1], crossed[1:, :, NS - 1 :]]
     over = [beside(after(some, partial)) for some in spins]
     blocks = [[mixed[0]], [beside_mixed], [crossed], over]
     late = [[x3], [beside(after(x3, partial))], [beside(x12)]]
     places = [[(7, 0)], [(7, 1)], [(3, 1), (5, 1)]]
-    return contract(places, late, partial, pair_source, op_index, slots, blocks)
+    return contract(places, late, partial, nops, pair_source, op_index, slots, blocks)
 
 
 def solution(mesh):

time: 47.1 us -> 47.1 us (level)
  no operation moved by 1% of the time
where the time goes in v4:
time: 47.1 us; the launch traced here: 46.3 us
  starting transfers between devices  15.6 us (33%)
  Pallas kernels  14.2 us (30%)
  waiting for transfers between devices  14 us (30%)
  local copies, waits for them, and re-layouts  1.69 us (4%)
  between operations  0.78 us (2%)
    ppermute x16, starting transfers between devices, swap(): return lax.ppermute(array, axis, [(i, i ^ mask) for i in range(size)])  15.6 us
    ppermute x16, waiting for transfers between devices, swap(): return lax.ppermute(array, axis, [(i, i ^ mask) for i in range(size)])  14 us
    pallas_call x1, Pallas kernels, mix(): pl.pallas_call(mix_kernel, in_specs=[pl.BlockSpec(memory_space=pltpu.SMEM...  4.99 us
    pallas_call x1, Pallas kernels, assemble(): pl.pallas_call(functools.partial(assemble_kernel, places, [len(group) for...  4.01 us
    pallas_call x1, Pallas kernels, contract(): pl.pallas_call(functools.partial(near_kernel, places, near_masks, [len(g)...  2.99 us
    pallas_call x1, Pallas kernels, contract(): pl.pallas_call(functools.partial(far_kernel, near_masks, far_masks, [len(...  2.16 us
    slice x1, local copies, waits for them, and re-layouts, per_device(): own = jnp.concatenate([own[:, 0], own[:, 1]], axis=1)  1.6 us
  transfers between devices with their start and end apart: 16, of which 6 were waited for; matrix products, arithmetic and copies ran while one was open for 0% of the time, Pallas kernels for 26%

profile of v4, /device:TPU:0, one launch (start us, length us, event | category | flops | bytes accessed | tf_op | source)
XLA Modules:
  0.0 46.3 jit_solution(7111034914140406013)
XLA Ops:
  0.0 1.6 %constant_dynamic-slice_fusion = (bf16[128,1,512]{2,1,0:T(2,128)(2,1)S(1)}, bf16[128,1,512]{2,1,0:T(2,128)(2,1)S(1)}) fusion(bf16[256,2,512]{2,1,0:T(2,128)(2,1)} %param.9, s32[]{:T(128)S(6)} %select_n.11, s32[]{:T(128)S(6)} %add.9), kind=kLoop, calls=%fused_computation.4 | loop fusion | bytes 524296 | tf_op jit(solution)/shard_map/slice | solution.py:324
  1.7 0.0 copy-start.1
  1.7 4.1 %collective-permute-start.4 = (bf16[128,1024]{1,0:T(8,128)(2,1)S(1)}, bf16[128,1024]{1,0:T(8,128)(2,1)S(1)}, u32[]{:S(2)}, u32[]{:S(2)}) collective-permute-start(bf16[128,1024]{1,0:T(8,128)(2,1)S(1)} %pad_maximum_fusion.1.refs_0_), channel_id=1, source_target_pairs={{0,16},{4,20},{8,24},{12,28},{16,0},{20,4},{24,8},{28,12},{1,17},{... | collective-permute-start | bytes 786440 | tf_op jit(solution)/shard_map/ppermute | solution.py:292
  5.8 1.5 %collective-permute-start.1 = (bf16[128,1024]{1,0:T(8,128)(2,1)S(1)}, bf16[128,1024]{1,0:T(8,128)(2,1)S(1)}, u32[]{:S(2)}, u32[]{:S(2)}) collective-permute-start(bf16[128,1024]{1,0:T(8,128)(2,1)S(1)} %pad_maximum_fusion.1.refs_0_), channel_id=1, source_target_pairs={{0,4},{4,0},{8,12},{12,8},{16,20},{20,16},{24,28},{28,24},{1,5},{5... | collective-permute-start | bytes 786440 | tf_op jit(solution)/shard_map/ppermute | solution.py:292
  7.3 1.6 %collective-permute-start.3 = (bf16[128,1024]{1,0:T(8,128)(2,1)S(1)}, bf16[128,1024]{1,0:T(8,128)(2,1)S(1)}, u32[]{:S(2)}, u32[]{:S(2)}) collective-permute-start(bf16[128,1024]{1,0:T(8,128)(2,1)S(1)} %pad_maximum_fusion.1.refs_0_), channel_id=1, source_target_pairs={{0,8},{4,12},{8,0},{12,4},{16,24},{20,28},{24,16},{28,20},{1,9},{5... | collective-permute-start | bytes 786440 | tf_op jit(solution)/shard_map/ppermute | solution.py:292
  8.9 5.0 %mix.1 = (bf16[1,2,4,64,512]{4,3,2,1,0:T(8,128)(2,1)S(1)}, bf16[1,2,4,64,512]{4,3,2,1,0:T(8,128)(2,1)S(1)}, bf16[2,2,4,64,512]{4,3,2,1,0:T(8,128)(2,1)S(1)}) custom-call(s32[2,2]{1,0:T(2,128)S(1)} %copy-done.2, s32[2,128]{1,0:T(2,128)S(1)} %copy-done.3, bf16[1,2,2,512,512]{4,3,2,1,0:T(8,128)(2,1)S(1)} %copy-done, bf16[1,2,2048,512]{3,2,1,0:T(8,128)(2,1)} %peramb_ref.1), custom_call_target="tpu_custom_call" | custom-call | flops 1000 | bytes 1000 | tf_op jit(solution)/shard_map/mix/pallas_call | solution.py:88
  13.9 1.6 %collective-permute-start.13 = (bf16[2,2,4,64,512]{4,3,2,1,0:T(8,128)(2,1)S(1)}, bf16[2,2,4,64,512]{4,3,2,1,0:T(8,128)(2,1)S(1)}, u32[]{:S(2)}, u32[]{:S(2)}) collective-permute-start(bf16[2,2,4,64,512]{4,3,2,1,0:T(8,128)(2,1)S(1)} %get-tuple-element.28), channel_id=1, source_target_pairs={{0,2},{1,3},{2,0},{3,1},{4,6},{5,7},{6,4},{7,5},{8,10},{9,11},{10,... | collective-permute-start | bytes 3145736 | tf_op jit(solution)/shard_map/ppermute | solution.py:292
  15.5 0.0 collective-permute-start.9
  15.5 2.4 %collective-permute-done.4 = bf16[128,1024]{1,0:T(8,128)(2,1)S(1)} collective-permute-done((bf16[128,1024]{1,0:T(8,128)(2,1)S(1)}, bf16[128,1024]{1,0:T(8,128)(2,1)S(1)}, u32[]{:S(2)}, u32[]{:S(2)}) %collective-permute-start.4) | collective-permute-done | bytes 262176 | tf_op jit(solution)/shard_map/ppermute | solution.py:292
  17.9 0.0 collective-permute-done.1.refs_2_
  17.9 0.0 collective-permute-start.2
  17.9 1.4 %collective-permute-done.3 = bf16[128,1024]{1,0:T(8,128)(2,1)S(1)} collective-permute-done((bf16[128,1024]{1,0:T(8,128)(2,1)S(1)}, bf16[128,1024]{1,0:T(8,128)(2,1)S(1)}, u32[]{:S(2)}, u32[]{:S(2)}) %collective-permute-start.3) | collective-permute-done | bytes 262176 | tf_op jit(solution)/shard_map/ppermute | solution.py:292
  19.3 0.6 %collective-permute-start.8 = (bf16[256,1024]{1,0:T(8,128)(2,1)S(1)}, bf16[256,1024]{1,0:T(8,128)(2,1)S(1)}, u32[]{:S(2)}, u32[]{:S(2)}) collective-permute-start(bf16[256,1024]{1,0:T(8,128)(2,1)S(1)} %pad_maximum_fusion.refs_4_), channel_id=1, source_target_pairs={{0,4},{4,0},{8,12},{12,8},{16,20},{20,16},{24,28},{28,24},{1,5},{5... | collective-permute-start | bytes 1572872 | tf_op jit(solution)/shard_map/ppermute | solution.py:292
  19.9 3.0 %collective-permute-start.6 = (bf16[128,1024]{1,0:T(8,128)(2,1)S(1)}, bf16[128,1024]{1,0:T(8,128)(2,1)S(1)}, u32[]{:S(2)}, u32[]{:S(2)}) collective-permute-start(bf16[128,1024]{1,0:T(8,128)(2,1)S(1)} %pad_maximum_fusion.1.refs_0_), channel_id=1, source_target_pairs={{0,24},{4,28},{8,16},{12,20},{16,8},{20,12},{24,0},{28,4},{1,25},{... | collective-permute-start | bytes 786440 | tf_op jit(solution)/shard_map/ppermute | solution.py:292
  22.9 0.0 collective-permute-done.2.refs_3_
  22.9 6.9 %collective-permute-done.6.refs_6_ = bf16[128,1024]{1,0:T(8,128)(2,1)S(1)} collective-permute-done((bf16[128,1024]{1,0:T(8,128)(2,1)S(1)}, bf16[128,1024]{1,0:T(8,128)(2,1)S(1)}, u32[]{:S(2)}, u32[]{:S(2)}) %collective-permute-start.6) | collective-permute-done | bytes 262176 | tf_op jit(solution)/shard_map/ppermute | solution.py:292
  29.9 0.0 collective-permute-start
  29.9 0.0 collective-permute-done.9.refs_4_
  29.9 0.5 %collective-permute-start.7 = (bf16[128,1024]{1,0:T(8,128)(2,1)S(1)}, bf16[128,1024]{1,0:T(8,128)(2,1)S(1)}, u32[]{:S(2)}, u32[]{:S(2)}) collective-permute-start(bf16[128,1024]{1,0:T(8,128)(2,1)S(1)} %collective-permute-done.6.refs_6_), channel_id=1, source_target_pairs={{0,1},{1,0},{2,3},{3,2},{4,5},{5,4},{6,7},{7,6},{8,9},{9,8},{10,11... | collective-permute-start | bytes 786440 | tf_op jit(solution)/shard_map/ppermute | solution.py:292
  30.4 1.9 %collective-permute-done.8.refs_8_ = bf16[256,1024]{1,0:T(8,128)(2,1)S(1)} collective-permute-done((bf16[256,1024]{1,0:T(8,128)(2,1)S(1)}, bf16[256,1024]{1,0:T(8,128)(2,1)S(1)}, u32[]{:S(2)}, u32[]{:S(2)}) %collective-permute-start.8) | collective-permute-done | bytes 524320 | tf_op jit(solution)/shard_map/ppermute | solution.py:292
  32.3 1.5 %collective-permute-start.10 = (bf16[128,1024]{1,0:T(8,128)(2,1)S(1)}, bf16[128,1024]{1,0:T(8,128)(2,1)S(1)}, u32[]{:S(2)}, u32[]{:S(2)}) collective-permute-start(bf16[128,1024]{1,0:T(8,128)(2,1)S(1)} %collective-permute-done.6.refs_6_), channel_id=1, source_target_pairs={{0,4},{4,0},{8,12},{12,8},{16,20},{20,16},{24,28},{28,24},{1,5},{5... | collective-permute-start | bytes 786440 | tf_op jit(solution)/shard_map/ppermute | solution.py:292
  33.8 0.0 collective-permute-done.refs_1_
  34.5 0.0 collective-permute-done.5.refs_5_
  34.5 4.0 %assemble.1.partial_ref = bf16[2,1024,512]{2,1,0:T(8,128)(2,1)S(1)} custom-call(s32[1]{0:T(128)S(6)} %copy.14.source_ref, s32[2,2]{1,0:T(2,128)S(1)} %copy-done.2, s32[16,128]{1,0:T(8,128)S(1)} %bitcast.5, bf16[128,1024]{1,0:T(8,128)(2,1)S(1)} %pad_maximum_fusion.1.refs_0_, bf16[128,1024]{1,0:T(8,128)(2,1)S(1)} %collective-permute-done.refs_1_, ...), custom_call_target="tpu_custom_call" | custom-call | flops 1000 | bytes 1000 | tf_op jit(solution)/shard_map/assemble/pallas_call | solution.py:154
  38.6 0.6 %collective-permute-start.14 = (bf16[1,2,3,64,512]{4,3,2,1,0:T(8,128)(2,1)S(1)}, bf16[1,2,3,64,512]{4,3,2,1,0:T(8,128)(2,1)S(1)}, u32[]{:S(2)}, u32[]{:S(2)}) collective-permute-start(bf16[1,2,3,64,512]{4,3,2,1,0:T(8,128)(2,1)S(1)} %slice.16), channel_id=1, source_target_pairs={{0,1},{1,0},{2,3},{3,2},{4,5},{5,4},{6,7},{7,6},{8,9},{9,8},{10,11... | collective-permute-start | bytes 1179656 | tf_op jit(solution)/shard_map/ppermute | solution.py:292
  39.2 0.4 collective-permute-done.10.refs_0_
  39.5 0.0 collective-permute-start.11
  39.6 0.6 %collective-permute-start.15 = (bf16[1,2,1,64,512]{4,3,2,1,0:T(8,128)(2,1)S(1)}, bf16[1,2,1,64,512]{4,3,2,1,0:T(8,128)(2,1)S(1)}, u32[]{:S(2)}, u32[]{:S(2)}) collective-permute-start(bf16[1,2,1,64,512]{4,3,2,1,0:T(8,128)(2,1)S(1)} %slice.17), channel_id=1, source_target_pairs={{0,1},{1,0},{2,3},{3,2},{4,5},{5,4},{6,7},{7,6},{8,9},{9,8},{10,11... | collective-permute-start | bytes 393224 | tf_op jit(solution)/shard_map/ppermute | solution.py:292
  40.1 0.9 %collective-permute-done.11.refs_1_ = bf16[128,1024]{1,0:T(8,128)(2,1)S(1)} collective-permute-done((bf16[128,1024]{1,0:T(8,128)(2,1)S(1)}, bf16[128,1024]{1,0:T(8,128)(2,1)S(1)}, u32[]{:S(2)}, u32[]{:S(2)}) %collective-permute-start.11) | collective-permute-done | bytes 262176 | tf_op jit(solution)/shard_map/ppermute | solution.py:292
  41.1 3.0 %near.1 = (bf16[2,1024,512]{2,1,0:T(8,128)(2,1)S(1)}, bf16[2,2,4,32,2,512]{5,4,3,2,1,0:T(2,128)(2,1)S(1)}) custom-call(s32[1]{0:T(128)S(6)} %copy.14.source_ref, s32[2,2]{1,0:T(2,128)S(1)} %copy-done.2, s32[16,128]{1,0:T(8,128)S(1)} %bitcast.6, bf16[2,1024,512]{2,1,0:T(8,128)(2,1)S(1)} %assemble.1.partial_ref, ...), custom_call_target="tpu_custom_call" | custom-call | flops 1000000000 | bytes 1000 | tf_op jit(solution)/shard_map/near/pallas_call | solution.py:262
  44.1 0.0 collective-permute-done.14.refs_1_
  44.1 2.2 %far.1 = bf16[2,4,32,2,2048]{4,3,2,1,0:T(2,128)(2,1)} custom-call(bf16[2,1024,512]{2,1,0:T(8,128)(2,1)S(1)} %get-tuple-element.26.right, bf16[2,2,4,32,2,512]{5,4,3,2,1,0:T(2,128)(2,1)S(1)} %get-tuple-element.27.near_ref, bf16[2,2,4,64,512]{4,3,2,1,0:T(8,128)(2,1)S(1)} %collective-permute-done.13.refs_0_, ...), custom_call_target="tpu_custom_call" | custom-call | flops 1000000000 | bytes 1000 | tf_op jit(solution)/shard_map/far/pallas_call | solution.py:275
  (18 shorter events, 0.2 us)
Async XLA Ops:
  0.0 8.9 %copy-start.2 = (s32[2,2]{1,0:T(2,128)S(1)}, s32[2,2]{1,0:T(2,128)}, u32[]{:S(2)}) copy-start(s32[2,2]{1,0:T(2,128)} %op_ref.5) | copy-start | bytes 52
  0.0 8.9 %copy-start.3 = (s32[2,128]{1,0:T(2,128)S(1)}, s32[2,128]{1,0:T(2,128)}, u32[]{:S(2)}) copy-start(s32[2,128]{1,0:T(2,128)} %listed_ref.1) | copy-start | bytes 3076
  0.0 8.9 %copy-start = (bf16[1,2,2,512,512]{4,3,2,1,0:T(8,128)(2,1)S(1)}, bf16[1,2,2,512,512]{4,3,2,1,0:T(8,128)(2,1)}, u32[]{:S(2)}) copy-start(bf16[1,2,2,512,512]{4,3,2,1,0:T(8,128)(2,1)} %sink_ref.1) | copy-start | bytes 6291460
  1.7 32.8 %copy-start.1 = (s32[2048]{0:T(1024)S(1)}, s32[2048]{0:T(1024)}, u32[]{:S(2)}) copy-start(s32[2048]{0:T(1024)} %param.10) | copy-start | bytes 24580
  1.7 16.2 %collective-permute-start.4 = (bf16[128,1024]{1,0:T(8,128)(2,1)S(1)}, bf16[128,1024]{1,0:T(8,128)(2,1)S(1)}, u32[]{:S(2)}, u32[]{:S(2)}) collective-permute-start(bf16[128,1024]{1,0:T(8,128)(2,1)S(1)} %pad_maximum_fusion.1.refs_0_), channel_id=1, source_target_pairs={{0,16},{4,20},{8,24},{12,28},{16,0},{20,4},{24,8},{28,12},{1,17},{... | collective-permute-start | bytes 786440 | tf_op jit(solution)/shard_map/ppermute | solution.py:292
  5.8 12.0 %collective-permute-start.1 = (bf16[128,1024]{1,0:T(8,128)(2,1)S(1)}, bf16[128,1024]{1,0:T(8,128)(2,1)S(1)}, u32[]{:S(2)}, u32[]{:S(2)}) collective-permute-start(bf16[128,1024]{1,0:T(8,128)(2,1)S(1)} %pad_maximum_fusion.1.refs_0_), channel_id=1, source_target_pairs={{0,4},{4,0},{8,12},{12,8},{16,20},{20,16},{24,28},{28,24},{1,5},{5... | collective-permute-start | bytes 786440 | tf_op jit(solution)/shard_map/ppermute | solution.py:292
  7.3 11.9 %collective-permute-start.3 = (bf16[128,1024]{1,0:T(8,128)(2,1)S(1)}, bf16[128,1024]{1,0:T(8,128)(2,1)S(1)}, u32[]{:S(2)}, u32[]{:S(2)}) collective-permute-start(bf16[128,1024]{1,0:T(8,128)(2,1)S(1)} %pad_maximum_fusion.1.refs_0_), channel_id=1, source_target_pairs={{0,8},{4,12},{8,0},{12,4},{16,24},{20,28},{24,16},{28,20},{1,9},{5... | collective-permute-start | bytes 786440 | tf_op jit(solution)/shard_map/ppermute | solution.py:292
  13.9 24.7 %collective-permute-start.13 = (bf16[2,2,4,64,512]{4,3,2,1,0:T(8,128)(2,1)S(1)}, bf16[2,2,4,64,512]{4,3,2,1,0:T(8,128)(2,1)S(1)}, u32[]{:S(2)}, u32[]{:S(2)}) collective-permute-start(bf16[2,2,4,64,512]{4,3,2,1,0:T(8,128)(2,1)S(1)} %get-tuple-element.28), channel_id=1, source_target_pairs={{0,2},{1,3},{2,0},{3,1},{4,6},{5,7},{6,4},{7,5},{8,10},{9,11},{10,... | collective-permute-start | bytes 3145736 | tf_op jit(solution)/shard_map/ppermute | solution.py:292
  15.5 14.4 %collective-permute-start.9 = (bf16[1,2,4,64,512]{4,3,2,1,0:T(8,128)(2,1)S(1)}, bf16[1,2,4,64,512]{4,3,2,1,0:T(8,128)(2,1)S(1)}, u32[]{:S(2)}, u32[]{:S(2)}) collective-permute-start(bf16[1,2,4,64,512]{4,3,2,1,0:T(8,128)(2,1)S(1)} %get-tuple-element.23), channel_id=1, source_target_pairs={{0,1},{1,0},{2,3},{3,2},{4,5},{5,4},{6,7},{7,6},{8,9},{9,8},{10,11... | collective-permute-start | bytes 1572872 | tf_op jit(solution)/shard_map/ppermute | solution.py:292
  17.9 5.1 %collective-permute-start.2 = (bf16[128,1024]{1,0:T(8,128)(2,1)S(1)}, bf16[128,1024]{1,0:T(8,128)(2,1)S(1)}, u32[]{:S(2)}, u32[]{:S(2)}) collective-permute-start(bf16[128,1024]{1,0:T(8,128)(2,1)S(1)} %collective-permute-done.1.refs_2_), channel_id=1, source_target_pairs={{0,1},{1,0},{2,3},{3,2},{4,5},{5,4},{6,7},{7,6},{8,9},{9,8},{10,11... | collective-permute-start | bytes 786440 | tf_op jit(solution)/shard_map/ppermute | solution.py:292
  19.3 13.0 %collective-permute-start.8 = (bf16[256,1024]{1,0:T(8,128)(2,1)S(1)}, bf16[256,1024]{1,0:T(8,128)(2,1)S(1)}, u32[]{:S(2)}, u32[]{:S(2)}) collective-permute-start(bf16[256,1024]{1,0:T(8,128)(2,1)S(1)} %pad_maximum_fusion.refs_4_), channel_id=1, source_target_pairs={{0,4},{4,0},{8,12},{12,8},{16,20},{20,16},{24,28},{28,24},{1,5},{5... | collective-permute-start | bytes 1572872 | tf_op jit(solution)/shard_map/ppermute | solution.py:292
  19.9 9.9 %collective-permute-start.6 = (bf16[128,1024]{1,0:T(8,128)(2,1)S(1)}, bf16[128,1024]{1,0:T(8,128)(2,1)S(1)}, u32[]{:S(2)}, u32[]{:S(2)}) collective-permute-start(bf16[128,1024]{1,0:T(8,128)(2,1)S(1)} %pad_maximum_fusion.1.refs_0_), channel_id=1, source_target_pairs={{0,24},{4,28},{8,16},{12,20},{16,8},{20,12},{24,0},{28,4},{1,25},{... | collective-permute-start | bytes 786440 | tf_op jit(solution)/shard_map/ppermute | solution.py:292
  22.9 11.6 %collective-permute-start.5 = (bf16[256,1024]{1,0:T(8,128)(2,1)S(1)}, bf16[256,1024]{1,0:T(8,128)(2,1)S(1)}, u32[]{:S(2)}, u32[]{:S(2)}) collective-permute-start(bf16[256,1024]{1,0:T(8,128)(2,1)S(1)} %pad_maximum_fusion.refs_4_), channel_id=1, source_target_pairs={{0,1},{1,0},{2,3},{3,2},{4,5},{5,4},{6,7},{7,6},{8,9},{9,8},{10,11... | collective-permute-start | bytes 1572872 | tf_op jit(solution)/shard_map/ppermute | solution.py:292
  29.9 4.0 %collective-permute-start = (bf16[128,1024]{1,0:T(8,128)(2,1)S(1)}, bf16[128,1024]{1,0:T(8,128)(2,1)S(1)}, u32[]{:S(2)}, u32[]{:S(2)}) collective-permute-start(bf16[128,1024]{1,0:T(8,128)(2,1)S(1)} %pad_maximum_fusion.1.refs_0_), channel_id=1, source_target_pairs={{0,1},{1,0},{2,3},{3,2},{4,5},{5,4},{6,7},{7,6},{8,9},{9,8},{10,11... | collective-permute-start | bytes 786440 | tf_op jit(solution)/shard_map/ppermute | solution.py:292
  29.9 4.7 %collective-permute-start.7 = (bf16[128,1024]{1,0:T(8,128)(2,1)S(1)}, bf16[128,1024]{1,0:T(8,128)(2,1)S(1)}, u32[]{:S(2)}, u32[]{:S(2)}) collective-permute-start(bf16[128,1024]{1,0:T(8,128)(2,1)S(1)} %collective-permute-done.6.refs_6_), channel_id=1, source_target_pairs={{0,1},{1,0},{2,3},{3,2},{4,5},{5,4},{6,7},{7,6},{8,9},{9,8},{10,11... | collective-permute-start | bytes 786440 | tf_op jit(solution)/shard_map/ppermute | solution.py:292
  32.3 7.2 %collective-permute-start.10 = (bf16[128,1024]{1,0:T(8,128)(2,1)S(1)}, bf16[128,1024]{1,0:T(8,128)(2,1)S(1)}, u32[]{:S(2)}, u32[]{:S(2)}) collective-permute-start(bf16[128,1024]{1,0:T(8,128)(2,1)S(1)} %collective-permute-done.6.refs_6_), channel_id=1, source_target_pairs={{0,4},{4,0},{8,12},{12,8},{16,20},{20,16},{24,28},{28,24},{1,5},{5... | collective-permute-start | bytes 786440 | tf_op jit(solution)/shard_map/ppermute | solution.py:292
  33.9 6.3 %collective-permute-start.12 = (bf16[256,1024]{1,0:T(8,128)(2,1)S(1)}, bf16[256,1024]{1,0:T(8,128)(2,1)S(1)}, u32[]{:S(2)}, u32[]{:S(2)}) collective-permute-start(bf16[256,1024]{1,0:T(8,128)(2,1)S(1)} %collective-permute-done.8.refs_8_), channel_id=1, source_target_pairs={{0,1},{1,0},{2,3},{3,2},{4,5},{5,4},{6,7},{7,6},{8,9},{9,8},{10,11... | collective-permute-start | bytes 1572872 | tf_op jit(solution)/shard_map/ppermute | solution.py:292
  38.6 5.5 %collective-permute-start.14 = (bf16[1,2,3,64,512]{4,3,2,1,0:T(8,128)(2,1)S(1)}, bf16[1,2,3,64,512]{4,3,2,1,0:T(8,128)(2,1)S(1)}, u32[]{:S(2)}, u32[]{:S(2)}) collective-permute-start(bf16[1,2,3,64,512]{4,3,2,1,0:T(8,128)(2,1)S(1)} %slice.16), channel_id=1, source_target_pairs={{0,1},{1,0},{2,3},{3,2},{4,5},{5,4},{6,7},{7,6},{8,9},{9,8},{10,11... | collective-permute-start | bytes 1179656 | tf_op jit(solution)/shard_map/ppermute | solution.py:292
  39.5 1.5 %collective-permute-start.11 = (bf16[128,1024]{1,0:T(8,128)(2,1)S(1)}, bf16[128,1024]{1,0:T(8,128)(2,1)S(1)}, u32[]{:S(2)}, u32[]{:S(2)}) collective-permute-start(bf16[128,1024]{1,0:T(8,128)(2,1)S(1)} %collective-permute-done.10.refs_0_), channel_id=1, source_target_pairs={{0,1},{1,0},{2,3},{3,2},{4,5},{5,4},{6,7},{7,6},{8,9},{9,8},{10,11... | collective-permute-start | bytes 786440 | tf_op jit(solution)/shard_map/ppermute | solution.py:292
  39.6 4.5 %collective-permute-start.15 = (bf16[1,2,1,64,512]{4,3,2,1,0:T(8,128)(2,1)S(1)}, bf16[1,2,1,64,512]{4,3,2,1,0:T(8,128)(2,1)S(1)}, u32[]{:S(2)}, u32[]{:S(2)}) collective-permute-start(bf16[1,2,1,64,512]{4,3,2,1,0:T(8,128)(2,1)S(1)} %slice.17), channel_id=1, source_target_pairs={{0,1},{1,0},{2,3},{3,2},{4,5},{5,4},{6,7},{7,6},{8,9},{9,8},{10,11... | collective-permute-start | bytes 393224 | tf_op jit(solution)/shard_map/ppermute | solution.py:292

commit v5 on v4

--- a/solution.py
+++ b/solution.py
@@ -181,10 +181,9 @@
         y = jnp.where(odd, pltpu.roll(wide, 1, 0), -pltpu.roll(wide, rows - 1, 0))
         turned.append(y.astype(BF16))
     if per_time == 1:
-        lhs = jnp.concatenate(
-            [jnp.concatenate(direct, axis=0), jnp.concatenate(turned, axis=0)], axis=1
-        )
-        whole = dot(lhs, right[k]).astype(BF16)
+        whole = dot(jnp.concatenate(direct, axis=0), right[k, :eigen])
+        whole += dot(jnp.concatenate(turned, axis=0), right[k, eigen:])
+        whole = whole.astype(BF16)
         results = [whole[n * rows : (n + 1) * rows] for n in range(len(masks))]
     else:
         results = []

time: 47.1 us -> 47.1 us (level)
  no operation moved by 1% of the time
where the time goes in v5:
time: 47.1 us; the launch traced here: 46.2 us
  starting transfers between devices  15.6 us (33%)
  Pallas kernels  14.1 us (30%)
  waiting for transfers between devices  14 us (30%)
  local copies, waits for them, and re-layouts  1.69 us (4%)
  between operations  0.78 us (2%)
    ppermute x16, starting transfers between devices, swap(): return lax.ppermute(array, axis, [(i, i ^ mask) for i in range(size)])  15.6 us
    ppermute x16, waiting for transfers between devices, swap(): return lax.ppermute(array, axis, [(i, i ^ mask) for i in range(size)])  14 us
    pallas_call x1, Pallas kernels, mix(): pl.pallas_call(mix_kernel, in_specs=[pl.BlockSpec(memory_space=pltpu.SMEM...  4.99 us
    pallas_call x1, Pallas kernels, assemble(): pl.pallas_call(functools.partial(assemble_kernel, places, [len(group) for...  4.01 us
    pallas_call x1, Pallas kernels, contract(): pl.pallas_call(functools.partial(near_kernel, places, near_masks, [len(g)...  3.03 us
    pallas_call x1, Pallas kernels, contract(): pl.pallas_call(functools.partial(far_kernel, near_masks, far_masks, [len(...  2.11 us
    slice x1, local copies, waits for them, and re-layouts, per_device(): own = jnp.concatenate([own[:, 0], own[:, 1]], axis=1)  1.6 us
  transfers between devices with their start and end apart: 16, of which 6 were waited for; matrix products, arithmetic and copies ran while one was open for 0% of the time, Pallas kernels for 26%

profile of v5, /device:TPU:0, one launch (start us, length us, event | category | flops | bytes accessed | tf_op | source)
XLA Modules:
  0.0 46.2 jit_solution(10144291603914473247)
XLA Ops:
  0.0 1.6 %constant_dynamic-slice_fusion = (bf16[128,1,512]{2,1,0:T(2,128)(2,1)S(1)}, bf16[128,1,512]{2,1,0:T(2,128)(2,1)S(1)}) fusion(bf16[256,2,512]{2,1,0:T(2,128)(2,1)} %param.9, s32[]{:T(128)S(6)} %select_n.11, s32[]{:T(128)S(6)} %add.9), kind=kLoop, calls=%fused_computation.4 | loop fusion | bytes 524296 | tf_op jit(solution)/shard_map/slice | solution.py:323
  1.7 0.0 copy-start.1
  1.7 4.1 %collective-permute-start.4 = (bf16[128,1024]{1,0:T(8,128)(2,1)S(1)}, bf16[128,1024]{1,0:T(8,128)(2,1)S(1)}, u32[]{:S(2)}, u32[]{:S(2)}) collective-permute-start(bf16[128,1024]{1,0:T(8,128)(2,1)S(1)} %pad_maximum_fusion.1.refs_0_), channel_id=1, source_target_pairs={{0,16},{4,20},{8,24},{12,28},{16,0},{20,4},{24,8},{28,12},{1,17},{... | collective-permute-start | bytes 786440 | tf_op jit(solution)/shard_map/ppermute | solution.py:291
  5.8 1.5 %collective-permute-start.1 = (bf16[128,1024]{1,0:T(8,128)(2,1)S(1)}, bf16[128,1024]{1,0:T(8,128)(2,1)S(1)}, u32[]{:S(2)}, u32[]{:S(2)}) collective-permute-start(bf16[128,1024]{1,0:T(8,128)(2,1)S(1)} %pad_maximum_fusion.1.refs_0_), channel_id=1, source_target_pairs={{0,4},{4,0},{8,12},{12,8},{16,20},{20,16},{24,28},{28,24},{1,5},{5... | collective-permute-start | bytes 786440 | tf_op jit(solution)/shard_map/ppermute | solution.py:291
  7.3 1.6 %collective-permute-start.3 = (bf16[128,1024]{1,0:T(8,128)(2,1)S(1)}, bf16[128,1024]{1,0:T(8,128)(2,1)S(1)}, u32[]{:S(2)}, u32[]{:S(2)}) collective-permute-start(bf16[128,1024]{1,0:T(8,128)(2,1)S(1)} %pad_maximum_fusion.1.refs_0_), channel_id=1, source_target_pairs={{0,8},{4,12},{8,0},{12,4},{16,24},{20,28},{24,16},{28,20},{1,9},{5... | collective-permute-start | bytes 786440 | tf_op jit(solution)/shard_map/ppermute | solution.py:291
  8.9 5.0 %mix.1 = (bf16[1,2,4,64,512]{4,3,2,1,0:T(8,128)(2,1)S(1)}, bf16[1,2,4,64,512]{4,3,2,1,0:T(8,128)(2,1)S(1)}, bf16[2,2,4,64,512]{4,3,2,1,0:T(8,128)(2,1)S(1)}) custom-call(s32[2,2]{1,0:T(2,128)S(1)} %copy-done.2, s32[2,128]{1,0:T(2,128)S(1)} %copy-done.3, bf16[1,2,2,512,512]{4,3,2,1,0:T(8,128)(2,1)S(1)} %copy-done, bf16[1,2,2048,512]{3,2,1,0:T(8,128)(2,1)} %peramb_ref.1), custom_call_target="tpu_custom_call" | custom-call | flops 1000 | bytes 1000 | tf_op jit(solution)/shard_map/mix/pallas_call | solution.py:88
  13.9 1.6 %collective-permute-start.13 = (bf16[2,2,4,64,512]{4,3,2,1,0:T(8,128)(2,1)S(1)}, bf16[2,2,4,64,512]{4,3,2,1,0:T(8,128)(2,1)S(1)}, u32[]{:S(2)}, u32[]{:S(2)}) collective-permute-start(bf16[2,2,4,64,512]{4,3,2,1,0:T(8,128)(2,1)S(1)} %get-tuple-element.28), channel_id=1, source_target_pairs={{0,2},{1,3},{2,0},{3,1},{4,6},{5,7},{6,4},{7,5},{8,10},{9,11},{10,... | collective-permute-start | bytes 3145736 | tf_op jit(solution)/shard_map/ppermute | solution.py:291
  15.5 0.0 collective-permute-start.9
  15.5 2.4 %collective-permute-done.4 = bf16[128,1024]{1,0:T(8,128)(2,1)S(1)} collective-permute-done((bf16[128,1024]{1,0:T(8,128)(2,1)S(1)}, bf16[128,1024]{1,0:T(8,128)(2,1)S(1)}, u32[]{:S(2)}, u32[]{:S(2)}) %collective-permute-start.4) | collective-permute-done | bytes 262176 | tf_op jit(solution)/shard_map/ppermute | solution.py:291
  17.9 0.0 collective-permute-done.1.refs_2_
  17.9 0.0 collective-permute-start.2
  17.9 1.4 %collective-permute-done.3 = bf16[128,1024]{1,0:T(8,128)(2,1)S(1)} collective-permute-done((bf16[128,1024]{1,0:T(8,128)(2,1)S(1)}, bf16[128,1024]{1,0:T(8,128)(2,1)S(1)}, u32[]{:S(2)}, u32[]{:S(2)}) %collective-permute-start.3) | collective-permute-done | bytes 262176 | tf_op jit(solution)/shard_map/ppermute | solution.py:291
  19.3 0.6 %collective-permute-start.8 = (bf16[256,1024]{1,0:T(8,128)(2,1)S(1)}, bf16[256,1024]{1,0:T(8,128)(2,1)S(1)}, u32[]{:S(2)}, u32[]{:S(2)}) collective-permute-start(bf16[256,1024]{1,0:T(8,128)(2,1)S(1)} %pad_maximum_fusion.refs_4_), channel_id=1, source_target_pairs={{0,4},{4,0},{8,12},{12,8},{16,20},{20,16},{24,28},{28,24},{1,5},{5... | collective-permute-start | bytes 1572872 | tf_op jit(solution)/shard_map/ppermute | solution.py:291
  19.9 3.0 %collective-permute-start.6 = (bf16[128,1024]{1,0:T(8,128)(2,1)S(1)}, bf16[128,1024]{1,0:T(8,128)(2,1)S(1)}, u32[]{:S(2)}, u32[]{:S(2)}) collective-permute-start(bf16[128,1024]{1,0:T(8,128)(2,1)S(1)} %pad_maximum_fusion.1.refs_0_), channel_id=1, source_target_pairs={{0,24},{4,28},{8,16},{12,20},{16,8},{20,12},{24,0},{28,4},{1,25},{... | collective-permute-start | bytes 786440 | tf_op jit(solution)/shard_map/ppermute | solution.py:291
  22.9 6.9 %collective-permute-done.6.refs_6_ = bf16[128,1024]{1,0:T(8,128)(2,1)S(1)} collective-permute-done((bf16[128,1024]{1,0:T(8,128)(2,1)S(1)}, bf16[128,1024]{1,0:T(8,128)(2,1)S(1)}, u32[]{:S(2)}, u32[]{:S(2)}) %collective-permute-start.6) | collective-permute-done | bytes 262176 | tf_op jit(solution)/shard_map/ppermute | solution.py:291
  29.9 0.0 collective-permute-start
  29.9 0.0 collective-permute-done.9.refs_4_
  29.9 0.5 %collective-permute-start.7 = (bf16[128,1024]{1,0:T(8,128)(2,1)S(1)}, bf16[128,1024]{1,0:T(8,128)(2,1)S(1)}, u32[]{:S(2)}, u32[]{:S(2)}) collective-permute-start(bf16[128,1024]{1,0:T(8,128)(2,1)S(1)} %collective-permute-done.6.refs_6_), channel_id=1, source_target_pairs={{0,1},{1,0},{2,3},{3,2},{4,5},{5,4},{6,7},{7,6},{8,9},{9,8},{10,11... | collective-permute-start | bytes 786440 | tf_op jit(solution)/shard_map/ppermute | solution.py:291
  30.4 1.9 %collective-permute-done.8.refs_8_ = bf16[256,1024]{1,0:T(8,128)(2,1)S(1)} collective-permute-done((bf16[256,1024]{1,0:T(8,128)(2,1)S(1)}, bf16[256,1024]{1,0:T(8,128)(2,1)S(1)}, u32[]{:S(2)}, u32[]{:S(2)}) %collective-permute-start.8) | collective-permute-done | bytes 524320 | tf_op jit(solution)/shard_map/ppermute | solution.py:291
  32.3 1.5 %collective-permute-start.10 = (bf16[128,1024]{1,0:T(8,128)(2,1)S(1)}, bf16[128,1024]{1,0:T(8,128)(2,1)S(1)}, u32[]{:S(2)}, u32[]{:S(2)}) collective-permute-start(bf16[128,1024]{1,0:T(8,128)(2,1)S(1)} %collective-permute-done.6.refs_6_), channel_id=1, source_target_pairs={{0,4},{4,0},{8,12},{12,8},{16,20},{20,16},{24,28},{28,24},{1,5},{5... | collective-permute-start | bytes 786440 | tf_op jit(solution)/shard_map/ppermute | solution.py:291
  33.8 0.0 collective-permute-done.refs_1_
  34.5 0.0 collective-permute-done.5.refs_5_
  34.5 4.0 %assemble.1.partial_ref = bf16[2,1024,512]{2,1,0:T(8,128)(2,1)S(1)} custom-call(s32[1]{0:T(128)S(6)} %copy.14.source_ref, s32[2,2]{1,0:T(2,128)S(1)} %copy-done.2, s32[16,128]{1,0:T(8,128)S(1)} %bitcast.5, bf16[128,1024]{1,0:T(8,128)(2,1)S(1)} %pad_maximum_fusion.1.refs_0_, bf16[128,1024]{1,0:T(8,128)(2,1)S(1)} %collective-permute-done.refs_1_, ...), custom_call_target="tpu_custom_call" | custom-call | flops 1000 | bytes 1000 | tf_op jit(solution)/shard_map/assemble/pallas_call | solution.py:154
  38.6 0.0 collective-permute-done.13.refs_0_
  38.6 0.6 %collective-permute-start.14 = (bf16[1,2,3,64,512]{4,3,2,1,0:T(8,128)(2,1)S(1)}, bf16[1,2,3,64,512]{4,3,2,1,0:T(8,128)(2,1)S(1)}, u32[]{:S(2)}, u32[]{:S(2)}) collective-permute-start(bf16[1,2,3,64,512]{4,3,2,1,0:T(8,128)(2,1)S(1)} %slice.16), channel_id=1, source_target_pairs={{0,1},{1,0},{2,3},{3,2},{4,5},{5,4},{6,7},{7,6},{8,9},{9,8},{10,11... | collective-permute-start | bytes 1179656 | tf_op jit(solution)/shard_map/ppermute | solution.py:291
  39.2 0.4 collective-permute-done.10.refs_0_
  39.5 0.0 collective-permute-start.11
  39.6 0.6 %collective-permute-start.15 = (bf16[1,2,1,64,512]{4,3,2,1,0:T(8,128)(2,1)S(1)}, bf16[1,2,1,64,512]{4,3,2,1,0:T(8,128)(2,1)S(1)}, u32[]{:S(2)}, u32[]{:S(2)}) collective-permute-start(bf16[1,2,1,64,512]{4,3,2,1,0:T(8,128)(2,1)S(1)} %slice.17), channel_id=1, source_target_pairs={{0,1},{1,0},{2,3},{3,2},{4,5},{5,4},{6,7},{7,6},{8,9},{9,8},{10,11... | collective-permute-start | bytes 393224 | tf_op jit(solution)/shard_map/ppermute | solution.py:291
  40.1 0.9 %collective-permute-done.11.refs_1_ = bf16[128,1024]{1,0:T(8,128)(2,1)S(1)} collective-permute-done((bf16[128,1024]{1,0:T(8,128)(2,1)S(1)}, bf16[128,1024]{1,0:T(8,128)(2,1)S(1)}, u32[]{:S(2)}, u32[]{:S(2)}) %collective-permute-start.11) | collective-permute-done | bytes 262176 | tf_op jit(solution)/shard_map/ppermute | solution.py:291
  41.1 3.0 %near.1 = (bf16[2,1024,512]{2,1,0:T(8,128)(2,1)S(1)}, bf16[2,2,4,32,2,512]{5,4,3,2,1,0:T(2,128)(2,1)S(1)}) custom-call(s32[1]{0:T(128)S(6)} %copy.14.source_ref, s32[2,2]{1,0:T(2,128)S(1)} %copy-done.2, s32[16,128]{1,0:T(8,128)S(1)} %bitcast.6, bf16[2,1024,512]{2,1,0:T(8,128)(2,1)S(1)} %assemble.1.partial_ref, ...), custom_call_target="tpu_custom_call" | custom-call | flops 1000000000 | bytes 1000 | tf_op jit(solution)/shard_map/near/pallas_call | solution.py:261
  44.1 0.0 collective-permute-done.14.refs_1_
  44.1 2.1 %far.1 = bf16[2,4,32,2,2048]{4,3,2,1,0:T(2,128)(2,1)} custom-call(bf16[2,1024,512]{2,1,0:T(8,128)(2,1)S(1)} %get-tuple-element.26.right, bf16[2,2,4,32,2,512]{5,4,3,2,1,0:T(2,128)(2,1)S(1)} %get-tuple-element.27.near_ref, bf16[2,2,4,64,512]{4,3,2,1,0:T(8,128)(2,1)S(1)} %collective-permute-done.13.refs_0_, ...), custom_call_target="tpu_custom_call" | custom-call | flops 1000000000 | bytes 1000 | tf_op jit(solution)/shard_map/far/pallas_call | solution.py:274
  (18 shorter events, 0.2 us)
Async XLA Ops:
  0.0 8.9 %copy-start.2 = (s32[2,2]{1,0:T(2,128)S(1)}, s32[2,2]{1,0:T(2,128)}, u32[]{:S(2)}) copy-start(s32[2,2]{1,0:T(2,128)} %op_ref.5) | copy-start | bytes 52
  0.0 8.9 %copy-start.3 = (s32[2,128]{1,0:T(2,128)S(1)}, s32[2,128]{1,0:T(2,128)}, u32[]{:S(2)}) copy-start(s32[2,128]{1,0:T(2,128)} %listed_ref.1) | copy-start | bytes 3076
  0.0 8.9 %copy-start = (bf16[1,2,2,512,512]{4,3,2,1,0:T(8,128)(2,1)S(1)}, bf16[1,2,2,512,512]{4,3,2,1,0:T(8,128)(2,1)}, u32[]{:S(2)}) copy-start(bf16[1,2,2,512,512]{4,3,2,1,0:T(8,128)(2,1)} %sink_ref.1) | copy-start | bytes 6291460
  1.7 32.8 %copy-start.1 = (s32[2048]{0:T(1024)S(1)}, s32[2048]{0:T(1024)}, u32[]{:S(2)}) copy-start(s32[2048]{0:T(1024)} %param.10) | copy-start | bytes 24580
  1.7 16.2 %collective-permute-start.4 = (bf16[128,1024]{1,0:T(8,128)(2,1)S(1)}, bf16[128,1024]{1,0:T(8,128)(2,1)S(1)}, u32[]{:S(2)}, u32[]{:S(2)}) collective-permute-start(bf16[128,1024]{1,0:T(8,128)(2,1)S(1)} %pad_maximum_fusion.1.refs_0_), channel_id=1, source_target_pairs={{0,16},{4,20},{8,24},{12,28},{16,0},{20,4},{24,8},{28,12},{1,17},{... | collective-permute-start | bytes 786440 | tf_op jit(solution)/shard_map/ppermute | solution.py:291
  5.8 12.0 %collective-permute-start.1 = (bf16[128,1024]{1,0:T(8,128)(2,1)S(1)}, bf16[128,1024]{1,0:T(8,128)(2,1)S(1)}, u32[]{:S(2)}, u32[]{:S(2)}) collective-permute-start(bf16[128,1024]{1,0:T(8,128)(2,1)S(1)} %pad_maximum_fusion.1.refs_0_), channel_id=1, source_target_pairs={{0,4},{4,0},{8,12},{12,8},{16,20},{20,16},{24,28},{28,24},{1,5},{5... | collective-permute-start | bytes 786440 | tf_op jit(solution)/shard_map/ppermute | solution.py:291
  7.3 11.9 %collective-permute-start.3 = (bf16[128,1024]{1,0:T(8,128)(2,1)S(1)}, bf16[128,1024]{1,0:T(8,128)(2,1)S(1)}, u32[]{:S(2)}, u32[]{:S(2)}) collective-permute-start(bf16[128,1024]{1,0:T(8,128)(2,1)S(1)} %pad_maximum_fusion.1.refs_0_), channel_id=1, source_target_pairs={{0,8},{4,12},{8,0},{12,4},{16,24},{20,28},{24,16},{28,20},{1,9},{5... | collective-permute-start | bytes 786440 | tf_op jit(solution)/shard_map/ppermute | solution.py:291
  13.9 24.7 %collective-permute-start.13 = (bf16[2,2,4,64,512]{4,3,2,1,0:T(8,128)(2,1)S(1)}, bf16[2,2,4,64,512]{4,3,2,1,0:T(8,128)(2,1)S(1)}, u32[]{:S(2)}, u32[]{:S(2)}) collective-permute-start(bf16[2,2,4,64,512]{4,3,2,1,0:T(8,128)(2,1)S(1)} %get-tuple-element.28), channel_id=1, source_target_pairs={{0,2},{1,3},{2,0},{3,1},{4,6},{5,7},{6,4},{7,5},{8,10},{9,11},{10,... | collective-permute-start | bytes 3145736 | tf_op jit(solution)/shard_map/ppermute | solution.py:291
  15.5 14.4 %collective-permute-start.9 = (bf16[1,2,4,64,512]{4,3,2,1,0:T(8,128)(2,1)S(1)}, bf16[1,2,4,64,512]{4,3,2,1,0:T(8,128)(2,1)S(1)}, u32[]{:S(2)}, u32[]{:S(2)}) collective-permute-start(bf16[1,2,4,64,512]{4,3,2,1,0:T(8,128)(2,1)S(1)} %get-tuple-element.23), channel_id=1, source_target_pairs={{0,1},{1,0},{2,3},{3,2},{4,5},{5,4},{6,7},{7,6},{8,9},{9,8},{10,11... | collective-permute-start | bytes 1572872 | tf_op jit(solution)/shard_map/ppermute | solution.py:291
  17.9 5.1 %collective-permute-start.2 = (bf16[128,1024]{1,0:T(8,128)(2,1)S(1)}, bf16[128,1024]{1,0:T(8,128)(2,1)S(1)}, u32[]{:S(2)}, u32[]{:S(2)}) collective-permute-start(bf16[128,1024]{1,0:T(8,128)(2,1)S(1)} %collective-permute-done.1.refs_2_), channel_id=1, source_target_pairs={{0,1},{1,0},{2,3},{3,2},{4,5},{5,4},{6,7},{7,6},{8,9},{9,8},{10,11... | collective-permute-start | bytes 786440 | tf_op jit(solution)/shard_map/ppermute | solution.py:291
  19.3 13.0 %collective-permute-start.8 = (bf16[256,1024]{1,0:T(8,128)(2,1)S(1)}, bf16[256,1024]{1,0:T(8,128)(2,1)S(1)}, u32[]{:S(2)}, u32[]{:S(2)}) collective-permute-start(bf16[256,1024]{1,0:T(8,128)(2,1)S(1)} %pad_maximum_fusion.refs_4_), channel_id=1, source_target_pairs={{0,4},{4,0},{8,12},{12,8},{16,20},{20,16},{24,28},{28,24},{1,5},{5... | collective-permute-start | bytes 1572872 | tf_op jit(solution)/shard_map/ppermute | solution.py:291
  19.9 9.9 %collective-permute-start.6 = (bf16[128,1024]{1,0:T(8,128)(2,1)S(1)}, bf16[128,1024]{1,0:T(8,128)(2,1)S(1)}, u32[]{:S(2)}, u32[]{:S(2)}) collective-permute-start(bf16[128,1024]{1,0:T(8,128)(2,1)S(1)} %pad_maximum_fusion.1.refs_0_), channel_id=1, source_target_pairs={{0,24},{4,28},{8,16},{12,20},{16,8},{20,12},{24,0},{28,4},{1,25},{... | collective-permute-start | bytes 786440 | tf_op jit(solution)/shard_map/ppermute | solution.py:291
  22.9 11.6 %collective-permute-start.5 = (bf16[256,1024]{1,0:T(8,128)(2,1)S(1)}, bf16[256,1024]{1,0:T(8,128)(2,1)S(1)}, u32[]{:S(2)}, u32[]{:S(2)}) collective-permute-start(bf16[256,1024]{1,0:T(8,128)(2,1)S(1)} %pad_maximum_fusion.refs_4_), channel_id=1, source_target_pairs={{0,1},{1,0},{2,3},{3,2},{4,5},{5,4},{6,7},{7,6},{8,9},{9,8},{10,11... | collective-permute-start | bytes 1572872 | tf_op jit(solution)/shard_map/ppermute | solution.py:291
  29.9 4.0 %collective-permute-start = (bf16[128,1024]{1,0:T(8,128)(2,1)S(1)}, bf16[128,1024]{1,0:T(8,128)(2,1)S(1)}, u32[]{:S(2)}, u32[]{:S(2)}) collective-permute-start(bf16[128,1024]{1,0:T(8,128)(2,1)S(1)} %pad_maximum_fusion.1.refs_0_), channel_id=1, source_target_pairs={{0,1},{1,0},{2,3},{3,2},{4,5},{5,4},{6,7},{7,6},{8,9},{9,8},{10,11... | collective-permute-start | bytes 786440 | tf_op jit(solution)/shard_map/ppermute | solution.py:291
  29.9 4.7 %collective-permute-start.7 = (bf16[128,1024]{1,0:T(8,128)(2,1)S(1)}, bf16[128,1024]{1,0:T(8,128)(2,1)S(1)}, u32[]{:S(2)}, u32[]{:S(2)}) collective-permute-start(bf16[128,1024]{1,0:T(8,128)(2,1)S(1)} %collective-permute-done.6.refs_6_), channel_id=1, source_target_pairs={{0,1},{1,0},{2,3},{3,2},{4,5},{5,4},{6,7},{7,6},{8,9},{9,8},{10,11... | collective-permute-start | bytes 786440 | tf_op jit(solution)/shard_map/ppermute | solution.py:291
  32.3 7.2 %collective-permute-start.10 = (bf16[128,1024]{1,0:T(8,128)(2,1)S(1)}, bf16[128,1024]{1,0:T(8,128)(2,1)S(1)}, u32[]{:S(2)}, u32[]{:S(2)}) collective-permute-start(bf16[128,1024]{1,0:T(8,128)(2,1)S(1)} %collective-permute-done.6.refs_6_), channel_id=1, source_target_pairs={{0,4},{4,0},{8,12},{12,8},{16,20},{20,16},{24,28},{28,24},{1,5},{5... | collective-permute-start | bytes 786440 | tf_op jit(solution)/shard_map/ppermute | solution.py:291
  33.9 6.3 %collective-permute-start.12 = (bf16[256,1024]{1,0:T(8,128)(2,1)S(1)}, bf16[256,1024]{1,0:T(8,128)(2,1)S(1)}, u32[]{:S(2)}, u32[]{:S(2)}) collective-permute-start(bf16[256,1024]{1,0:T(8,128)(2,1)S(1)} %collective-permute-done.8.refs_8_), channel_id=1, source_target_pairs={{0,1},{1,0},{2,3},{3,2},{4,5},{5,4},{6,7},{7,6},{8,9},{9,8},{10,11... | collective-permute-start | bytes 1572872 | tf_op jit(solution)/shard_map/ppermute | solution.py:291
  38.6 5.5 %collective-permute-start.14 = (bf16[1,2,3,64,512]{4,3,2,1,0:T(8,128)(2,1)S(1)}, bf16[1,2,3,64,512]{4,3,2,1,0:T(8,128)(2,1)S(1)}, u32[]{:S(2)}, u32[]{:S(2)}) collective-permute-start(bf16[1,2,3,64,512]{4,3,2,1,0:T(8,128)(2,1)S(1)} %slice.16), channel_id=1, source_target_pairs={{0,1},{1,0},{2,3},{3,2},{4,5},{5,4},{6,7},{7,6},{8,9},{9,8},{10,11... | collective-permute-start | bytes 1179656 | tf_op jit(solution)/shard_map/ppermute | solution.py:291
  39.5 1.5 %collective-permute-start.11 = (bf16[128,1024]{1,0:T(8,128)(2,1)S(1)}, bf16[128,1024]{1,0:T(8,128)(2,1)S(1)}, u32[]{:S(2)}, u32[]{:S(2)}) collective-permute-start(bf16[128,1024]{1,0:T(8,128)(2,1)S(1)} %collective-permute-done.10.refs_0_), channel_id=1, source_target_pairs={{0,1},{1,0},{2,3},{3,2},{4,5},{5,4},{6,7},{7,6},{8,9},{9,8},{10,11... | collective-permute-start | bytes 786440 | tf_op jit(solution)/shard_map/ppermute | solution.py:291
  39.6 4.6 %collective-permute-start.15 = (bf16[1,2,1,64,512]{4,3,2,1,0:T(8,128)(2,1)S(1)}, bf16[1,2,1,64,512]{4,3,2,1,0:T(8,128)(2,1)S(1)}, u32[]{:S(2)}, u32[]{:S(2)}) collective-permute-start(bf16[1,2,1,64,512]{4,3,2,1,0:T(8,128)(2,1)S(1)} %slice.17), channel_id=1, source_target_pairs={{0,1},{1,0},{2,3},{3,2},{4,5},{5,4},{6,7},{7,6},{8,9},{9,8},{10,11... | collective-permute-start | bytes 393224 | tf_op jit(solution)/shard_map/ppermute | solution.py:291
